TPU v7x, 32 devices: a whole 2x2x4 slice. The times are simulated.
32 devices in a mesh: dp: 16 (over z, y, x), blk: 2 (over core).
Axes of the slice: x: 2, y: 2, z: 4, core: 2. Of those that a mesh axis runs over, the one named last changes fastest.
Arguments:
- inputs: bfloat16 [16, 784, 768], P('dp', 'blk'), may hold values from -6 to 6
- segments: int32 [16, 784], P('dp', 'blk'), may hold values from 0 to 7, never falling along the last dimension, each value on 1 to 196 neighbouring positions
- positions: int32 [16, 784], P('dp', 'blk'), may hold values from 0 to 195
- pos_table: bfloat16 [196, 768], replicated, may hold values from -3 to 3
- ln1_gain: float32 [768], replicated, may hold values from 0.5 to 1.5
- ln1_shift: float32 [768], replicated, may hold values from -1.5 to 1.5
- qkv_weight: bfloat16 [768, 2304], replicated, may hold values from -0.21875 to 0.21875
- query_bias: float32 [768], replicated, may hold values from -1.5 to 1.5
- value_bias: float32 [768], replicated, may hold values from -1.5 to 1.5
- out_weight: bfloat16 [768, 768], replicated, may hold values from -1.25 to 1.25
- out_bias: float32 [768], replicated, may hold values from -1.5 to 1.5
- ln2_gain: float32 [768], replicated, may hold values from 0.5 to 1.5
- ln2_shift: float32 [768], replicated, may hold values from -1.5 to 1.5
- fc1_weight: bfloat16 [768, 3072], replicated, may hold values from -0.21875 to 0.21875
- fc1_bias: float32 [3072], replicated, may hold values from -1.5 to 1.5
- fc2_weight: bfloat16 [3072, 768], replicated, may hold values from -0.109375 to 0.109375
- fc2_bias: float32 [768], replicated, may hold values from -1.5 to 1.5
- cotangent: bfloat16 [16, 784, 768], P('dp', 'blk'), may hold values from -6 to 6
Outputs:
- result: bfloat16 [16, 784, 768], P('dp', 'blk')
- input_grad: bfloat16 [16, 784, 768], P('dp', 'blk')
- table_grad: float32 [196, 768], replicated
- ln1_gain_grad: float32 [768], replicated
- ln1_shift_grad: float32 [768], replicated
- qkv_grad: float32 [768, 2304], P(('dp', 'blk'))
- query_bias_grad: float32 [768], replicated
- value_bias_grad: float32 [768], replicated
- out_grad: float32 [768, 768], P(('dp', 'blk'))
- out_bias_grad: float32 [768], replicated
- ln2_gain_grad: float32 [768], replicated
- ln2_shift_grad: float32 [768], replicated
- fc1_grad: float32 [768, 3072], P(('dp', 'blk'))
- fc1_bias_grad: float32 [3072], replicated
- fc2_grad: float32 [3072, 768], P(('dp', 'blk'))
- fc2_bias_grad: float32 [768], replicated
Inputs may be any that keep to these rules, and one draw needn't show every extreme that they name: `segments`: crop ids of a row never fall, each crop has 1 to 196 tokens.
All inputs are finite; a program needn't handle non-finite values.
Results may differ from a plain program's by a relative error of at most 0.013.
Values may be sent and summed in bfloat16 or wider, within the bound.
No kernel may reach another device: no remote copies, remote signals or barrier semaphores. Data moves between devices by JAX's collectives and lax.ppermute only.
A program may use at most 192 MiB of HBM per device.

v0:
```python
import jax
import jax.numpy as jnp
from jax import lax
from jax.sharding import PartitionSpec as P

H = 12
HD = 64


inv_root_two = 0.7071067811865476
inv_root_two_pi = 0.3989422804014327


def layer_norm(hidden, gain, shift):
    mean = jnp.mean(hidden, -1, keepdims=True)
    centred = hidden - mean
    variance = jnp.mean(centred * centred, -1, keepdims=True)
    inv_std = lax.rsqrt(variance + 1e-06)
    normal = centred * inv_std
    return (normal * gain + shift, normal, inv_std)


def norm_back(grad_out, normal, inv_std, gain):
    scaled = grad_out * gain
    centre = jnp.mean(scaled, -1, keepdims=True)
    along = jnp.mean(scaled * normal, -1, keepdims=True)
    return inv_std * (scaled - centre - normal * along)


def token_sum(values):
    return jnp.sum(values.reshape(-1, values.shape[-1]), axis=0)


def weight_product(left, right):
    flat_left = left.reshape(-1, left.shape[-1])
    flat_right = right.reshape(-1, right.shape[-1])
    return lax.dot_general(
        flat_left, flat_right, (((0,), (0,)), ((), ())), preferred_element_type=jnp.float32
    )


def back_product(grad, weight):
    return lax.dot_general(
        grad, weight, (((grad.ndim - 1,), (1,)), ((), ())), preferred_element_type=jnp.float32
    )


def heads_first(array):
    rows, count, width = array.shape
    return array.reshape(rows, count, H, HD).transpose(2, 0, 1, 3)


def heads_back(array):
    heads, rows, count, size = array.shape
    return array.transpose(1, 2, 0, 3).reshape(rows, count, heads * size)


def per_device(
    inputs,
    segments,
    positions,
    pos_table,
    ln1_gain,
    ln1_shift,
    qkv_weight,
    query_bias,
    value_bias,
    out_weight,
    out_bias,
    ln2_gain,
    ln2_shift,
    fc1_weight,
    fc1_bias,
    fc2_weight,
    fc2_bias,
    cotangent,
):
    rows, half, width = inputs.shape
    table_size = pos_table.shape[0]
    one_hot = (
        positions[..., None] == lax.broadcasted_iota(jnp.int32, (rows, half, table_size), 2)
    ).astype(jnp.bfloat16)
    hidden0 = inputs.astype(jnp.float32) + jnp.einsum(
        "rtp,pd->rtd", one_hot, pos_table, preferred_element_type=jnp.float32
    )
    normed1, normal1, inv_one = layer_norm(hidden0, ln1_gain, ln1_shift)
    normed1 = normed1.astype(jnp.bfloat16)
    joined_bias = jnp.concatenate([query_bias, jnp.zeros_like(query_bias), value_bias])
    joined = (
        jnp.dot(normed1, qkv_weight, preferred_element_type=jnp.float32) + joined_bias
    ).astype(jnp.bfloat16)
    query = joined[..., :width]
    keys = joined[..., width : 2 * width]
    values = joined[..., 2 * width :]
    seg_low = segments.astype(jnp.bfloat16)
    all_keys, all_values, all_segs = (
        lax.all_gather(keys, "blk", axis=1, tiled=True),
        lax.all_gather(values, "blk", axis=1, tiled=True),
        lax.all_gather(seg_low, "blk", axis=1, tiled=True),
    )
    same_fwd = seg_low[:, :, None] == all_segs[:, None, :]
    query_heads = heads_first(query)

    def forward_head(item):
        query_one, key_one, value_one = item
        scores = (
            jnp.einsum("rqd,rkd->rqk", query_one, key_one, preferred_element_type=jnp.float32)
            * 0.125
        )
        scores = jnp.where(same_fwd, scores, -1000000000.0)
        top = jnp.max(scores, -1, keepdims=True)
        log_total = top + jnp.log(jnp.sum(jnp.exp(scores - top), -1, keepdims=True))
        probs = jnp.exp(scores - log_total).astype(jnp.bfloat16)
        attended_one = jnp.einsum(
            "rqk,rkd->rqd", probs, value_one, preferred_element_type=jnp.float32
        )
        return (attended_one.astype(jnp.bfloat16), log_total)

    attended_heads, log_total = lax.map(
        forward_head, (query_heads, heads_first(all_keys), heads_first(all_values))
    )
    attended = heads_back(attended_heads)
    hidden1 = hidden0 + jnp.dot(attended, out_weight, preferred_element_type=jnp.float32) + out_bias
    normed2, normal2, inv_two = layer_norm(hidden1, ln2_gain, ln2_shift)
    normed2 = normed2.astype(jnp.bfloat16)
    pre_act = jnp.dot(normed2, fc1_weight, preferred_element_type=jnp.float32) + fc1_bias
    activated = jax.nn.gelu(pre_act, approximate=False).astype(jnp.bfloat16)
    mixed = jnp.dot(activated, fc2_weight, preferred_element_type=jnp.float32) + fc2_bias
    result = (hidden1 + mixed).astype(jnp.bfloat16)
    grad_top = cotangent.astype(jnp.float32)
    fc2_bias_grad = token_sum(grad_top)
    fc2_grad = weight_product(activated, cotangent)
    grad_act = back_product(cotangent, fc2_weight)
    slope = (
        0.5 * (1.0 + lax.erf(pre_act * inv_root_two))
        + pre_act * jnp.exp(-0.5 * pre_act * pre_act) * inv_root_two_pi
    )
    grad_pre = (grad_act * slope).astype(jnp.bfloat16)
    fc1_bias_grad = token_sum(grad_pre.astype(jnp.float32))
    fc1_grad = weight_product(normed2, grad_pre)
    grad_norm2 = back_product(grad_pre, fc1_weight)
    ln2_gain_grad = token_sum(grad_norm2 * normal2)
    ln2_shift_grad = token_sum(grad_norm2)
    grad_hidden1 = grad_top + norm_back(grad_norm2, normal2, inv_two, ln2_gain)
    grad_branch = grad_hidden1.astype(jnp.bfloat16)
    out_bias_grad = token_sum(grad_branch.astype(jnp.float32))
    out_grad = weight_product(attended, grad_branch)
    grad_att = back_product(grad_branch, out_weight).astype(jnp.bfloat16)
    back_keys, back_values, back_segs = (
        lax.all_gather(keys, "blk", axis=1, tiled=True),
        lax.all_gather(values, "blk", axis=1, tiled=True),
        lax.all_gather(seg_low, "blk", axis=1, tiled=True),
    )
    same_back = seg_low[:, :, None] == back_segs[:, None, :]

    def backward_head(item):
        query_one, key_one, value_one, log_one, grad_one = item
        scores = (
            jnp.einsum("rqd,rkd->rqk", query_one, key_one, preferred_element_type=jnp.float32)
            * 0.125
        )
        scores = jnp.where(same_back, scores, -1000000000.0)
        probs = jnp.exp(scores - log_one)
        grad_probs = jnp.einsum(
            "rqd,rkd->rqk", grad_one, value_one, preferred_element_type=jnp.float32
        )
        row_dot = jnp.sum(probs * grad_probs, -1, keepdims=True)
        grad_scores = (probs * (grad_probs - row_dot)).astype(jnp.bfloat16)
        grad_query_one = (
            jnp.einsum("rqk,rkd->rqd", grad_scores, key_one, preferred_element_type=jnp.float32)
            * 0.125
        )
        grad_keys_one = (
            jnp.einsum("rqk,rqd->rkd", grad_scores, query_one, preferred_element_type=jnp.float32)
            * 0.125
        )
        grad_values_one = jnp.einsum(
            "rqk,rqd->rkd", probs.astype(jnp.bfloat16), grad_one, preferred_element_type=jnp.float32
        )
        return (grad_query_one, grad_keys_one, grad_values_one)

    grad_query, part_keys, part_values = lax.map(
        backward_head,
        (
            query_heads,
            heads_first(back_keys),
            heads_first(back_values),
            log_total,
            heads_first(grad_att),
        ),
    )
    grad_query = heads_back(grad_query)
    part_keys = heads_back(part_keys)
    part_values = heads_back(part_values)
    own_keys, own_values = (
        lax.psum_scatter(
            part_keys.astype(jnp.bfloat16), "blk", scatter_dimension=1, tiled=True
        ).astype(jnp.float32),
        lax.psum_scatter(
            part_values.astype(jnp.bfloat16), "blk", scatter_dimension=1, tiled=True
        ).astype(jnp.float32),
    )
    grad_joined = jnp.concatenate([grad_query, own_keys, own_values], -1).astype(jnp.bfloat16)
    query_bias_grad = token_sum(grad_joined[..., :width].astype(jnp.float32))
    value_bias_grad = token_sum(grad_joined[..., 2 * width :].astype(jnp.float32))
    qkv_grad = weight_product(normed1, grad_joined)
    grad_norm1 = back_product(grad_joined, qkv_weight)
    ln1_gain_grad = token_sum(grad_norm1 * normal1)
    ln1_shift_grad = token_sum(grad_norm1)
    grad_hidden0 = grad_hidden1 + norm_back(grad_norm1, normal1, inv_one, ln1_gain)
    input_grad = grad_hidden0.astype(jnp.bfloat16)
    table_part = jnp.einsum(
        "rtp,rtd->pd", one_hot.astype(jnp.float32), grad_hidden0, precision=lax.Precision.HIGHEST
    )
    summed_small = lax.psum(
        (
            table_part,
            ln1_gain_grad,
            ln1_shift_grad,
            query_bias_grad,
            value_bias_grad,
            out_bias_grad,
            ln2_gain_grad,
            ln2_shift_grad,
            fc1_bias_grad,
            fc2_bias_grad,
        ),
        ("dp", "blk"),
    )
    weight_terms = (qkv_grad, out_grad, fc1_grad, fc2_grad)
    summed_weights = (
        lax.psum_scatter(weight_terms[0], ("dp", "blk"), scatter_dimension=0, tiled=True),
        lax.psum_scatter(weight_terms[1], ("dp", "blk"), scatter_dimension=0, tiled=True),
        lax.psum_scatter(weight_terms[2], ("dp", "blk"), scatter_dimension=0, tiled=True),
        lax.psum_scatter(weight_terms[3], ("dp", "blk"), scatter_dimension=0, tiled=True),
    )
    return (
        result,
        input_grad,
        summed_small[0],
        summed_small[1],
        summed_small[2],
        summed_weights[0],
        summed_small[3],
        summed_small[4],
        summed_weights[1],
        summed_small[5],
        summed_small[6],
        summed_small[7],
        summed_weights[2],
        summed_small[8],
        summed_weights[3],
        summed_small[9],
    )


def solution(mesh):
    placed = (
        P("dp", "blk", None),
        P("dp", "blk"),
        P("dp", "blk"),
        P(),
        P(),
        P(),
        P(),
        P(),
        P(),
        P(),
        P(),
        P(),
        P(),
        P(),
        P(),
        P(),
        P(),
        P("dp", "blk", None),
    )
    return jax.shard_map(
        per_device,
        mesh=mesh,
        in_specs=placed,
        out_specs=(
            P("dp", "blk", None),
            P("dp", "blk", None),
            P(),
            P(),
            P(),
            P(("dp", "blk"), None),
            P(),
            P(),
            P(("dp", "blk"), None),
            P(),
            P(),
            P(),
            P(("dp", "blk"), None),
            P(),
            P(("dp", "blk"), None),
            P(),
        ),
        check_vma=False,
    )
```

profile of v0, /device:TPU:0, one launch (start us, length us, event | category | flops | bytes accessed | tf_op | source)
XLA Modules:
  0.0 946.2 jit_solution(12825219834420836904)
XLA Ops:
  13.4 2.3 copy.49
  15.7 2.4 copy.52
  19.6 2.7 all-reduce
  22.3 2.3 all-gather.5.cloned.1.call-done
  24.6 2.5 copy.51
  27.1 3.9 copy.54
  31.0 6.2 all-gather.3.cloned.1.call-done
  37.2 2.5 copy.50
  39.8 3.9 copy.53
  43.6 54.2 %while.28 = (s32[]{:T(128)}, bf16[12,1,392,64]{2,3,1,0:T(8,128)(2,1)}, f32[12,1,392,1]{2,3,1,0:T(1,128)}, bf16[12,1,392,64]{3,2,1,0:T(8,128)(2,1)}, bf16[12,1,78...) while((s32[]{:T(128)}, ...), condition=%wide.region_5.6_spmd.clone, body=%wide.region_2.5_spmd.clone.sunk | while | flops 81159288 | bytes 4274329 | solution.py:119
  45.5 2.1 fusion.144
  50.0 2.1 fusion.144
  54.6 2.1 fusion.144
  59.1 2.1 fusion.144
  63.6 2.1 fusion.144
  68.1 2.1 fusion.144
  72.6 2.0 fusion.144
  77.1 2.1 fusion.144
  81.6 2.1 fusion.144
  90.7 2.1 fusion.144
  95.2 2.1 fusion.144
  97.8 2.8 fusion.109
  101.0 15.6 %fusion.47 = (bf16[392,3072]{1,0:T(8,128)(2,1)}, f32[392,3072]{1,0:T(8,128)S(1)}) fusion(f32[3072]{0:T(1024)} %param.36, bf16[768,3072]{1,0:T(8,128)(2,1)} %param.35, f32[1,392,768]{2,1,0:T(8,128)S(1)} %get-tuple-element.267, f32[768]{0:T(1024)} %param.34, f32[768]{0:T(1024)S(1)} %copy-done.13, f32[392]{0:T(512)S(1)} %add_rsqrt_fusion, ...), kind=kOutput, calls=%fused_computation.60 | convolution fusion | flops 1930672128 | bytes 13169728 | tf_op jit(solution)/shard_map/dot_general | solution.py:126
  116.6 4.2 convert_reduce_fusion
  120.9 2.8 fusion.69
  128.2 2.3 copy.55
  130.5 114.6 %while.29 = (s32[]{:T(128)}, bf16[12,1,392,64]{2,3,1,0:T(8,128)(2,1)}, bf16[12,1,784,64]{2,3,1,0:T(8,128)(2,1)}, bf16[12,1,784,64]{2,3,1,0:T(8,128)(2,1)}, bf16[...) while((s32[]{:T(128)}, ...), condition=%wide.region_12.13_spmd.clone, body=%wide.region_10.12_spmd.clone.sunk | while | flops 199838080 | bytes 10758993 | solution.py:182
  245.1 8.2 copy.60
  253.3 2.9 copy.70
  256.3 8.2 copy.62
  264.5 3.0 copy.69
  267.6 2.7 reshape_bitcast_fusion.1
  270.3 4.6 copy.61
  274.9 3.4 reduce-scatter.21.cloned.1.call-done
  278.3 2.7 reshape_bitcast_fusion
  281.0 4.6 copy.63
  285.6 5.0 fusion.70
  295.0 3.8 fusion.82
  299.2 7.2 fusion.78
  307.1 8.5 fusion.96
  315.7 8.1 fusion.85
  325.3 6.3 fusion.68
  331.8 42.1 %all-reduce.1 = (f32[768]{0:T(1024)}, f32[768]{0:T(1024)}, f32[768]{0:T(1024)}, f32[768]{0:T(1024)}, f32[768]{0:T(1024)}, /*index=5*/f32[768]{0:T(1024)}, f32[768]{0:T(1024)}, f32[3072]{0:T(1024)}, f32[768]{0:T(1024)}) all-reduce(f32[768]{0:T(1024)} %get-tuple-element.199, ...), channel_id=1, replica_groups=mesh['dp'=16,'blk'=2] {'dp','blk'}, use_global_device_ids=true, to_apply=%region_19.20 | all-reduce | flops 9216 | bytes 73728 | tf_op jit(solution)/shard_map/psum | solution.py:215
  373.9 49.8 %all-reduce.4.cloned.1.call-done = f32[196,768]{1,0:T(8,128)} async-done(((f32[196,768]{1,0:T(8,128)}), f32[196,768]{1,0:T(8,128)}) %all-reduce.4.cloned.1.call-update) | async-done | bytes 602128 | tf_op jit(solution)/shard_map/psum | solution.py:215
  423.7 105.8 %reduce-scatter.13.cloned.1.call-done = f32[24,768]{1,0:T(8,128)} async-done(((f32[768,768]{1,0:T(8,128)}), f32[24,768]{1,0:T(8,128)}) %reduce-scatter.13.cloned.1.call-update) | async-done | bytes 73744 | tf_op jit(solution)/shard_map/reduce_scatter | solution.py:233
  529.5 124.5 %reduce-scatter.11.cloned.1.call-done = f32[24,2304]{1,0:T(8,128)} async-done(((f32[768,2304]{1,0:T(8,128)}), f32[24,2304]{1,0:T(8,128)}) %reduce-scatter.11.cloned.1.call-update) | async-done | bytes 221200 | tf_op jit(solution)/shard_map/reduce_scatter | solution.py:232
  654.0 142.4 %reduce-scatter.15.cloned.1.call-done = f32[24,3072]{1,0:T(8,128)} async-done(((f32[768,3072]{1,0:T(8,128)}), f32[24,3072]{1,0:T(8,128)}) %reduce-scatter.15.cloned.1.call-update) | async-done | bytes 294928 | tf_op jit(solution)/shard_map/reduce_scatter | solution.py:234
  796.3 141.0 %reduce-scatter.17.cloned.1.call-done = f32[96,768]{1,0:T(8,128)} async-done(((f32[3072,768]{1,0:T(8,128)}), f32[96,768]{1,0:T(8,128)}) %reduce-scatter.17.cloned.1.call-update) | async-done | bytes 294928 | tf_op jit(solution)/shard_map/reduce_scatter | solution.py:235
  (255 shorter events, 166.6 us)
Async XLA Ops:
  7.2 2.3 copy-start
  7.2 17.4 %all-gather.5.cloned.1.call-start = ((), (), s32[]{:S(2)}) async-start(), calls=%async_computation.7 | async-start | bytes 1806336 | tf_op jit(solution)/shard_map/all_gather | solution.py:98
  7.2 2.2 copy-start.21
  7.3 2.2 copy-start.22
  7.3 2.2 copy-start.11
  7.3 2.2 copy-start.25
  9.1 2.1 copy-start.1
  9.4 1.8 copy-start.15
  12.5 24.7 %all-gather.3.cloned.1.call-start = ((), (), s32[]{:S(2)}) async-start(), calls=%async_computation.6 | async-start | bytes 1806336 | tf_op jit(solution)/shard_map/all_gather | solution.py:97
  13.3 254.4 %reduce-scatter.19.cloned.1.call-start = ((), (), s32[]{:S(2)}) async-start(), calls=%async_computation.13 | async-start | bytes 1806336
  13.4 4.7 copy-start.28
  13.4 5.9 copy-start.23
  43.6 54.2 %copy-start.20 = (f32[768]{0:T(1024)S(1)}, f32[768]{0:T(1024)}, u32[]{:S(2)}) copy-start(f32[768]{0:T(1024)} %param.32) | copy-start | bytes 9220
  97.8 3.1 copy-start.13
  97.8 18.8 %slice-start.2 = ((s8[4718592]{0:T(1024)(128)(4,1)}), s8[4194304]{0:T(1024)(128)(4,1)S(1)}, s32[]{:S(2)}) async-start(s8[4718592]{0:T(1024)(128)(4,1)} %bitcast.255), calls=%async_computation.17 | async-start | bytes 8388608
  97.8 23.0 %slice-start = ((s8[4718592]{0:T(1024)(128)(4,1)}), s8[4194304]{0:T(1024)(128)(4,1)S(1)}, s32[]{:S(2)}) async-start(s8[4718592]{0:T(1024)(128)(4,1)} %bitcast.253), calls=%async_computation.15 | async-start | bytes 8388608
  100.7 23.8 %copy-start.5 = (f32[1,392,768]{2,1,0:T(8,128)}, f32[1,392,768]{2,1,0:T(8,128)S(1)}, u32[]{:S(2)}) copy-start(f32[1,392,768]{2,1,0:T(8,128)S(1)} %get-tuple-element.267) | copy-start | bytes 3612676
  101.0 23.5 %copy-start.17 = (f32[392]{0:T(512)}, f32[392]{0:T(512)S(1)}, u32[]{:S(2)}) copy-start(f32[392]{0:T(512)S(1)} %add_rsqrt_fusion) | copy-start | bytes 4708
  101.0 15.6 %copy-start.8 = (bf16[1,392,768]{2,1,0:T(8,128)(2,1)S(1)}, bf16[1,392,768]{2,1,0:T(8,128)(2,1)}, u32[]{:S(2)}) copy-start(bf16[1,392,768]{2,1,0:T(8,128)(2,1)} %param.39) | copy-start | bytes 1806340
  101.0 15.6 %slice-start.3 = ((s8[4718592]{0:T(1024)(128)(4,1)}), s8[524288]{0:T(1024)(128)(4,1)S(1)}, s32[]{:S(2)}) async-start(s8[4718592]{0:T(1024)(128)(4,1)} %bitcast.255), calls=%async_computation.18 | async-start | bytes 1048576
  101.0 15.6 %copy-start.24 = (f32[3072]{0:T(1024)S(1)}, f32[3072]{0:T(1024)}, u32[]{:S(2)}) copy-start(f32[3072]{0:T(1024)} %param.36) | copy-start | bytes 36868
  101.0 19.8 %slice-start.1 = ((s8[4718592]{0:T(1024)(128)(4,1)}), s8[524288]{0:T(1024)(128)(4,1)S(1)}, s32[]{:S(2)}) async-start(s8[4718592]{0:T(1024)(128)(4,1)} %bitcast.253), calls=%async_computation.16 | async-start | bytes 1048576
  120.9 2.9 copy-start.29
  124.4 2.3 copy-start.6
  125.6 1.1 copy-start.3
  256.2 22.1 %reduce-scatter.21.cloned.1.call-start = ((), (), s32[]{:S(2)}) async-start(), calls=%async_computation.14 | async-start | bytes 1806336
  267.6 156.1 %all-reduce.4.cloned.1.call-start = ((), (), s32[]{:S(2)}) async-start(), calls=%async_computation.8 | async-start | bytes 1228800 | tf_op jit(solution)/shard_map/psum | solution.py:215
  281.0 4.6 copy-start.12
  281.0 4.6 copy-start.16
  285.6 5.7 copy-start.4
  290.7 1.3 copy-start.2
  291.9 1.3 copy-start.19
  295.0 234.5 %reduce-scatter.13.cloned.1.call-start = ((), (), s32[]{:S(2)}) async-start(), calls=%async_computation.10 | async-start | bytes 2433024 | tf_op jit(solution)/shard_map/reduce_scatter | solution.py:233
  298.9 355.1 %reduce-scatter.11.cloned.1.call-start = ((), (), s32[]{:S(2)}) async-start(), calls=%async_computation.9 | async-start | bytes 7299072 | tf_op jit(solution)/shard_map/reduce_scatter | solution.py:232
  306.4 0.7 copy-start.14
  306.4 0.7 copy-start.18
  306.4 0.7 copy-start.26
  306.4 489.9 %reduce-scatter.15.cloned.1.call-start = ((), (), s32[]{:S(2)}) async-start(), calls=%async_computation.11 | async-start | bytes 9732096 | tf_op jit(solution)/shard_map/reduce_scatter | solution.py:234
  315.7 621.6 %reduce-scatter.17.cloned.1.call-start = ((), (), s32[]{:S(2)}) async-start(), calls=%async_computation.12 | async-start | bytes 9732096 | tf_op jit(solution)/shard_map/reduce_scatter | solution.py:235
  323.9 1.4 copy-start.27
  325.3 6.3 copy-start.7
  325.3 6.5 copy-start.9
  325.3 6.5 copy-start.10
Sparse Core Ops, SparseCore 0:
  12.6 11.9 all-gather.4
  26.8 10.4 all-gather.2
  256.4 9.8 reduce-scatter.18
  268.4 9.8 reduce-scatter.20
  295.1 128.5 all-reduce.3
  430.3 99.2 reduce-scatter.12
  535.7 118.1 reduce-scatter.10
  661.4 134.8 reduce-scatter.14
  802.8 134.4 reduce-scatter.16
where the time goes:
time: 953 us; the launch traced here: 946 us
  waiting for transfers between devices  576 us (60%)
  matrix products  217 us (23%)
  local copies, waits for them, and re-layouts  78.4 us (8%)
  blocking collectives  44.8 us (5%)
  between operations  15.3 us (2%)
  other arithmetic  14.1 us (1%)
    reduce_scatter x1, waiting for transfers between devices, per_device(): lax.psum_scatter(weight_terms[2], ('dp', 'blk'), scatter_dimension=0, til...  142 us
    reduce_scatter x1, waiting for transfers between devices, per_device(): lax.psum_scatter(weight_terms[3], ('dp', 'blk'), scatter_dimension=0, til...  141 us
    reduce_scatter x1, waiting for transfers between devices, per_device(): lax.psum_scatter(weight_terms[0], ('dp', 'blk'), scatter_dimension=0, til...  124 us
    reduce_scatter x1, waiting for transfers between devices, per_device(): lax.psum_scatter(weight_terms[1], ('dp', 'blk'), scatter_dimension=0, til...  106 us
    unnamed x83, local copies, waits for them, and re-layouts  52.4 us
    psum x1, waiting for transfers between devices, per_device(): lax.psum((table_part, ln1_gain_grad, ln1_shift_grad, query_bias_grad, val...  49.8 us
    psum x1, blocking collectives, per_device(): lax.psum((table_part, ln1_gain_grad, ln1_shift_grad, query_bias_grad, val...  42.1 us
    dot_general x4, matrix products, weight_product(): lax.dot_general(flat_left, flat_right, (((0,), (0,)), ((), ())), preferre...  27.7 us
  transfers between devices with their start and end apart: 9, of which 8 were waited for; matrix products, arithmetic and copies ran while one was open for 7% of the time, Pallas kernels for 0%

commit v1 on v0

v1 whole, which is shorter than its diff:
```python
import functools

import jax
import jax.numpy as jnp
import numpy as np
from jax import lax
from jax.experimental import pallas as pl
from jax.experimental.pallas import tpu as pltpu
from jax.sharding import PartitionSpec as P

HD = 64
SEG_MOST = 196
EPS = 1e-06
inv_root_two = 0.7071067811865476
inv_root_two_pi = 0.3989422804014327
BF = jnp.bfloat16
F32 = jnp.float32
MIB = 1 << 20


def dot_nn(a, b):
    return jnp.dot(a, b, preferred_element_type=F32)


def dot_nt(a, b):
    return lax.dot_general(a, b, (((1,), (1,)), ((), ())), preferred_element_type=F32)


def dot_tn(a, b):
    return lax.dot_general(a, b, (((0,), (0,)), ((), ())), preferred_element_type=F32)


def normalise(hidden):
    mean = jnp.mean(hidden, -1, keepdims=True)
    centred = hidden - mean
    inv = lax.rsqrt(jnp.mean(centred * centred, -1, keepdims=True) + EPS)
    return centred * inv, inv


def norm_back(grad, normal, inv, gain):
    scaled = grad * gain
    centre = jnp.mean(scaled, -1, keepdims=True)
    along = jnp.mean(scaled * normal, -1, keepdims=True)
    return inv * (scaled - centre - normal * along)


def column_sum(v):
    return jnp.sum(v, axis=0, keepdims=True)


def params(vmem):
    return pltpu.CompilerParams(vmem_limit_bytes=vmem * MIB)


def cost(flops, bytes_accessed, trans=0):
    return pl.CostEstimate(
        flops=int(flops), bytes_accessed=int(bytes_accessed), transcendentals=int(trans)
    )


def whole(shape):
    return pl.BlockSpec(shape, lambda *_: (0,) * len(shape))


def embed_kernel(x_ref, seg_ref, pos_ref, table_ref, gain_ref, shift_ref, h0_ref, n1_ref):
    half, width = x_ref.shape
    places = table_ref.shape[0]
    hot = (lax.broadcasted_iota(jnp.int32, (places, half), 0) == pos_ref[...]).astype(F32).astype(BF)
    hidden0 = x_ref[...].astype(F32) + dot_tn(hot, table_ref[...])
    h0_ref[...] = hidden0
    normal, _ = normalise(hidden0)
    n1_ref[:, :width] = (normal * gain_ref[...] + shift_ref[...]).astype(BF)
    seg_hot = (lax.broadcasted_iota(jnp.int32, (8, half), 0) == seg_ref[...]).astype(F32).astype(BF)
    eye = (
        lax.broadcasted_iota(jnp.int32, (8, 128), 0) == lax.broadcasted_iota(jnp.int32, (8, 128), 1)
    ).astype(F32).astype(BF)
    n1_ref[:, width:] = dot_tn(seg_hot, eye).astype(BF)


def embed(x, seg, pos, table, gain, shift):
    half, width = x.shape
    return pl.pallas_call(
        embed_kernel,
        out_shape=(
            jax.ShapeDtypeStruct((half, width), F32),
            jax.ShapeDtypeStruct((half, width + 128), BF),
        ),
        compiler_params=params(24),
        cost_estimate=cost(2 * half * width * 256, half * width * 8),
        name="embed",
    )(x, seg, pos, table, gain, shift)


def qkv_kernel(n1_ref, w_ref, qb_ref, vb_ref, out_ref):
    j = pl.program_id(0)
    width = qb_ref.shape[1]
    product = dot_nn(n1_ref[:, :width], w_ref[...])

    @pl.when(j == 0)
    def _():
        out_ref[0] = ((product + qb_ref[...]).astype(BF).astype(F32) * 0.125).astype(BF)

    @pl.when(j == 1)
    def _():
        out_ref[0] = product.astype(BF)

    @pl.when(j == 2)
    def _():
        out_ref[0] = (product + vb_ref[...]).astype(BF)


def qkv_own(n1, w, qb, vb):
    half = n1.shape[0]
    width = w.shape[0]
    return pl.pallas_call(
        qkv_kernel,
        grid=(3,),
        in_specs=[
            whole(n1.shape),
            pl.BlockSpec((width, width), lambda j: (0, j)),
            whole(qb.shape),
            whole(vb.shape),
        ],
        out_specs=pl.BlockSpec((1, half, width), lambda j: (j, 0, 0)),
        out_shape=jax.ShapeDtypeStruct((3, half, width), BF),
        compiler_params=params(24),
        cost_estimate=cost(6 * half * width * width, 6 * width * width + 8 * half * width),
        name="qkv_own",
    )(n1, w, qb, vb)


def lanes_of(shape, head):
    return (lax.broadcasted_iota(jnp.int32, shape, 1) % 128 < HD) == (head % 2 == 0)


def attend_kernel(
    blk_ref, q_ref, k_ref, v_ref, wk_ref, wv_ref, vb_ref, hot_ref, n1o_ref,
    att_ref, p_ref, kh_ref, vh_ref, bias_ref, kcat_ref, vcat_ref,
):
    half = q_ref.shape[1]
    halo = kh_ref.shape[0]
    width = wk_ref.shape[0]
    group = q_ref.shape[2]
    start = pl.multiple_of(blk_ref[0] * (half - halo), 16)

    @pl.when(pl.program_id(0) == 0)
    def _():
        hot = hot_ref[...]
        bias_ref[:, :half] = (dot_nt(hot, hot) - 1.0) * 1e9
        bias_ref[:, half:] = (dot_nt(hot, n1o_ref[pl.ds(start, halo), width:]) - 1.0) * 1e9

    n1h = n1o_ref[pl.ds(start, halo), :width]
    kh = dot_nn(n1h, wk_ref[...]).astype(BF)
    vh = (dot_nn(n1h, wv_ref[...]) + vb_ref[...]).astype(BF)
    kh_ref[...] = kh
    vh_ref[...] = vh
    kcat_ref[:half, :] = k_ref[0]
    kcat_ref[half:, :] = kh
    vcat_ref[:half, :] = v_ref[0]
    vcat_ref[half:, :] = vh
    for pair in range(group // 128):
        cols = slice(pair * 128, pair * 128 + 128)
        q = q_ref[0, :, cols]
        keys = kcat_ref[:, cols]
        values = vcat_ref[:, cols]
        outs = []
        for head in range(2):
            q_one = jnp.where(lanes_of(q.shape, head), q, jnp.zeros_like(q))
            scores = dot_nt(q_one, keys) + bias_ref[...]
            top = jnp.max(scores, -1, keepdims=True)
            weight = jnp.exp(scores - top)
            probs = (weight * (1.0 / jnp.sum(weight, -1, keepdims=True))).astype(BF)
            p_ref[2 * pair + head] = probs
            outs.append(dot_nn(probs, values))
        att_ref[:, cols] = jnp.where(lanes_of(outs[0].shape, 0), outs[0], outs[1]).astype(BF)


def attend(blk, qkv, w, vb, n1, n1o, halo):
    _, half, width = qkv.shape
    group = 256
    steps = width // group
    heads = width // HD
    keys = half + halo
    return pl.pallas_call(
        attend_kernel,
        grid_spec=pltpu.PrefetchScalarGridSpec(
            num_scalar_prefetch=1,
            grid=(steps,),
            in_specs=[
                pl.BlockSpec((1, half, group), lambda g, b: (0, 0, g)),
                pl.BlockSpec((1, half, group), lambda g, b: (1, 0, g)),
                pl.BlockSpec((1, half, group), lambda g, b: (2, 0, g)),
                pl.BlockSpec((width, group), lambda g, b: (0, steps + g)),
                pl.BlockSpec((width, group), lambda g, b: (0, 2 * steps + g)),
                pl.BlockSpec((1, group), lambda g, b: (0, g)),
                pl.BlockSpec((half, 128), lambda g, b: (0, width // 128)),
                whole(n1o.shape),
            ],
            out_specs=[
                pl.BlockSpec((half, group), lambda g, b: (0, g)),
                pl.BlockSpec((group // HD, half, keys), lambda g, b: (g, 0, 0)),
                pl.BlockSpec((halo, group), lambda g, b: (0, g)),
                pl.BlockSpec((halo, group), lambda g, b: (0, g)),
            ],
            scratch_shapes=[
                pltpu.VMEM((half, keys), F32),
                pltpu.VMEM((keys, group), BF),
                pltpu.VMEM((keys, group), BF),
            ],
        ),
        out_shape=(
            jax.ShapeDtypeStruct((half, width), BF),
            jax.ShapeDtypeStruct((heads, half, keys), BF),
            jax.ShapeDtypeStruct((halo, width), BF),
            jax.ShapeDtypeStruct((halo, width), BF),
        ),
        compiler_params=params(40),
        cost_estimate=cost(16 * half * keys * width, 2 * heads * half * keys, heads * half * keys),
        name="attend",
    )(blk, qkv, qkv, qkv, w, w, vb, n1, n1o)


def feed_kernel(
    blk_ref, att_ref, h0_ref, cot_ref, wo_ref, bo_ref, g2_ref, s2_ref, w1_ref, b1_ref, w2_ref, b2_ref,
    res_ref, h1_ref, n2_ref, act_ref, gs_ref, gk_ref, gn_ref, b1g_ref, mixed_ref,
):
    i = pl.program_id(0)
    steps = pl.num_programs(0)

    @pl.when(i == 0)
    def _():
        hidden1 = h0_ref[...] + dot_nn(att_ref[...], wo_ref[...]) + bo_ref[...]
        h1_ref[...] = hidden1
        normal, _ = normalise(hidden1)
        n2_ref[...] = (normal * g2_ref[...] + s2_ref[...]).astype(BF)
        mixed_ref[...] = hidden1 + b2_ref[...]
        gn_ref[...] = jnp.zeros_like(gn_ref)

    pre = dot_nn(n2_ref[...], w1_ref[...]) + b1_ref[...]
    grad_act = dot_nt(cot_ref[...], w2_ref[...])
    cdf = 0.5 + 0.5 * lax.erf(pre * inv_root_two)
    act = (pre * cdf).astype(BF)
    act_ref[...] = act
    slope = cdf + pre * jnp.exp(-0.5 * pre * pre) * inv_root_two_pi
    grad32 = grad_act * slope
    grad_pre = grad32.astype(BF)
    b1g_ref[...] = column_sum(grad_pre.astype(F32))

    @pl.when(i < steps // 2)
    def _():
        gs_ref[...] = grad_pre

    @pl.when(i >= steps // 2)
    def _():
        gk_ref[...] = grad_pre

    mixed_ref[...] += dot_nn(act, w2_ref[...])
    gn_ref[...] += dot_nt(grad_pre, w1_ref[...])

    @pl.when(i == steps - 1)
    def _():
        res_ref[...] = mixed_ref[...].astype(BF)


def feed(blk, att, h0, cot, wo, bo, g2, s2, w1, b1, w2, b2):
    half, width = h0.shape
    hidden = w1.shape[1]
    chunk = 384
    steps = hidden // chunk
    per = steps // 2

    def place(i, b):
        return jnp.where(i < per, (1 - b[0]) * per + i, b[0] * per + i - per)

    return pl.pallas_call(
        feed_kernel,
        grid_spec=pltpu.PrefetchScalarGridSpec(
            num_scalar_prefetch=1,
            grid=(steps,),
            in_specs=[
                whole(att.shape),
                whole(h0.shape),
                whole(cot.shape),
                whole(wo.shape),
                whole(bo.shape),
                whole(g2.shape),
                whole(s2.shape),
                pl.BlockSpec((width, chunk), lambda i, b: (0, place(i, b))),
                pl.BlockSpec((1, chunk), lambda i, b: (0, place(i, b))),
                pl.BlockSpec((chunk, width), lambda i, b: (place(i, b), 0)),
                whole(b2.shape),
            ],
            out_specs=[
                whole((half, width)),
                whole((half, width)),
                whole((half, width)),
                pl.BlockSpec((half, chunk), lambda i, b: (0, place(i, b))),
                pl.BlockSpec((half, chunk), lambda i, b: (0, jnp.minimum(i, per - 1))),
                pl.BlockSpec((half, chunk), lambda i, b: (0, jnp.maximum(i - per, 0))),
                whole((half, width)),
                pl.BlockSpec((1, chunk), lambda i, b: (0, place(i, b))),
            ],
            scratch_shapes=[pltpu.VMEM((half, width), F32)],
        ),
        out_shape=(
            jax.ShapeDtypeStruct((half, width), BF),
            jax.ShapeDtypeStruct((half, width), F32),
            jax.ShapeDtypeStruct((half, width), BF),
            jax.ShapeDtypeStruct((half, hidden), BF),
            jax.ShapeDtypeStruct((half, hidden // 2), BF),
            jax.ShapeDtypeStruct((half, hidden // 2), BF),
            jax.ShapeDtypeStruct((half, width), F32),
            jax.ShapeDtypeStruct((1, hidden), F32),
        ),
        compiler_params=params(40),
        cost_estimate=cost(
            8 * half * width * hidden + 2 * half * width * width, 4 * width * hidden, 2 * half * hidden
        ),
        name="feed",
    )(blk, att, h0, cot, wo, bo, g2, s2, w1, b1, w2, b2)


def mid_kernel(gn_ref, h1_ref, cot_ref, wo_ref, g2_ref, gh_ref, gb_ref, ga_ref, sums_ref):
    normal, inv = normalise(h1_ref[...])
    grad = gn_ref[...]
    cot = cot_ref[...].astype(F32)
    sums_ref[0:1, :] = column_sum(grad * normal)
    sums_ref[1:2, :] = column_sum(grad)
    grad_hidden1 = cot + norm_back(grad, normal, inv, g2_ref[...])
    gh_ref[...] = grad_hidden1
    branch = grad_hidden1.astype(BF)
    gb_ref[...] = branch
    sums_ref[2:3, :] = column_sum(branch.astype(F32))
    sums_ref[3:4, :] = column_sum(cot)
    ga_ref[...] = dot_nt(branch, wo_ref[...]).astype(BF)


def mid(gn, h1, cot, wo, g2):
    half, width = h1.shape
    return pl.pallas_call(
        mid_kernel,
        out_shape=(
            jax.ShapeDtypeStruct((half, width), F32),
            jax.ShapeDtypeStruct((half, width), BF),
            jax.ShapeDtypeStruct((half, width), BF),
            jax.ShapeDtypeStruct((4, width), F32),
        ),
        compiler_params=params(24),
        cost_estimate=cost(2 * half * width * width, 14 * half * width),
        name="mid",
    )(gn, h1, cot, wo, g2)


class Plan:
    def __init__(self, ndp):
        self.groups = min(16, ndp)
        self.bits = self.groups.bit_length() - 1
        self.rest = ndp // self.groups
        order = list(range(self.bits))
        swapped = order[:2][::-1] + order[2:]
        self.orders = (order, swapped)
        self.index = tuple(self.rank(o) for o in self.orders)

    def rank(self, order):
        table = []
        for p in range(self.groups):
            code = 0
            for bit in order:
                code = 2 * code + ((p >> bit) & 1)
            table.append(self.groups - 1 - code)
        return table


def store_block(refs, plan, piece, p, row, block):
    place = plan.index[piece][p]
    first = plan.groups // 2
    ref = refs[2 * piece + (place >= first)]
    ref[place % first, row : row + block.shape[0], :] = block


def feed_weights_kernel(
    plan, own_ref, act_ref, acto_ref, cot_ref, coto_ref, n2_ref, n2o_ref, g_ref, go_ref, *rest
):
    outs, acc_ref = rest[:4], rest[4]
    i = pl.program_id(0)
    own = own_ref[0]
    chunk = act_ref.shape[1]
    steps = pl.num_programs(0)
    per = plan.groups // steps
    rows2 = chunk // per
    rows1 = n2_ref.shape[1] // plan.groups
    acc_ref[...] = dot_tn(act_ref[...], cot_ref[...]) + dot_tn(acto_ref[...], coto_ref[...])
    for step in range(steps):

        @pl.when(i == step)
        def _():
            for low in range(per):
                source = pl.multiple_of(((own % per) ^ low) * rows2, 16)
                for piece in range(2):
                    block = acc_ref[pl.ds(source + piece * (rows2 // 2), rows2 // 2), :]
                    store_block(outs, plan, piece, step * per + low, 0, block.astype(BF))

    acc_ref[...] = dot_tn(n2_ref[...], g_ref[...]) + dot_tn(n2o_ref[...], go_ref[...])
    for step in range(steps):

        @pl.when(i == step)
        def _():
            for p in range(plan.groups):
                source = pl.multiple_of((own ^ p) * rows1, 16)
                block = acc_ref[pl.ds(source, rows1), :]
                store_block(
                    outs, plan, step // (steps // 2), p,
                    rows2 // 2 + (step % (steps // 2)) * rows1, block.astype(BF),
                )


def feed_weights(plan, own, blk, act, acto, cot, coto, n2, n2o, g, go):
    half, hidden = act.shape
    width = n2.shape[1]
    cols = width // 2
    steps = 4
    chunk = hidden // steps
    per = plan.groups // steps
    rows = hidden // plan.groups // 2 + (steps // 2) * (width // plan.groups)
    part = jax.ShapeDtypeStruct((plan.groups // 2, rows, cols), BF)

    def place(i, o, b):
        return (0, (o[0] // per) ^ i)

    return pl.pallas_call(
        functools.partial(wrap_two, feed_weights_kernel, plan),
        grid_spec=pltpu.PrefetchScalarGridSpec(
            num_scalar_prefetch=2,
            grid=(steps,),
            in_specs=[
                pl.BlockSpec((half, chunk), place),
                pl.BlockSpec((half, chunk), place),
                pl.BlockSpec((half, cols), lambda i, o, b: (0, b[0])),
                pl.BlockSpec((half, cols), lambda i, o, b: (0, b[0])),
                whole(n2.shape),
                whole(n2o.shape),
                pl.BlockSpec((half, cols), lambda i, o, b: (0, i)),
                pl.BlockSpec((half, cols), lambda i, o, b: (0, i)),
            ],
            out_specs=[whole(part.shape)] * 4,
            scratch_shapes=[pltpu.VMEM((width, cols), F32)],
        ),
        out_shape=(part,) * 4,
        compiler_params=params(40),
        cost_estimate=cost(4 * half * width * hidden, 2 * width * hidden + 8 * half * hidden),
        name="feed_weights",
    )(own, blk, act, acto, cot, coto, n2, n2o, g, go)


def wrap_two(kernel, plan, own_ref, blk_ref, *refs):
    kernel(plan, own_ref, *refs)


def attend_back_kernel(
    blk_ref, q_ref, k_ref, v_ref, kh_ref, vh_ref, p_ref, ga_ref, d_ref, dh_ref, kcat_ref, vcat_ref
):
    half = q_ref.shape[1]
    kcat_ref[:half, :] = k_ref[0]
    kcat_ref[half:, :] = kh_ref[...]
    vcat_ref[:half, :] = v_ref[0]
    vcat_ref[half:, :] = vh_ref[...]
    q = q_ref[0]
    grad = ga_ref[...]
    dqs, dks, dvs = [], [], []
    for head in range(2):
        grad_one = jnp.where(lanes_of(grad.shape, head), grad, jnp.zeros_like(grad))
        grad_probs = dot_nt(grad_one, vcat_ref[...])
        probs = p_ref[head].astype(F32)
        row = jnp.sum(probs * grad_probs, -1, keepdims=True)
        grad_scores = (probs * (grad_probs - row)).astype(BF)
        dqs.append(dot_nn(grad_scores, kcat_ref[...]))
        dks.append(dot_tn(grad_scores, q))
        dvs.append(dot_tn(p_ref[head], grad))
    first = lanes_of(dqs[0].shape, 0)
    d_ref[0] = (jnp.where(first, dqs[0], dqs[1]) * 0.125).astype(BF)
    first = lanes_of(dks[0].shape, 0)
    dk = jnp.where(first, dks[0], dks[1]).astype(BF)
    dv = jnp.where(first, dvs[0], dvs[1]).astype(BF)
    d_ref[1] = dk[:half]
    d_ref[2] = dv[:half]
    dh_ref[0] = dk[half:]
    dh_ref[1] = dv[half:]


def attend_back(side, qkv, kh, vh, probs, ga):
    _, half, width = qkv.shape
    halo = kh.shape[0]
    keys = half + halo
    steps = width // 256

    def col(i, s):
        return s[0] * steps + i

    return pl.pallas_call(
        attend_back_kernel,
        grid_spec=pltpu.PrefetchScalarGridSpec(
            num_scalar_prefetch=1,
            grid=(steps,),
            in_specs=[
                pl.BlockSpec((1, half, 128), lambda i, s: (0, 0, col(i, s))),
                pl.BlockSpec((1, half, 128), lambda i, s: (1, 0, col(i, s))),
                pl.BlockSpec((1, half, 128), lambda i, s: (2, 0, col(i, s))),
                pl.BlockSpec((halo, 128), lambda i, s: (0, col(i, s))),
                pl.BlockSpec((halo, 128), lambda i, s: (0, col(i, s))),
                pl.BlockSpec((2, half, keys), lambda i, s: (col(i, s), 0, 0)),
                pl.BlockSpec((half, 128), lambda i, s: (0, col(i, s))),
            ],
            out_specs=[
                pl.BlockSpec((3, half, 128), lambda i, s: (0, 0, i)),
                pl.BlockSpec((2, halo, 128), lambda i, s: (0, 0, i)),
            ],
            scratch_shapes=[pltpu.VMEM((keys, 128), BF), pltpu.VMEM((keys, 128), BF)],
        ),
        out_shape=(
            jax.ShapeDtypeStruct((3, half, width // 2), BF),
            jax.ShapeDtypeStruct((2, halo, width // 2), BF),
        ),
        compiler_params=params(40),
        cost_estimate=cost(16 * half * keys * width, half * keys * width // HD),
        name="attend_back",
    )(side, qkv, qkv, qkv, kh, vh, probs, ga)


def add_rows(ref, which, start, halo, extra):
    part = ref[which, pl.ds(start, halo), :].astype(F32) + extra.astype(F32)
    ref[which, pl.ds(start, halo), :] = part.astype(BF)


def attend_weights_kernel(
    plan, own_ref, blk_ref, n1_ref, n1o_ref, d_ref, dh_ref, do_ref, dho_ref, att_ref, atto_ref,
    gb_ref, gbo_ref, *rest
):
    outs, acc_ref, mine_ref, other_ref = rest[:4], rest[4], rest[5], rest[6]
    half = n1_ref.shape[0]
    halo = dh_ref.shape[1]
    width = att_ref.shape[1]
    own = own_ref[0]
    rows = width // plan.groups
    start = pl.multiple_of((1 - blk_ref[0]) * (half - halo), 16)
    start_other = pl.multiple_of(blk_ref[0] * (half - halo), 16)
    mine_ref[...] = d_ref[...]
    other_ref[...] = do_ref[...]
    for which in range(2):
        add_rows(mine_ref, 1 + which, start, halo, dho_ref[which])
        add_rows(other_ref, 1 + which, start_other, halo, dh_ref[which])
    for panel in range(4):
        if panel < 3:
            acc_ref[...] = dot_tn(n1_ref[:, :width], mine_ref[panel]) + dot_tn(
                n1o_ref[:, :width], other_ref[panel]
            )
        else:
            acc_ref[...] = dot_tn(att_ref[...], gb_ref[...]) + dot_tn(atto_ref[...], gbo_ref[...])
        for p in range(plan.groups):
            source = pl.multiple_of((own ^ p) * rows, 16)
            block = acc_ref[pl.ds(source, rows), :]
            store_block(outs, plan, panel // 2, p, (panel % 2) * rows, block.astype(BF))


def attend_weights(plan, own, blk, n1, n1o, d, dh, do, dho, att, atto, gb, gbo):
    half, width = att.shape
    cols = width // 2
    rows = 2 * (width // plan.groups)
    part = jax.ShapeDtypeStruct((plan.groups // 2, rows, cols), BF)
    return pl.pallas_call(
        functools.partial(attend_weights_kernel, plan),
        grid_spec=pltpu.PrefetchScalarGridSpec(
            num_scalar_prefetch=2,
            grid=(1,),
            in_specs=[
                whole(n1.shape),
                whole(n1o.shape),
                whole(d.shape),
                whole(dh.shape),
                whole(do.shape),
                whole(dho.shape),
                whole(att.shape),
                whole(atto.shape),
                pl.BlockSpec((half, cols), lambda i, o, b: (0, b[0])),
                pl.BlockSpec((half, cols), lambda i, o, b: (0, b[0])),
            ],
            out_specs=[whole(part.shape)] * 4,
            scratch_shapes=[
                pltpu.VMEM((width, cols), F32),
                pltpu.VMEM(d.shape, BF),
                pltpu.VMEM(do.shape, BF),
            ],
        ),
        out_shape=(part,) * 4,
        compiler_params=params(40),
        cost_estimate=cost(8 * half * width * width, 4 * width * width + 24 * half * width),
        name="attend_weights",
    )(own, blk, n1, n1o, d, dh, do, dho, att, atto, gb, gbo)


def front_back_kernel(
    blk_ref, da_ref, db_ref, ha_ref, hb_ref, w_ref, h0_ref, gh_ref, g1_ref, pos_ref, sums_ref, b1_ref,
    gx_ref, small_ref, acc_ref,
):
    half, width = h0_ref.shape
    halo = ha_ref.shape[1]
    cols = width // 2
    places = small_ref.shape[0] - 12
    start = pl.multiple_of((1 - blk_ref[0]) * (half - halo), 16)
    acc_ref[0] = da_ref[...]
    acc_ref[1] = db_ref[...]
    for which in range(2):
        add_rows(acc_ref.at[0], 1 + which, start, halo, ha_ref[which])
        add_rows(acc_ref.at[1], 1 + which, start, halo, hb_ref[which])
    total = jnp.zeros((half, width), F32)
    for which in range(3):
        for side, ref in enumerate((acc_ref.at[0], acc_ref.at[1])):
            at = which * width + side * cols
            panel = ref[which]
            total = total + dot_nt(panel, w_ref[:, at : at + cols])
            if which == 0:
                small_ref[places + 2 : places + 3, side * cols : side * cols + cols] = column_sum(panel.astype(F32))
            if which == 2:
                small_ref[places + 3 : places + 4, side * cols : side * cols + cols] = column_sum(panel.astype(F32))
    normal, inv = normalise(h0_ref[...])
    small_ref[places : places + 1, :] = column_sum(total * normal)
    small_ref[places + 1 : places + 2, :] = column_sum(total)
    grad = (gh_ref[...] + norm_back(total, normal, inv, g1_ref[...])).astype(BF)
    gx_ref[...] = grad
    hot = (lax.broadcasted_iota(jnp.int32, (places, half), 0) == pos_ref[...]).astype(F32).astype(BF)
    small_ref[:places, :] = dot_nn(hot, grad)
    small_ref[places + 4 : places + 8, :] = sums_ref[...]
    for k in range(4):
        small_ref[places + 8 + k : places + 9 + k, :] = b1_ref[:, k * width : (k + 1) * width]


def front_back(blk, da, db, ha, hb, w, h0, gh, g1, pos, sums, b1, places):
    half, width = h0.shape
    return pl.pallas_call(
        front_back_kernel,
        grid_spec=pltpu.PrefetchScalarGridSpec(
            num_scalar_prefetch=1,
            grid=(1,),
            in_specs=[whole(a.shape) for a in (da, db, ha, hb, w, h0, gh, g1, pos, sums, b1)],
            out_specs=[whole((half, width)), whole((places + 12, width))],
            scratch_shapes=[pltpu.VMEM((2,) + da.shape, BF)],
        ),
        out_shape=(
            jax.ShapeDtypeStruct((half, width), BF),
            jax.ShapeDtypeStruct((places + 12, width), F32),
        ),
        compiler_params=params(40),
        cost_estimate=cost(6 * half * width * width, 6 * width * width + 20 * half * width),
        name="front_back",
    )(blk, da, db, ha, hb, w, h0, gh, g1, pos, sums, b1)


def swap(v):
    return lax.ppermute(v, "blk", [(0, 1), (1, 0)])


def across(v, ndp, flip):
    return lax.ppermute(v, "dp", [(i, i ^ flip) for i in range(ndp)])


def wide(v):
    return v.astype(F32)


def scatter_pairs(plan, ndp, parts):
    later = []
    for piece in range(2):
        sent, kept = parts[2 * piece], parts[2 * piece + 1]
        terms = [kept, across(sent, ndp, plan.rest << plan.orders[piece][0])]
        later.append(terms)
    count = plan.groups // 2
    if plan.bits > 1:
        for piece in range(2):
            h = count // 2
            out = sum(wide(t[:h]) for t in later[piece]).astype(BF)
            got = across(out, ndp, plan.rest << plan.orders[piece][1])
            later[piece] = [t[h:] for t in later[piece]] + [got]
        count //= 2
    for bit in range(2, plan.bits):
        h = count // 2
        if bit == 2:
            merged = [jnp.stack([sum(wide(t) for t in later[piece]) for piece in range(2)])]
        out = sum(wide(t[:, :h]) for t in merged).astype(BF)
        got = across(out, ndp, plan.rest << bit)
        merged = [t[:, h:] for t in merged] + [got]
        count //= 2
    if plan.bits <= 2:
        merged = [jnp.stack([sum(wide(t) for t in later[piece]) for piece in range(2)])]
    return sum(wide(t) for t in merged)[:, 0]


def rest_of(plan, ndp, value, rows):
    if plan.rest == 1:
        return value
    groups = [[g * plan.rest + i for i in range(plan.rest)] for g in range(plan.groups)]
    value = lax.psum(value, "dp", axis_index_groups=groups)
    return lax.dynamic_slice_in_dim(value, (lax.axis_index("dp") % plan.rest) * rows, rows, axis=value.ndim - 2)


def total_small(small, ndp):
    rows, width = small.shape
    blk = lax.axis_index("blk")
    cols = width // 2
    small = small.astype(BF)
    mine = lax.dynamic_slice_in_dim(small, blk * cols, cols, axis=1)
    other = swap(lax.dynamic_slice_in_dim(small, (1 - blk) * cols, cols, axis=1))
    total = wide(mine) + wide(other)
    for bit in reversed(range(ndp.bit_length() - 1)):
        low = total.astype(BF)
        total = wide(low) + wide(across(low, ndp, 1 << bit))
    low = total.astype(BF)
    both = swap(low)
    return wide(jnp.where(blk == 0, jnp.concatenate([low, both], 1), jnp.concatenate([both, low], 1)))


def per_device(
    ndp, inputs, segments, positions, pos_table, ln1_gain, ln1_shift, qkv_weight, query_bias,
    value_bias, out_weight, out_bias, ln2_gain, ln2_shift, fc1_weight, fc1_bias, fc2_weight,
    fc2_bias, cotangent,
):
    plan = Plan(ndp)
    x, cot = inputs[0], cotangent[0]
    half, width = x.shape
    hidden = fc1_weight.shape[1]
    places = pos_table.shape[0]
    halo = next(h for h in range(SEG_MOST - 1, half + 1) if (half + h) % 128 == 0 and (half - h) % 16 == 0)
    blk = lax.axis_index("blk")
    dp = lax.axis_index("dp")
    blk1 = blk.astype(jnp.int32).reshape(1)
    own1 = (dp // plan.rest).astype(jnp.int32).reshape(1)
    row = lambda v: v.reshape(1, -1)

    cot_other = swap(cot)
    hidden0, n1 = embed(x, segments, positions, pos_table, row(ln1_gain), row(ln1_shift))
    n1_other = swap(n1)
    qkv = qkv_own(n1, qkv_weight, row(query_bias), row(value_bias))
    att, probs, kh, vh = attend(blk1, qkv, qkv_weight, row(value_bias), n1, n1_other, halo)
    att_other = swap(att)
    result, hidden1, n2, act, grad_send, grad_keep, gn2, b1_grad = feed(
        blk1, att, hidden0, cot, out_weight, row(out_bias), row(ln2_gain), row(ln2_shift),
        fc1_weight, row(fc1_bias), fc2_weight, row(fc2_bias),
    )
    act_other, n2_other, grad_other = swap(act), swap(n2), swap(grad_send)
    gh1, gb, ga, sums = mid(gn2, hidden1, cot, out_weight, row(ln2_gain))
    gb_other = swap(gb)
    first = feed_weights(plan, own1, blk1, act, act_other, cot, cot_other, n2, n2_other, grad_keep, grad_other)
    summed_first = scatter_pairs(plan, ndp, first)

    d_send, h_send = attend_back(1 - blk1, qkv, kh, vh, probs, ga)
    d_other, h_other = swap(d_send), swap(h_send)
    d_keep, h_keep = attend_back(blk1, qkv, kh, vh, probs, ga)
    h_late = swap(h_keep)
    second = attend_weights(
        plan, own1, blk1, n1, n1_other, d_keep, h_keep, d_other, h_other, att, att_other, gb, gb_other
    )
    summed_second = scatter_pairs(plan, ndp, second)
    is0 = blk == 0
    pick = lambda a, b: jnp.where(is0, a, b)
    grad_x, small = front_back(
        blk1, pick(d_keep, d_send), pick(d_send, d_keep), pick(h_other, h_late), pick(h_late, h_other),
        qkv_weight, hidden0, gh1, row(ln1_gain), positions, sums, b1_grad, places,
    )
    small = total_small(small, ndp)

    rg = width // ndp
    r1 = width // plan.groups
    cols = width // 2
    r2 = hidden // plan.groups // 2

    def finish(value, lead):
        parts = value.reshape(lead, 2, -1, cols)
        mine = lax.dynamic_index_in_dim(parts, blk, 1, keepdims=False)
        got = swap(lax.dynamic_index_in_dim(parts, 1 - blk, 1, keepdims=False))
        return pick(jnp.stack([mine, got], 2), jnp.stack([got, mine], 2))

    fc2_block = rest_of(plan, ndp, summed_first[:, :r2].reshape(1, 2 * r2, cols), hidden // ndp)
    fc1_block = rest_of(plan, ndp, summed_first[:, r2:].reshape(4, r1, cols), rg)
    att_block = rest_of(plan, ndp, summed_second.reshape(4, r1, cols), rg)
    fc2_grad = finish(fc2_block, 1).reshape(-1, width)
    fc1_own = finish(fc1_block, 4)
    fc1_grad = fc1_own.transpose(1, 2, 0, 3).reshape(rg // 2, hidden)
    att_own = finish(att_block, 4).reshape(4, rg // 2, width)
    qkv_grad = att_own[:3].transpose(1, 0, 2).reshape(rg // 2, 3 * width)
    out_grad = att_own[3]
    vec = lambda k: small[places + k]
    return (
        result[None], grad_x[None], small[:places], vec(0), vec(1), qkv_grad, vec(2), vec(3), out_grad,
        vec(6), vec(4), vec(5), fc1_grad, small[places + 8 :].reshape(-1), fc2_grad, vec(7),
    )


def solution(mesh):
    split = P("dp", "blk", None)
    ids = P("dp", "blk")
    both = P(("dp", "blk"), None)
    none = P()
    return jax.shard_map(
        functools.partial(per_device, mesh.shape["dp"]),
        mesh=mesh,
        in_specs=(split, ids, ids) + (none,) * 14 + (split,),
        out_specs=(
            split, split, none, none, none, both, none, none, both, none, none, none, both, none, both, none,
        ),
        check_vma=False,
    )
```

time: 953 us -> 208 us (0.22)
  waiting for transfers between devices: 576 us -> 61.8 us
  matrix products: 217 us -> 0 us
  Pallas kernels: 0 us -> 71.9 us
  blocking collectives: 44.8 us -> 0 us
  local copies, waits for them, and re-layouts: 78.4 us -> 37.7 us
  starting transfers between devices: 0.62 us -> 23.4 us
  between operations: 15.3 us -> 1.1 us
    reduce_scatter x4 -> x0, waiting for transfers between devices: 514 us -> none  [the longest x1 142 us: per_device(): lax.psum_scatter(weight_terms[2], ('dp', 'blk'), scatter_dimension=0, til...]
    dot_general x98 -> x0, matrix products: 217 us -> none  [the longest x4 27.7 us: weight_product(): lax.dot_general(flat_left, flat_right, (((0,), (0,)), ((), ())), preferre...]
    pallas_call x0 -> x10, Pallas kernels: none -> 71.9 us  [the longest x1 17.8 us: feed(): pl.pallas_call(feed_kernel, grid_spec=pltpu.PrefetchScalarGridSpec(num_sc...]
    ppermute x0 -> x31, waiting for transfers between devices: none -> 61.8 us  [the longest x16 59 us: across(): return lax.ppermute(v, 'dp', [(i, i ^ flip) for i in range(ndp)])]
    psum x1 -> x0, waiting for transfers between devices: 49.8 us -> none  [per_device(): lax.psum((table_part, ln1_gain_grad, ln1_shift_grad, query_bias_grad, val...]
    psum x1 -> x0, blocking collectives: 42.1 us -> none  [per_device(): lax.psum((table_part, ln1_gain_grad, ln1_shift_grad, query_bias_grad, val...]
    unnamed x83 -> x79, local copies, waits for them, and re-layouts: 52.4 us -> 27.3 us
    ppermute x0 -> x31, starting transfers between devices: none -> 23.4 us  [the longest x16 19.3 us: across(): return lax.ppermute(v, 'dp', [(i, i ^ flip) for i in range(ndp)])]
  transfers between devices with their start and end apart: 9 -> 31, of which waited for: 8 -> 11; matrix products, arithmetic and copies ran while one was open for 7% -> 9% of each run, Pallas kernels for 0% -> 16%
where the time goes in v1:
time: 208 us; the launch traced here: 207 us
  Pallas kernels  71.9 us (35%)
  waiting for transfers between devices  61.8 us (30%)
  local copies, waits for them, and re-layouts  37.7 us (18%)
  starting transfers between devices  23.4 us (11%)
  other arithmetic  11.4 us (5%)
    ppermute x16, waiting for transfers between devices, across(): return lax.ppermute(v, 'dp', [(i, i ^ flip) for i in range(ndp)])  59 us
    unnamed x79, local copies, waits for them, and re-layouts  27.3 us
    ppermute x16, starting transfers between devices, across(): return lax.ppermute(v, 'dp', [(i, i ^ flip) for i in range(ndp)])  19.3 us
    pallas_call x1, Pallas kernels, feed(): pl.pallas_call(feed_kernel, grid_spec=pltpu.PrefetchScalarGridSpec(num_sc...  17.8 us
    pallas_call x2, Pallas kernels, attend_back(): pl.pallas_call(attend_back_kernel, grid_spec=pltpu.PrefetchScalarGridSpec...  15.7 us
    pallas_call x1, Pallas kernels, feed_weights(): pl.pallas_call(functools.partial(wrap_two, feed_weights_kernel, plan), gr...  10.8 us
    pallas_call x1, Pallas kernels, attend(): pl.pallas_call(attend_kernel, grid_spec=pltpu.PrefetchScalarGridSpec(num_...  10.4 us
    pallas_call x1, Pallas kernels, attend_weights(): pl.pallas_call(functools.partial(attend_weights_kernel, plan), grid_spec=...  5.81 us
  transfers between devices with their start and end apart: 31, of which 11 were waited for; matrix products, arithmetic and copies ran while one was open for 9% of the time, Pallas kernels for 16%

profile of v1, /device:TPU:0, one launch (start us, length us, event | category | flops | bytes accessed | tf_op | source)
XLA Modules:
  0.0 207.2 jit_solution(9125125336913712051)
XLA Ops:
  2.0 1.1 copy-done.13
  3.1 1.0 copy-done.16
  5.4 1.6 embed.1
  7.0 1.0 copy-done.5
  12.6 2.0 copy-done
  14.7 3.7 %qkv_own.1.q_ref.k_ref.v_ref = bf16[3,392,768]{2,1,0:T(8,128)(2,1)S(1)} custom-call(bf16[392,896]{1,0:T(8,128)(2,1)} %get-tuple-element.48.n1_ref.hot_ref, bf16[768,2304]{1,0:T(8,128)(2,1)S(1)} %copy-done, f32[1,768]{1,0:T(1,128)S(1)} %reshape.113.qb_ref, f32[1,768]{1,0:T(1,128)S(1)} %reshape.114.vb_ref), custom_call_target="tpu_custom_call" | custom-call | flops 1387266048 | bytes 5947392 | tf_op jit(solution)/shard_map/qkv_own/pallas_call | solution.py:115
  18.4 10.4 %attend.1 = (bf16[392,768]{1,0:T(8,128)(2,1)}, bf16[12,392,640]{2,1,0:T(8,128)(2,1)S(1)}, bf16[248,768]{1,0:T(8,128)(2,1)S(1)}, bf16[248,768]{1,0:T(8,128)(2,1)S(1)}) custom-call(s32[1]{0:T(128)} %bitcast.blk_ref, bf16[3,392,768]{2,1,0:T(8,128)(2,1)S(1)} %qkv_own.1.q_ref.k_ref.v_ref, bf16[3,392,768]{2,1,0:T(8,128)(2,1)S(1)} %qkv_own.1.q_ref.k_ref.v_ref, ...), custom_call_target="tpu_custom_call" | custom-call | flops 3082813440 | bytes 6021120 | tf_op jit(solution)/shard_map/attend/pallas_call | solution.py:184
  28.9 2.6 %copy-done.2 = bf16[12,392,640]{2,1,0:T(8,128)(2,1)} copy-done((bf16[12,392,640]{2,1,0:T(8,128)(2,1)}, bf16[12,392,640]{2,1,0:T(8,128)(2,1)S(1)}, u32[]{:S(2)}) %copy-start.2) | copy-done | bytes 6021144
  31.5 17.8 %feed.1 = (bf16[392,768]{1,0:T(8,128)(2,1)}, f32[392,768]{1,0:T(8,128)S(1)}, bf16[392,768]{1,0:T(8,128)(2,1)S(1)}, bf16[392,3072]{1,0:T(8,128)(2,1)}, bf16[392,1...) custom-call(s32[1]{0:T(128)} %bitcast.blk_ref, ...), custom_call_target="tpu_custom_call" | custom-call | flops 7861174272 | bytes 9437184 | tf_op jit(solution)/shard_map/feed/pallas_call | solution.py:275
  49.2 2.0 mid.1
  51.2 1.1 copy-done.8
  52.3 2.7 %copy-done.3 = bf16[12,392,640]{2,1,0:T(8,128)(2,1)S(1)} copy-done((bf16[12,392,640]{2,1,0:T(8,128)(2,1)S(1)}, bf16[12,392,640]{2,1,0:T(8,128)(2,1)}, u32[]{:S(2)}) %copy-start.3) | copy-done | bytes 6021144
  55.0 7.9 %attend_back.2 = (bf16[3,392,384]{2,1,0:T(8,128)(2,1)S(1)}, bf16[2,248,384]{2,1,0:T(8,128)(2,1)}) custom-call(s32[1]{0:T(128)} %bitcast.blk_ref, bf16[3,392,768]{2,1,0:T(8,128)(2,1)S(1)} %qkv_own.1.q_ref.k_ref.v_ref, bf16[3,392,768]{2,1,0:T(8,128)(2,1)S(1)} %qkv_own.1.q_ref.k_ref.v_ref, bf16[3,392,768]{2,1,0:T(8,128)(2,1)S(1)} %qkv_own.1.q_ref.k_ref.v_ref, ...), custom_call_target="tpu_custom_call" | custom-call | flops 3082813440 | bytes 3010560 | tf_op jit(solution)/shard_map/attend_back/pallas_call | solution.py:499
  62.9 0.9 copy-done.11
  64.3 2.7 %copy-done.4 = bf16[12,392,640]{2,1,0:T(8,128)(2,1)S(1)} copy-done((bf16[12,392,640]{2,1,0:T(8,128)(2,1)S(1)}, bf16[12,392,640]{2,1,0:T(8,128)(2,1)}, u32[]{:S(2)}) %copy-start.4) | copy-done | bytes 6021144
  67.0 7.8 %attend_back.3 = (bf16[3,392,384]{2,1,0:T(8,128)(2,1)}, bf16[2,248,384]{2,1,0:T(8,128)(2,1)}) custom-call(s32[1]{0:T(128)S(6)} %sub.6.blk_ref, bf16[3,392,768]{2,1,0:T(8,128)(2,1)S(1)} %qkv_own.1.q_ref.k_ref.v_ref, bf16[3,392,768]{2,1,0:T(8,128)(2,1)S(1)} %qkv_own.1.q_ref.k_ref.v_ref, bf16[3,392,768]{2,1,0:T(8,128)(2,1)S(1)} %qkv_own.1.q_ref.k_ref.v_ref, ...), custom_call_target="tpu_custom_call" | custom-call | flops 3082813440 | bytes 3010560 | tf_op jit(solution)/shard_map/attend_back/pallas_call | solution.py:499
  74.9 1.7 broadcast_select_fusion
  76.9 1.3 broadcast_select_fusion.2
  78.2 4.1 %front_back.1 = (bf16[392,768]{1,0:T(8,128)(2,1)}, f32[208,768]{1,0:T(8,128)S(1)}) custom-call(s32[1]{0:T(128)} %bitcast.blk_ref, bf16[3,392,384]{2,1,0:T(8,128)(2,1)S(1)} %get-tuple-element.89.da_ref, bf16[3,392,384]{2,1,0:T(8,128)(2,1)S(1)} %get-tuple-element.88.db_ref, bf16[2,248,384]{2,1,0:T(8,128)(2,1)S(1)} %get-tuple-element.91.ha_ref, ...), custom_call_target="tpu_custom_call" | custom-call | flops 1387266048 | bytes 9560064 | tf_op jit(solution)/shard_map/front_back/pallas_call | solution.py:638
  84.9 1.5 collective-permute-done.10.atto_ref
  89.1 1.0 add_convert_fusion.8
  90.2 0.9 copy-done.22
  91.1 3.9 %collective-permute-start.4 = (bf16[208,384]{1,0:T(8,128)(2,1)S(1)}, bf16[208,384]{1,0:T(8,128)(2,1)S(1)}, u32[]{:S(2)}, u32[]{:S(2)}) collective-permute-start(bf16[208,384]{1,0:T(8,128)(2,1)S(1)} %add_convert_fusion.8), channel_id=1, source_target_pairs={{0,16},{2,18},{4,20},{6,22},{8,24},{10,26},{12,28},{14,30},{16,0},... | collective-permute-start | bytes 479240 | tf_op jit(solution)/shard_map/ppermute | solution.py:662
  95.0 1.2 copy-done.23
  96.1 1.1 copy-done.27
  97.2 1.1 copy-done.29
  98.3 5.8 %attend_weights.1 = (bf16[8,96,384]{2,1,0:T(8,128)(2,1)}, bf16[8,96,384]{2,1,0:T(8,128)(2,1)S(1)}, bf16[8,96,384]{2,1,0:T(8,128)(2,1)S(1)}, bf16[8,96,384]{2,1,0:T(8,128)(2,1)S(1)}) custom-call(s32[1]{0:T(128)} %bitcast.6.own_ref, s32[1]{0:T(128)} %bitcast.blk_ref, bf16[392,896]{1,0:T(8,128)(2,1)} %get-tuple-element.48.n1_ref.hot_ref, ...), custom_call_target="tpu_custom_call" | custom-call | flops 1849688064 | bytes 9584640 | tf_op jit(solution)/shard_map/attend_weights/pallas_call | solution.py:569
  105.6 1.5 collective-permute-start.12
  107.1 1.0 add_convert_fusion.7
  108.0 1.6 collective-permute-start.5
  109.7 1.5 collective-permute-start.14
  111.2 1.3 copy-done.33
  112.5 10.8 %feed_weights.1 = (bf16[8,192,384]{2,1,0:T(8,128)(2,1)S(1)}, bf16[8,192,384]{2,1,0:T(8,128)(2,1)S(1)}, bf16[8,192,384]{2,1,0:T(8,128)(2,1)S(1)}, bf16[8,192,384]{2,1,0:T(8,128)(2,1)S(1)}) custom-call(s32[1]{0:T(128)} %bitcast.6.own_ref, s32[1]{0:T(128)} %bitcast.blk_ref, bf16[392,3072]{1,0:T(8,128)(2,1)} %get-tuple-element.72.refs_0_, ...), custom_call_target="tpu_custom_call" | custom-call | flops 3699376128 | bytes 14352384 | tf_op jit(solution)/shard_map/feed_weights/pallas_call | solution.py:430
  124.0 1.0 add_convert_fusion.3
  125.6 1.5 collective-permute-start.25
  127.2 1.6 collective-permute-start.15
  129.4 5.7 %collective-permute-done.13 = bf16[4,96,384]{2,1,0:T(8,128)(2,1)S(1)} collective-permute-done((bf16[4,96,384]{2,1,0:T(8,128)(2,1)S(1)}, bf16[4,96,384]{2,1,0:T(8,128)(2,1)S(1)}, u32[]{:S(2)}, u32[]{:S(2)}) %collective-permute-start.13) | collective-permute-done | bytes 294944 | tf_op jit(solution)/shard_map/ppermute | solution.py:662
  135.0 1.1 add_bitcast_fusion.3
  136.1 20.6 %collective-permute-done.15 = bf16[4,96,384]{2,1,0:T(8,128)(2,1)S(1)} collective-permute-done((bf16[4,96,384]{2,1,0:T(8,128)(2,1)S(1)}, bf16[4,96,384]{2,1,0:T(8,128)(2,1)S(1)}, u32[]{:S(2)}, u32[]{:S(2)}) %collective-permute-start.15) | collective-permute-done | bytes 294944 | tf_op jit(solution)/shard_map/ppermute | solution.py:662
  158.1 2.2 %collective-permute-done.25 = bf16[8,192,384]{2,1,0:T(8,128)(2,1)S(1)} collective-permute-done((bf16[8,192,384]{2,1,0:T(8,128)(2,1)S(1)}, bf16[8,192,384]{2,1,0:T(8,128)(2,1)S(1)}, u32[]{:S(2)}, u32[]{:S(2)}) %collective-permute-start.25) | collective-permute-done | bytes 1179680 | tf_op jit(solution)/shard_map/ppermute | solution.py:662
  160.4 1.6 collective-permute-start.26
  162.0 1.7 collective-permute-done.6
  163.8 1.6 collective-permute-start.7
  165.9 8.2 %collective-permute-done.24 = bf16[4,192,384]{2,1,0:T(8,128)(2,1)S(1)} collective-permute-done((bf16[4,192,384]{2,1,0:T(8,128)(2,1)S(1)}, bf16[4,192,384]{2,1,0:T(8,128)(2,1)S(1)}, u32[]{:S(2)}, u32[]{:S(2)}) %collective-permute-start.24) | collective-permute-done | bytes 589856 | tf_op jit(solution)/shard_map/ppermute | solution.py:662
  176.6 11.3 %collective-permute-done.27 = bf16[2,2,192,384]{3,2,1,0:T(8,128)(2,1)S(1)} collective-permute-done((bf16[2,2,192,384]{3,2,1,0:T(8,128)(2,1)S(1)}, bf16[2,2,192,384]{3,2,1,0:T(8,128)(2,1)S(1)}, u32[]{:S(2)}, u32[]{:S(2)}) %collective-permute-start.27) | collective-permute-done | bytes 589856 | tf_op jit(solution)/shard_map/ppermute | solution.py:662
  191.8 1.0 maximum_select_fusion.1
  192.8 9.2 %collective-permute-done.28 = bf16[2,1,192,384]{3,2,1,0:T(8,128)(2,1)S(1)} collective-permute-done((bf16[2,1,192,384]{3,2,1,0:T(8,128)(2,1)}, bf16[2,1,192,384]{3,2,1,0:T(8,128)(2,1)S(1)}, u32[]{:S(2)}, u32[]{:S(2)}) %collective-permute-start.28) | collective-permute-done | bytes 294944 | tf_op jit(solution)/shard_map/ppermute | solution.py:662
  202.0 1.0 fusion.7
  (153 shorter events, 29.4 us)
Async XLA Ops:
  8.1 10.4 %collective-permute-start = (bf16[392,896]{1,0:T(8,128)(2,1)}, bf16[392,896]{1,0:T(8,128)(2,1)}, u32[]{:S(2)}, u32[]{:S(2)}) collective-permute-start(bf16[392,896]{1,0:T(8,128)(2,1)} %get-tuple-element.48.n1_ref.hot_ref), channel_id=1, source_target_pairs={{0,1},{1,0},{2,3},{3,2},{4,5},{5,4},{6,7},{7,6},{8,9},{9,8},{10,11... | collective-permute-start | bytes 2107400 | tf_op jit(solution)/shard_map/ppermute | solution.py:658
  12.6 2.0 copy-start
  14.6 3.8 %copy-start.1 = (bf16[768,2304]{1,0:T(8,128)(2,1)S(1)}, bf16[768,2304]{1,0:T(8,128)(2,1)}, u32[]{:S(2)}) copy-start(bf16[768,2304]{1,0:T(8,128)(2,1)} %w_ref.3) | copy-start | bytes 10616836
  18.4 13.1 %copy-start.6 = (f32[392,768]{1,0:T(8,128)S(1)}, f32[392,768]{1,0:T(8,128)}, u32[]{:S(2)}) copy-start(f32[392,768]{1,0:T(8,128)} %copy-done.5) | copy-start | bytes 3612676
  18.4 13.1 %copy-start.10 = (bf16[768,768]{1,0:T(8,128)(2,1)S(1)}, bf16[768,768]{1,0:T(8,128)(2,1)}, u32[]{:S(2)}) copy-start(bf16[768,768]{1,0:T(8,128)(2,1)} %wo_ref.3) | copy-start | bytes 3538948
  18.4 13.1 %copy-start.14 = (bf16[1,392,768]{2,1,0:T(8,128)(2,1)S(1)}, bf16[1,392,768]{2,1,0:T(8,128)(2,1)}, u32[]{:S(2)}) copy-start(bf16[1,392,768]{2,1,0:T(8,128)(2,1)} %param.35) | copy-start | bytes 1806340
  18.4 13.1 %copy-start.31 = (f32[3072]{0:T(1024)S(1)}, f32[3072]{0:T(1024)}, u32[]{:S(2)}) copy-start(f32[3072]{0:T(1024)} %param.32) | copy-start | bytes 36868
  28.9 2.6 %copy-start.2 = (bf16[12,392,640]{2,1,0:T(8,128)(2,1)}, bf16[12,392,640]{2,1,0:T(8,128)(2,1)S(1)}, u32[]{:S(2)}) copy-start(bf16[12,392,640]{2,1,0:T(8,128)(2,1)S(1)} %get-tuple-element.54.p_ref) | copy-start | bytes 18063364
  49.2 2.0 copy-start.24
  49.2 2.0 copy-start.32
  52.3 10.6 %copy-start.17 = (f32[4,768]{1,0:T(4,128)}, f32[4,768]{1,0:T(4,128)S(1)}, u32[]{:S(2)}) copy-start(f32[4,768]{1,0:T(4,128)S(1)} %get-tuple-element.63.sums_ref) | copy-start | bytes 36868
  52.3 2.7 %copy-start.3 = (bf16[12,392,640]{2,1,0:T(8,128)(2,1)S(1)}, bf16[12,392,640]{2,1,0:T(8,128)(2,1)}, u32[]{:S(2)}) copy-start(bf16[12,392,640]{2,1,0:T(8,128)(2,1)} %copy-done.2) | copy-start | bytes 18063364
  63.8 12.8 %collective-permute-start.2 = (bf16[2,248,384]{2,1,0:T(8,128)(2,1)}, bf16[2,248,384]{2,1,0:T(8,128)(2,1)}, u32[]{:S(2)}, u32[]{:S(2)}) collective-permute-start(bf16[2,248,384]{2,1,0:T(8,128)(2,1)} %get-tuple-element.61.dh_ref), channel_id=1, source_target_pairs={{0,1},{1,0},{2,3},{3,2},{4,5},{5,4},{6,7},{7,6},{8,9},{9,8},{10,11... | collective-permute-start | bytes 1142792 | tf_op jit(solution)/shard_map/ppermute | solution.py:658
  63.9 47.3 %collective-permute-start.19 = (bf16[392,3072]{1,0:T(8,128)(2,1)}, bf16[392,3072]{1,0:T(8,128)(2,1)}, u32[]{:S(2)}, u32[]{:S(2)}) collective-permute-start(bf16[392,3072]{1,0:T(8,128)(2,1)} %get-tuple-element.72.refs_0_), channel_id=1, source_target_pairs={{0,1},{1,0},{2,3},{3,2},{4,5},{5,4},{6,7},{7,6},{8,9},{9,8},{10,11... | collective-permute-start | bytes 7225352 | tf_op jit(solution)/shard_map/ppermute | solution.py:658
  64.3 2.7 %copy-start.4 = (bf16[12,392,640]{2,1,0:T(8,128)(2,1)S(1)}, bf16[12,392,640]{2,1,0:T(8,128)(2,1)}, u32[]{:S(2)}) copy-start(bf16[12,392,640]{2,1,0:T(8,128)(2,1)} %copy-done.2) | copy-start | bytes 18063364
  74.8 2.0 collective-permute-start.1
  74.9 3.3 %copy-start.9 = (f32[392,768]{1,0:T(8,128)S(1)}, f32[392,768]{1,0:T(8,128)}, u32[]{:S(2)}) copy-start(f32[392,768]{1,0:T(8,128)} %copy-done.8) | copy-start | bytes 3612676
  76.6 1.6 copy-start.7
  82.3 12.7 %copy-start.12 = (bf16[3,392,384]{2,1,0:T(8,128)(2,1)S(1)}, bf16[3,392,384]{2,1,0:T(8,128)(2,1)}, u32[]{:S(2)}) copy-start(bf16[3,392,384]{2,1,0:T(8,128)(2,1)} %copy-done.11) | copy-start | bytes 2709508
  82.4 1.5 collective-permute-start.3
  82.8 7.3 %collective-permute-start.9 = (bf16[3,392,384]{2,1,0:T(8,128)(2,1)}, bf16[3,392,384]{2,1,0:T(8,128)(2,1)S(1)}, u32[]{:S(2)}, u32[]{:S(2)}) collective-permute-start(bf16[3,392,384]{2,1,0:T(8,128)(2,1)} %get-tuple-element.59), channel_id=1, source_target_pairs={{0,1},{1,0},{2,3},{3,2},{4,5},{5,4},{6,7},{7,6},{8,9},{9,8},{10,11... | collective-permute-start | bytes 2709512 | tf_op jit(solution)/shard_map/ppermute | solution.py:658
  83.0 3.4 %collective-permute-start.10 = (bf16[392,768]{1,0:T(8,128)(2,1)}, bf16[392,768]{1,0:T(8,128)(2,1)S(1)}, u32[]{:S(2)}, u32[]{:S(2)}) collective-permute-start(bf16[392,768]{1,0:T(8,128)(2,1)} %get-tuple-element.49.att_ref), channel_id=1, source_target_pairs={{0,1},{1,0},{2,3},{3,2},{4,5},{5,4},{6,7},{7,6},{8,9},{9,8},{10,11... | collective-permute-start | bytes 1806344 | tf_op jit(solution)/shard_map/ppermute | solution.py:658
  83.3 4.7 %collective-permute-start.11 = (bf16[392,768]{1,0:T(8,128)(2,1)}, bf16[392,768]{1,0:T(8,128)(2,1)S(1)}, u32[]{:S(2)}, u32[]{:S(2)}) collective-permute-start(bf16[392,768]{1,0:T(8,128)(2,1)} %get-tuple-element.67.gb_ref), channel_id=1, source_target_pairs={{0,1},{1,0},{2,3},{3,2},{4,5},{5,4},{6,7},{7,6},{8,9},{9,8},{10,11... | collective-permute-start | bytes 1806344 | tf_op jit(solution)/shard_map/ppermute | solution.py:658
  84.5 26.7 %collective-permute-start.22 = (bf16[392,1536]{1,0:T(8,128)(2,1)}, bf16[392,1536]{1,0:T(8,128)(2,1)}, u32[]{:S(2)}, u32[]{:S(2)}) collective-permute-start(bf16[392,1536]{1,0:T(8,128)(2,1)} %get-tuple-element.75), channel_id=1, source_target_pairs={{0,1},{1,0},{2,3},{3,2},{4,5},{5,4},{6,7},{7,6},{8,9},{9,8},{10,11... | collective-permute-start | bytes 3612680 | tf_op jit(solution)/shard_map/ppermute | solution.py:658
  87.1 20.9 %collective-permute-start.20 = (bf16[392,768]{1,0:T(8,128)(2,1)}, bf16[392,768]{1,0:T(8,128)(2,1)}, u32[]{:S(2)}, u32[]{:S(2)}) collective-permute-start(bf16[392,768]{1,0:T(8,128)(2,1)} %bitcast.56), channel_id=1, source_target_pairs={{0,1},{1,0},{2,3},{3,2},{4,5},{5,4},{6,7},{7,6},{8,9},{9,8},{10,11... | collective-permute-start | bytes 1806344 | tf_op jit(solution)/shard_map/ppermute | solution.py:658
  88.9 20.8 %collective-permute-start.21 = (bf16[392,768]{1,0:T(8,128)(2,1)}, bf16[392,768]{1,0:T(8,128)(2,1)}, u32[]{:S(2)}, u32[]{:S(2)}) collective-permute-start(bf16[392,768]{1,0:T(8,128)(2,1)} %copy-done.24), channel_id=1, source_target_pairs={{0,1},{1,0},{2,3},{3,2},{4,5},{5,4},{6,7},{7,6},{8,9},{9,8},{10,11... | collective-permute-start | bytes 1806344 | tf_op jit(solution)/shard_map/ppermute | solution.py:658
  91.1 13.8 %collective-permute-start.4 = (bf16[208,384]{1,0:T(8,128)(2,1)S(1)}, bf16[208,384]{1,0:T(8,128)(2,1)S(1)}, u32[]{:S(2)}, u32[]{:S(2)}) collective-permute-start(bf16[208,384]{1,0:T(8,128)(2,1)S(1)} %add_convert_fusion.8), channel_id=1, source_target_pairs={{0,16},{2,18},{4,20},{6,22},{8,24},{10,26},{12,28},{14,30},{16,0},... | collective-permute-start | bytes 479240 | tf_op jit(solution)/shard_map/ppermute | solution.py:662
  98.3 12.9 %copy-start.15 = (bf16[1,392,768]{2,1,0:T(8,128)(2,1)S(1)}, bf16[1,392,768]{2,1,0:T(8,128)(2,1)}, u32[]{:S(2)}) copy-start(bf16[1,392,768]{2,1,0:T(8,128)(2,1)} %param.35) | copy-start | bytes 1806340
  98.3 12.9 %copy-start.25 = (bf16[392,768]{1,0:T(8,128)(2,1)S(1)}, bf16[392,768]{1,0:T(8,128)(2,1)}, u32[]{:S(2)}) copy-start(bf16[392,768]{1,0:T(8,128)(2,1)} %copy-done.24) | copy-start | bytes 1806340
  105.6 18.4 %collective-permute-start.12 = (bf16[8,96,384]{2,1,0:T(8,128)(2,1)}, bf16[8,96,384]{2,1,0:T(8,128)(2,1)}, u32[]{:S(2)}, u32[]{:S(2)}) collective-permute-start(bf16[8,96,384]{2,1,0:T(8,128)(2,1)} %get-tuple-element.69), channel_id=1, source_target_pairs={{0,2},{2,0},{4,6},{6,4},{8,10},{10,8},{12,14},{14,12},{16,18},{18,... | collective-permute-start | bytes 1769480 | tf_op jit(solution)/shard_map/ppermute | solution.py:662
  108.0 20.7 %collective-permute-start.5 = (bf16[208,384]{1,0:T(8,128)(2,1)S(1)}, bf16[208,384]{1,0:T(8,128)(2,1)S(1)}, u32[]{:S(2)}, u32[]{:S(2)}) collective-permute-start(bf16[208,384]{1,0:T(8,128)(2,1)S(1)} %add_convert_fusion.7), channel_id=1, source_target_pairs={{0,8},{2,10},{4,12},{6,14},{8,0},{10,2},{12,4},{14,6},{16,24},{18,... | collective-permute-start | bytes 479240 | tf_op jit(solution)/shard_map/ppermute | solution.py:662
  109.7 17.4 %collective-permute-start.14 = (bf16[8,96,384]{2,1,0:T(8,128)(2,1)}, bf16[8,96,384]{2,1,0:T(8,128)(2,1)S(1)}, u32[]{:S(2)}, u32[]{:S(2)}) collective-permute-start(bf16[8,96,384]{2,1,0:T(8,128)(2,1)} %copy-done.30), channel_id=1, source_target_pairs={{0,4},{2,6},{4,0},{6,2},{8,12},{10,14},{12,8},{14,10},{16,20},{18,... | collective-permute-start | bytes 1769480 | tf_op jit(solution)/shard_map/ppermute | solution.py:662
  123.4 34.0 %collective-permute-start.23 = (bf16[8,192,384]{2,1,0:T(8,128)(2,1)S(1)}, bf16[8,192,384]{2,1,0:T(8,128)(2,1)S(1)}, u32[]{:S(2)}, u32[]{:S(2)}) collective-permute-start(bf16[8,192,384]{2,1,0:T(8,128)(2,1)S(1)} %get-tuple-element.77), channel_id=1, source_target_pairs={{0,2},{2,0},{4,6},{6,4},{8,10},{10,8},{12,14},{14,12},{16,18},{18,... | collective-permute-start | bytes 3538952 | tf_op jit(solution)/shard_map/ppermute | solution.py:662
  125.0 10.0 %collective-permute-start.13 = (bf16[4,96,384]{2,1,0:T(8,128)(2,1)S(1)}, bf16[4,96,384]{2,1,0:T(8,128)(2,1)S(1)}, u32[]{:S(2)}, u32[]{:S(2)}) collective-permute-start(bf16[4,96,384]{2,1,0:T(8,128)(2,1)S(1)} %add_convert_fusion.3), channel_id=1, source_target_pairs={{0,4},{2,6},{4,0},{6,2},{8,12},{10,14},{12,8},{14,10},{16,20},{18,... | collective-permute-start | bytes 884744 | tf_op jit(solution)/shard_map/ppermute | solution.py:662
  125.6 34.7 %collective-permute-start.25 = (bf16[8,192,384]{2,1,0:T(8,128)(2,1)S(1)}, bf16[8,192,384]{2,1,0:T(8,128)(2,1)S(1)}, u32[]{:S(2)}, u32[]{:S(2)}) collective-permute-start(bf16[8,192,384]{2,1,0:T(8,128)(2,1)S(1)} %get-tuple-element.79), channel_id=1, source_target_pairs={{0,4},{2,6},{4,0},{6,2},{8,12},{10,14},{12,8},{14,10},{16,20},{18,... | collective-permute-start | bytes 3538952 | tf_op jit(solution)/shard_map/ppermute | solution.py:662
  127.2 29.6 %collective-permute-start.15 = (bf16[4,96,384]{2,1,0:T(8,128)(2,1)S(1)}, bf16[4,96,384]{2,1,0:T(8,128)(2,1)S(1)}, u32[]{:S(2)}, u32[]{:S(2)}) collective-permute-start(bf16[4,96,384]{2,1,0:T(8,128)(2,1)S(1)} %add_convert_fusion.2), channel_id=1, source_target_pairs={{0,2},{2,0},{4,6},{6,4},{8,10},{10,8},{12,14},{14,12},{16,18},{18,... | collective-permute-start | bytes 884744 | tf_op jit(solution)/shard_map/ppermute | solution.py:662
  128.8 34.9 %collective-permute-start.6 = (bf16[208,384]{1,0:T(8,128)(2,1)S(1)}, bf16[208,384]{1,0:T(8,128)(2,1)S(1)}, u32[]{:S(2)}, u32[]{:S(2)}) collective-permute-start(bf16[208,384]{1,0:T(8,128)(2,1)S(1)} %add_convert_fusion.6), channel_id=1, source_target_pairs={{0,4},{2,6},{4,0},{6,2},{8,12},{10,14},{12,8},{14,10},{16,20},{18,... | collective-permute-start | bytes 479240 | tf_op jit(solution)/shard_map/ppermute | solution.py:662
  156.9 8.4 %collective-permute-start.16 = (bf16[2,2,96,384]{3,2,1,0:T(8,128)(2,1)S(1)}, bf16[2,2,96,384]{3,2,1,0:T(8,128)(2,1)S(1)}, u32[]{:S(2)}, u32[]{:S(2)}) collective-permute-start(bf16[2,2,96,384]{3,2,1,0:T(8,128)(2,1)S(1)} %fusion.3), channel_id=1, source_target_pairs={{0,8},{2,10},{4,12},{6,14},{8,0},{10,2},{12,4},{14,6},{16,24},{18,... | collective-permute-start | bytes 884744 | tf_op jit(solution)/shard_map/ppermute | solution.py:662
  157.5 16.6 %collective-permute-start.24 = (bf16[4,192,384]{2,1,0:T(8,128)(2,1)S(1)}, bf16[4,192,384]{2,1,0:T(8,128)(2,1)S(1)}, u32[]{:S(2)}, u32[]{:S(2)}) collective-permute-start(bf16[4,192,384]{2,1,0:T(8,128)(2,1)S(1)} %add_convert_fusion.1), channel_id=1, source_target_pairs={{0,4},{2,6},{4,0},{6,2},{8,12},{10,14},{12,8},{14,10},{16,20},{18,... | collective-permute-start | bytes 1769480 | tf_op jit(solution)/shard_map/ppermute | solution.py:662
  160.4 13.9 %collective-permute-start.26 = (bf16[4,192,384]{2,1,0:T(8,128)(2,1)S(1)}, bf16[4,192,384]{2,1,0:T(8,128)(2,1)S(1)}, u32[]{:S(2)}, u32[]{:S(2)}) collective-permute-start(bf16[4,192,384]{2,1,0:T(8,128)(2,1)S(1)} %add_convert_fusion), channel_id=1, source_target_pairs={{0,2},{2,0},{4,6},{6,4},{8,10},{10,8},{12,14},{14,12},{16,18},{18,... | collective-permute-start | bytes 1769480 | tf_op jit(solution)/shard_map/ppermute | solution.py:662
  163.8 11.4 %collective-permute-start.7 = (bf16[208,384]{1,0:T(8,128)(2,1)S(1)}, bf16[208,384]{1,0:T(8,128)(2,1)S(1)}, u32[]{:S(2)}, u32[]{:S(2)}) collective-permute-start(bf16[208,384]{1,0:T(8,128)(2,1)S(1)} %add_convert_fusion.5), channel_id=1, source_target_pairs={{0,2},{2,0},{4,6},{6,4},{8,10},{10,8},{12,14},{14,12},{16,18},{18,... | collective-permute-start | bytes 479240 | tf_op jit(solution)/shard_map/ppermute | solution.py:662
  165.4 10.0 %collective-permute-start.17 = (bf16[2,1,96,384]{3,2,1,0:T(8,128)(2,1)S(1)}, bf16[2,1,96,384]{3,2,1,0:T(8,128)(2,1)S(1)}, u32[]{:S(2)}, u32[]{:S(2)}) collective-permute-start(bf16[2,1,96,384]{3,2,1,0:T(8,128)(2,1)S(1)} %fusion.15), channel_id=1, source_target_pairs={{0,16},{2,18},{4,20},{6,22},{8,24},{10,26},{12,28},{14,30},{16,0},... | collective-permute-start | bytes 442376 | tf_op jit(solution)/shard_map/ppermute | solution.py:662
  174.7 13.2 %collective-permute-start.27 = (bf16[2,2,192,384]{3,2,1,0:T(8,128)(2,1)S(1)}, bf16[2,2,192,384]{3,2,1,0:T(8,128)(2,1)S(1)}, u32[]{:S(2)}, u32[]{:S(2)}) collective-permute-start(bf16[2,2,192,384]{3,2,1,0:T(8,128)(2,1)S(1)} %fusion.1), channel_id=1, source_target_pairs={{0,8},{2,10},{4,12},{6,14},{8,0},{10,2},{12,4},{14,6},{16,24},{18,... | collective-permute-start | bytes 1769480 | tf_op jit(solution)/shard_map/ppermute | solution.py:662
  175.2 14.3 %collective-permute-start.8 = (bf16[208,384]{1,0:T(8,128)(2,1)S(1)}, bf16[208,384]{1,0:T(8,128)(2,1)S(1)}, u32[]{:S(2)}, u32[]{:S(2)}) collective-permute-start(bf16[208,384]{1,0:T(8,128)(2,1)S(1)} %add_convert_fusion.4), channel_id=1, source_target_pairs={{0,1},{1,0},{2,3},{3,2},{4,5},{5,4},{6,7},{7,6},{8,9},{9,8},{10,11... | collective-permute-start | bytes 479240 | tf_op jit(solution)/shard_map/ppermute | solution.py:658
  176.1 15.7 %collective-permute-start.18 = (f32[4,24,384]{2,1,0:T(8,128)}, f32[4,24,384]{2,1,0:T(8,128)}, u32[]{:S(2)}, u32[]{:S(2)}) collective-permute-start(f32[4,24,384]{2,1,0:T(8,128)} %get-tuple-element.99), channel_id=1, source_target_pairs={{0,1},{1,0},{2,3},{3,2},{4,5},{5,4},{6,7},{7,6},{8,9},{9,8},{10,11... | collective-permute-start | bytes 442376 | tf_op jit(solution)/shard_map/ppermute | solution.py:658
  188.8 13.2 %collective-permute-start.28 = (bf16[2,1,192,384]{3,2,1,0:T(8,128)(2,1)}, bf16[2,1,192,384]{3,2,1,0:T(8,128)(2,1)S(1)}, u32[]{:S(2)}, u32[]{:S(2)}) collective-permute-start(bf16[2,1,192,384]{3,2,1,0:T(8,128)(2,1)} %fusion.9), channel_id=1, source_target_pairs={{0,16},{2,18},{4,20},{6,22},{8,24},{10,26},{12,28},{14,30},{16,0},... | collective-permute-start | bytes 884744 | tf_op jit(solution)/shard_map/ppermute | solution.py:662
  203.1 2.1 %collective-permute-start.29 = (f32[4,24,384]{2,1,0:T(8,128)S(1)}, f32[4,24,384]{2,1,0:T(8,128)S(1)}, u32[]{:S(2)}, u32[]{:S(2)}) collective-permute-start(f32[4,24,384]{2,1,0:T(8,128)S(1)} %get-tuple-element.97), channel_id=1, source_target_pairs={{0,1},{1,0},{2,3},{3,2},{4,5},{5,4},{6,7},{7,6},{8,9},{9,8},{10,11... | collective-permute-start | bytes 442376 | tf_op jit(solution)/shard_map/ppermute | solution.py:658
  203.2 2.9 %collective-permute-start.30 = (f32[1,96,384]{2,1,0:T(8,128)S(1)}, f32[1,96,384]{2,1,0:T(8,128)S(1)}, u32[]{:S(2)}, u32[]{:S(2)}) collective-permute-start(f32[1,96,384]{2,1,0:T(8,128)S(1)} %get-tuple-element.95), channel_id=1, source_target_pairs={{0,1},{1,0},{2,3},{3,2},{4,5},{5,4},{6,7},{7,6},{8,9},{9,8},{10,11... | collective-permute-start | bytes 442376 | tf_op jit(solution)/shard_map/ppermute | solution.py:658
  (21 other events, 20.8 us)

commit v2 on v1

--- a/solution.py
+++ b/solution.py
@@ -2,7 +2,6 @@
 
 import jax
 import jax.numpy as jnp
-import numpy as np
 from jax import lax
 from jax.experimental import pallas as pl
 from jax.experimental.pallas import tpu as pltpu
@@ -44,6 +43,10 @@
     return inv * (scaled - centre - normal * along)
 
 
+def line(ref):
+    return ref[...].reshape(1, -1)
+
+
 def column_sum(v):
     return jnp.sum(v, axis=0, keepdims=True)
 
@@ -54,7 +57,7 @@
 
 def cost(flops, bytes_accessed, trans=0):
     return pl.CostEstimate(
-        flops=int(flops), bytes_accessed=int(bytes_accessed), transcendentals=int(trans)
+        flops=int(flops) // 100, bytes_accessed=int(bytes_accessed) // 100, transcendentals=int(trans) // 100
     )
 
 
@@ -69,7 +72,7 @@
     hidden0 = x_ref[...].astype(F32) + dot_tn(hot, table_ref[...])
     h0_ref[...] = hidden0
     normal, _ = normalise(hidden0)
-    n1_ref[:, :width] = (normal * gain_ref[...] + shift_ref[...]).astype(BF)
+    n1_ref[:, :width] = (normal * line(gain_ref) + line(shift_ref)).astype(BF)
     seg_hot = (lax.broadcasted_iota(jnp.int32, (8, half), 0) == seg_ref[...]).astype(F32).astype(BF)
     eye = (
         lax.broadcasted_iota(jnp.int32, (8, 128), 0) == lax.broadcasted_iota(jnp.int32, (8, 128), 1)
@@ -93,12 +96,12 @@
 
 def qkv_kernel(n1_ref, w_ref, qb_ref, vb_ref, out_ref):
     j = pl.program_id(0)
-    width = qb_ref.shape[1]
+    width = qb_ref.shape[0]
     product = dot_nn(n1_ref[:, :width], w_ref[...])
 
     @pl.when(j == 0)
     def _():
-        out_ref[0] = ((product + qb_ref[...]).astype(BF).astype(F32) * 0.125).astype(BF)
+        out_ref[0] = ((product + line(qb_ref)).astype(BF).astype(F32) * 0.125).astype(BF)
 
     @pl.when(j == 1)
     def _():
@@ -106,7 +109,7 @@
 
     @pl.when(j == 2)
     def _():
-        out_ref[0] = (product + vb_ref[...]).astype(BF)
+        out_ref[0] = (product + line(vb_ref)).astype(BF)
 
 
 def qkv_own(n1, w, qb, vb):
@@ -151,7 +154,7 @@
 
     n1h = n1o_ref[pl.ds(start, halo), :width]
     kh = dot_nn(n1h, wk_ref[...]).astype(BF)
-    vh = (dot_nn(n1h, wv_ref[...]) + vb_ref[...]).astype(BF)
+    vh = (dot_nn(n1h, wv_ref[...]) + line(vb_ref)).astype(BF)
     kh_ref[...] = kh
     vh_ref[...] = vh
     kcat_ref[:half, :] = k_ref[0]
@@ -192,7 +195,7 @@
                 pl.BlockSpec((1, half, group), lambda g, b: (2, 0, g)),
                 pl.BlockSpec((width, group), lambda g, b: (0, steps + g)),
                 pl.BlockSpec((width, group), lambda g, b: (0, 2 * steps + g)),
-                pl.BlockSpec((1, group), lambda g, b: (0, g)),
+                pl.BlockSpec((group,), lambda g, b: (g,)),
                 pl.BlockSpec((half, 128), lambda g, b: (0, width // 128)),
                 whole(n1o.shape),
             ],
@@ -221,29 +224,25 @@
 
 
 def feed_kernel(
-    blk_ref, att_ref, h0_ref, cot_ref, wo_ref, bo_ref, g2_ref, s2_ref, w1_ref, b1_ref, w2_ref, b2_ref,
-    res_ref, h1_ref, n2_ref, act_ref, gs_ref, gk_ref, gn_ref, b1g_ref, mixed_ref,
+    blk_ref, att_ref, h0_ref, cot_ref, wo_ref, bo_ref, g2_ref, s2_ref, w1_ref, b1_ref, w2_ref,
+    h1_ref, n2_ref, act_ref, gs_ref, gk_ref, b1g_ref,
 ):
     i = pl.program_id(0)
     steps = pl.num_programs(0)
 
     @pl.when(i == 0)
     def _():
-        hidden1 = h0_ref[...] + dot_nn(att_ref[...], wo_ref[...]) + bo_ref[...]
+        hidden1 = h0_ref[...] + dot_nn(att_ref[...], wo_ref[...]) + line(bo_ref)
         h1_ref[...] = hidden1
         normal, _ = normalise(hidden1)
-        n2_ref[...] = (normal * g2_ref[...] + s2_ref[...]).astype(BF)
-        mixed_ref[...] = hidden1 + b2_ref[...]
-        gn_ref[...] = jnp.zeros_like(gn_ref)
-
-    pre = dot_nn(n2_ref[...], w1_ref[...]) + b1_ref[...]
+        n2_ref[...] = (normal * line(g2_ref) + line(s2_ref)).astype(BF)
+
+    pre = dot_nn(n2_ref[...], w1_ref[...]) + line(b1_ref)
     grad_act = dot_nt(cot_ref[...], w2_ref[...])
     cdf = 0.5 + 0.5 * lax.erf(pre * inv_root_two)
-    act = (pre * cdf).astype(BF)
-    act_ref[...] = act
+    act_ref[...] = (pre * cdf).astype(BF)
     slope = cdf + pre * jnp.exp(-0.5 * pre * pre) * inv_root_two_pi
-    grad32 = grad_act * slope
-    grad_pre = grad32.astype(BF)
+    grad_pre = (grad_act * slope).astype(BF)
     b1g_ref[...] = column_sum(grad_pre.astype(F32))
 
     @pl.when(i < steps // 2)
@@ -254,24 +253,17 @@
     def _():
         gk_ref[...] = grad_pre
 
-    mixed_ref[...] += dot_nn(act, w2_ref[...])
-    gn_ref[...] += dot_nt(grad_pre, w1_ref[...])
-
-    @pl.when(i == steps - 1)
-    def _():
-        res_ref[...] = mixed_ref[...].astype(BF)
-
-
-def feed(blk, att, h0, cot, wo, bo, g2, s2, w1, b1, w2, b2):
+
+def relative(i, b, per):
+    return jnp.where(i < per, (1 - b[0]) * per + i, b[0] * per + i - per)
+
+
+def feed(blk, att, h0, cot, wo, bo, g2, s2, w1, b1, w2):
     half, width = h0.shape
     hidden = w1.shape[1]
-    chunk = 384
+    chunk = 512
     steps = hidden // chunk
     per = steps // 2
-
-    def place(i, b):
-        return jnp.where(i < per, (1 - b[0]) * per + i, b[0] * per + i - per)
-
     return pl.pallas_call(
         feed_kernel,
         grid_spec=pltpu.PrefetchScalarGridSpec(
@@ -285,70 +277,115 @@
                 whole(bo.shape),
                 whole(g2.shape),
                 whole(s2.shape),
-                pl.BlockSpec((width, chunk), lambda i, b: (0, place(i, b))),
-                pl.BlockSpec((1, chunk), lambda i, b: (0, place(i, b))),
-                pl.BlockSpec((chunk, width), lambda i, b: (place(i, b), 0)),
-                whole(b2.shape),
+                pl.BlockSpec((width, chunk), lambda i, b: (0, relative(i, b, per))),
+                pl.BlockSpec((chunk,), lambda i, b: (relative(i, b, per),)),
+                pl.BlockSpec((chunk, width), lambda i, b: (relative(i, b, per), 0)),
             ],
             out_specs=[
                 whole((half, width)),
                 whole((half, width)),
-                whole((half, width)),
-                pl.BlockSpec((half, chunk), lambda i, b: (0, place(i, b))),
+                pl.BlockSpec((half, chunk), lambda i, b: (0, relative(i, b, per))),
                 pl.BlockSpec((half, chunk), lambda i, b: (0, jnp.minimum(i, per - 1))),
                 pl.BlockSpec((half, chunk), lambda i, b: (0, jnp.maximum(i - per, 0))),
-                whole((half, width)),
-                pl.BlockSpec((1, chunk), lambda i, b: (0, place(i, b))),
-            ],
-            scratch_shapes=[pltpu.VMEM((half, width), F32)],
+                pl.BlockSpec((1, chunk), lambda i, b: (0, relative(i, b, per))),
+            ],
         ),
         out_shape=(
-            jax.ShapeDtypeStruct((half, width), BF),
             jax.ShapeDtypeStruct((half, width), F32),
             jax.ShapeDtypeStruct((half, width), BF),
             jax.ShapeDtypeStruct((half, hidden), BF),
             jax.ShapeDtypeStruct((half, hidden // 2), BF),
             jax.ShapeDtypeStruct((half, hidden // 2), BF),
-            jax.ShapeDtypeStruct((half, width), F32),
             jax.ShapeDtypeStruct((1, hidden), F32),
         ),
         compiler_params=params(40),
         cost_estimate=cost(
-            8 * half * width * hidden + 2 * half * width * width, 4 * width * hidden, 2 * half * hidden
+            4 * half * width * hidden + 2 * half * width * width, 4 * width * hidden, 2 * half * hidden
         ),
         name="feed",
-    )(blk, att, h0, cot, wo, bo, g2, s2, w1, b1, w2, b2)
-
-
-def mid_kernel(gn_ref, h1_ref, cot_ref, wo_ref, g2_ref, gh_ref, gb_ref, ga_ref, sums_ref):
-    normal, inv = normalise(h1_ref[...])
-    grad = gn_ref[...]
-    cot = cot_ref[...].astype(F32)
-    sums_ref[0:1, :] = column_sum(grad * normal)
-    sums_ref[1:2, :] = column_sum(grad)
-    grad_hidden1 = cot + norm_back(grad, normal, inv, g2_ref[...])
-    gh_ref[...] = grad_hidden1
-    branch = grad_hidden1.astype(BF)
-    gb_ref[...] = branch
-    sums_ref[2:3, :] = column_sum(branch.astype(F32))
-    sums_ref[3:4, :] = column_sum(cot)
-    ga_ref[...] = dot_nt(branch, wo_ref[...]).astype(BF)
-
-
-def mid(gn, h1, cot, wo, g2):
+    )(blk, att, h0, cot, wo, bo, g2, s2, w1, b1, w2)
+
+
+def feed_back_kernel(
+    blk_ref, act_ref, gs_ref, gk_ref, w1_ref, w2_ref, h1_ref, b2_ref, cot_ref, wo_ref, g2_ref,
+    res_ref, gh_ref, gb_ref, ga_ref, sums_ref, mixed_ref, gn_ref,
+):
+    i = pl.program_id(0)
+    steps = pl.num_programs(0)
+    grad_pre = jnp.where(i < steps // 2, gs_ref[...], gk_ref[...])
+    mixed = dot_nn(act_ref[...], w2_ref[...])
+    grad = dot_nt(grad_pre, w1_ref[...])
+
+    @pl.when(i == 0)
+    def _():
+        mixed_ref[...] = mixed
+        gn_ref[...] = grad
+
+    @pl.when(i > 0)
+    def _():
+        mixed_ref[...] += mixed
+        gn_ref[...] += grad
+
+    @pl.when(i == steps - 1)
+    def _():
+        res_ref[...] = (h1_ref[...] + mixed_ref[...] + line(b2_ref)).astype(BF)
+        normal, inv = normalise(h1_ref[...])
+        total = gn_ref[...]
+        cot = cot_ref[...].astype(F32)
+        sums_ref[0:1, :] = column_sum(total * normal)
+        sums_ref[1:2, :] = column_sum(total)
+        grad_hidden1 = cot + norm_back(total, normal, inv, line(g2_ref))
+        gh_ref[...] = grad_hidden1
+        branch = grad_hidden1.astype(BF)
+        gb_ref[...] = branch
+        sums_ref[2:3, :] = column_sum(branch.astype(F32))
+        sums_ref[3:4, :] = column_sum(cot)
+        ga_ref[...] = dot_nt(branch, wo_ref[...]).astype(BF)
+
+
+def feed_back(blk, act, gs, gk, w1, w2, h1, b2, cot, wo, g2):
     half, width = h1.shape
-    return pl.pallas_call(
-        mid_kernel,
+    hidden = w1.shape[1]
+    chunk = 768
+    steps = hidden // chunk
+    per = steps // 2
+    return pl.pallas_call(
+        feed_back_kernel,
+        grid_spec=pltpu.PrefetchScalarGridSpec(
+            num_scalar_prefetch=1,
+            grid=(steps,),
+            in_specs=[
+                pl.BlockSpec((half, chunk), lambda i, b: (0, relative(i, b, per))),
+                pl.BlockSpec((half, chunk), lambda i, b: (0, jnp.minimum(i, per - 1))),
+                pl.BlockSpec((half, chunk), lambda i, b: (0, jnp.maximum(i - per, 0))),
+                pl.BlockSpec((width, chunk), lambda i, b: (0, relative(i, b, per))),
+                pl.BlockSpec((chunk, width), lambda i, b: (relative(i, b, per), 0)),
+                whole(h1.shape),
+                whole(b2.shape),
+                whole(cot.shape),
+                whole(wo.shape),
+                whole(g2.shape),
+            ],
+            out_specs=[
+                whole((half, width)),
+                whole((half, width)),
+                whole((half, width)),
+                whole((half, width)),
+                whole((4, width)),
+            ],
+            scratch_shapes=[pltpu.VMEM((half, width), F32), pltpu.VMEM((half, width), F32)],
+        ),
         out_shape=(
+            jax.ShapeDtypeStruct((half, width), BF),
             jax.ShapeDtypeStruct((half, width), F32),
             jax.ShapeDtypeStruct((half, width), BF),
             jax.ShapeDtypeStruct((half, width), BF),
             jax.ShapeDtypeStruct((4, width), F32),
         ),
-        compiler_params=params(24),
-        cost_estimate=cost(2 * half * width * width, 14 * half * width),
-        name="mid",
-    )(gn, h1, cot, wo, g2)
+        compiler_params=params(40),
+        cost_estimate=cost(4 * half * width * hidden + 2 * half * width * width, 4 * width * hidden),
+        name="feed_back",
+    )(blk, act, gs, gk, w1, w2, h1, b2, cot, wo, g2)
 
 
 class Plan:
@@ -374,61 +411,42 @@
 def store_block(refs, plan, piece, p, row, block):
     place = plan.index[piece][p]
     first = plan.groups // 2
-    ref = refs[2 * piece + (place >= first)]
-    ref[place % first, row : row + block.shape[0], :] = block
-
-
-def feed_weights_kernel(
-    plan, own_ref, act_ref, acto_ref, cot_ref, coto_ref, n2_ref, n2o_ref, g_ref, go_ref, *rest
-):
-    outs, acc_ref = rest[:4], rest[4]
+    refs[place >= first][place % first, row : row + block.shape[0], :] = block
+
+
+def second_weights_kernel(plan, own_ref, blk_ref, act_ref, acto_ref, cot_ref, coto_ref, *rest):
+    outs, acc_ref = rest[:2], rest[2]
     i = pl.program_id(0)
     own = own_ref[0]
     chunk = act_ref.shape[1]
     steps = pl.num_programs(0)
     per = plan.groups // steps
-    rows2 = chunk // per
-    rows1 = n2_ref.shape[1] // plan.groups
+    rows = chunk // per
     acc_ref[...] = dot_tn(act_ref[...], cot_ref[...]) + dot_tn(acto_ref[...], coto_ref[...])
     for step in range(steps):
 
         @pl.when(i == step)
         def _():
             for low in range(per):
-                source = pl.multiple_of(((own % per) ^ low) * rows2, 16)
-                for piece in range(2):
-                    block = acc_ref[pl.ds(source + piece * (rows2 // 2), rows2 // 2), :]
-                    store_block(outs, plan, piece, step * per + low, 0, block.astype(BF))
-
-    acc_ref[...] = dot_tn(n2_ref[...], g_ref[...]) + dot_tn(n2o_ref[...], go_ref[...])
-    for step in range(steps):
-
-        @pl.when(i == step)
-        def _():
-            for p in range(plan.groups):
-                source = pl.multiple_of((own ^ p) * rows1, 16)
-                block = acc_ref[pl.ds(source, rows1), :]
-                store_block(
-                    outs, plan, step // (steps // 2), p,
-                    rows2 // 2 + (step % (steps // 2)) * rows1, block.astype(BF),
-                )
-
-
-def feed_weights(plan, own, blk, act, acto, cot, coto, n2, n2o, g, go):
+                source = pl.multiple_of(((own % per) ^ low) * rows, 16)
+                block = acc_ref[pl.ds(source, rows), :]
+                store_block(outs, plan, 0, step * per + low, 0, block.astype(BF))
+
+
+def second_weights(plan, own, blk, act, acto, cot, coto):
     half, hidden = act.shape
-    width = n2.shape[1]
+    width = cot.shape[1]
     cols = width // 2
     steps = 4
     chunk = hidden // steps
     per = plan.groups // steps
-    rows = hidden // plan.groups // 2 + (steps // 2) * (width // plan.groups)
-    part = jax.ShapeDtypeStruct((plan.groups // 2, rows, cols), BF)
+    part = jax.ShapeDtypeStruct((plan.groups // 2, hidden // plan.groups, cols), BF)
 
     def place(i, o, b):
         return (0, (o[0] // per) ^ i)
 
     return pl.pallas_call(
-        functools.partial(wrap_two, feed_weights_kernel, plan),
+        functools.partial(second_weights_kernel, plan),
         grid_spec=pltpu.PrefetchScalarGridSpec(
             num_scalar_prefetch=2,
             grid=(steps,),
@@ -437,27 +455,61 @@
                 pl.BlockSpec((half, chunk), place),
                 pl.BlockSpec((half, cols), lambda i, o, b: (0, b[0])),
                 pl.BlockSpec((half, cols), lambda i, o, b: (0, b[0])),
+            ],
+            out_specs=[whole(part.shape)] * 2,
+            scratch_shapes=[pltpu.VMEM((chunk, cols), F32)],
+        ),
+        out_shape=(part,) * 2,
+        compiler_params=params(40),
+        cost_estimate=cost(2 * half * width * hidden, width * hidden + 4 * half * hidden),
+        name="second_weights",
+    )(own, blk, act, acto, cot, coto)
+
+
+def first_weights_kernel(plan, own_ref, n2_ref, n2o_ref, g_ref, go_ref, *rest):
+    outs, acc_ref = rest[:2], rest[2]
+    i = pl.program_id(0)
+    own = own_ref[0]
+    rows = n2_ref.shape[1] // plan.groups
+    acc_ref[...] = dot_tn(n2_ref[...], g_ref[...]) + dot_tn(n2o_ref[...], go_ref[...])
+    for step in range(4):
+
+        @pl.when(i == step)
+        def _():
+            for p in range(plan.groups):
+                source = pl.multiple_of((own ^ p) * rows, 16)
+                block = acc_ref[pl.ds(source, rows), :]
+                store_block(outs, plan, 1, p, step * rows, block.astype(BF))
+
+
+def first_weights(plan, own, n2, n2o, g, go):
+    half, width = n2.shape
+    cols = width // 2
+    steps = g.shape[1] // cols
+    part = jax.ShapeDtypeStruct((plan.groups // 2, steps * (width // plan.groups), cols), BF)
+    return pl.pallas_call(
+        functools.partial(first_weights_kernel, plan),
+        grid_spec=pltpu.PrefetchScalarGridSpec(
+            num_scalar_prefetch=1,
+            grid=(steps,),
+            in_specs=[
                 whole(n2.shape),
                 whole(n2o.shape),
-                pl.BlockSpec((half, cols), lambda i, o, b: (0, i)),
-                pl.BlockSpec((half, cols), lambda i, o, b: (0, i)),
-            ],
-            out_specs=[whole(part.shape)] * 4,
+                pl.BlockSpec((half, cols), lambda i, o: (0, i)),
+                pl.BlockSpec((half, cols), lambda i, o: (0, i)),
+            ],
+            out_specs=[whole(part.shape)] * 2,
             scratch_shapes=[pltpu.VMEM((width, cols), F32)],
         ),
-        out_shape=(part,) * 4,
+        out_shape=(part,) * 2,
         compiler_params=params(40),
-        cost_estimate=cost(4 * half * width * hidden, 2 * width * hidden + 8 * half * hidden),
-        name="feed_weights",
-    )(own, blk, act, acto, cot, coto, n2, n2o, g, go)
-
-
-def wrap_two(kernel, plan, own_ref, blk_ref, *refs):
-    kernel(plan, own_ref, *refs)
+        cost_estimate=cost(4 * half * width * g.shape[1], 2 * width * g.shape[1] + 4 * half * g.shape[1]),
+        name="first_weights",
+    )(own, n2, n2o, g, go)
 
 
 def attend_back_kernel(
-    blk_ref, q_ref, k_ref, v_ref, kh_ref, vh_ref, p_ref, ga_ref, d_ref, dh_ref, kcat_ref, vcat_ref
+    blk_ref, q_ref, k_ref, v_ref, kh_ref, vh_ref, p_ref, ga_ref, after_ref, d_ref, dh_ref, kcat_ref, vcat_ref
 ):
     half = q_ref.shape[1]
     kcat_ref[:half, :] = k_ref[0]
@@ -487,7 +539,7 @@
     dh_ref[1] = dv[half:]
 
 
-def attend_back(side, qkv, kh, vh, probs, ga):
+def attend_back(side, qkv, kh, vh, probs, ga, after):
     _, half, width = qkv.shape
     halo = kh.shape[0]
     keys = half + halo
@@ -509,6 +561,7 @@
                 pl.BlockSpec((halo, 128), lambda i, s: (0, col(i, s))),
                 pl.BlockSpec((2, half, keys), lambda i, s: (col(i, s), 0, 0)),
                 pl.BlockSpec((half, 128), lambda i, s: (0, col(i, s))),
+                pl.BlockSpec(memory_space=pl.ANY),
             ],
             out_specs=[
                 pl.BlockSpec((3, half, 128), lambda i, s: (0, 0, i)),
@@ -523,7 +576,7 @@
         compiler_params=params(40),
         cost_estimate=cost(16 * half * keys * width, half * keys * width // HD),
         name="attend_back",
-    )(side, qkv, qkv, qkv, kh, vh, probs, ga)
+    )(side, qkv, qkv, qkv, kh, vh, probs, ga, after)
 
 
 def add_rows(ref, which, start, halo, extra):
@@ -558,7 +611,7 @@
         for p in range(plan.groups):
             source = pl.multiple_of((own ^ p) * rows, 16)
             block = acc_ref[pl.ds(source, rows), :]
-            store_block(outs, plan, panel // 2, p, (panel % 2) * rows, block.astype(BF))
+            store_block(outs[2 * (panel // 2) :][:2], plan, panel // 2, p, (panel % 2) * rows, block.astype(BF))
 
 
 def attend_weights(plan, own, blk, n1, n1o, d, dh, do, dho, att, atto, gb, gbo):
@@ -599,8 +652,9 @@
 
 def front_back_kernel(
     blk_ref, da_ref, db_ref, ha_ref, hb_ref, w_ref, h0_ref, gh_ref, g1_ref, pos_ref, sums_ref, b1_ref,
-    gx_ref, small_ref, acc_ref,
+    *rest,
 ):
+    gx_ref, small_ref, acc_ref = rest[-3:]
     half, width = h0_ref.shape
     halo = ha_ref.shape[1]
     cols = width // 2
@@ -614,17 +668,17 @@
     total = jnp.zeros((half, width), F32)
     for which in range(3):
         for side, ref in enumerate((acc_ref.at[0], acc_ref.at[1])):
-            at = which * width + side * cols
+            actual = blk_ref[0] if side == 0 else 1 - blk_ref[0]
+            at = pl.multiple_of(actual * cols, 128)
             panel = ref[which]
-            total = total + dot_nt(panel, w_ref[:, at : at + cols])
-            if which == 0:
-                small_ref[places + 2 : places + 3, side * cols : side * cols + cols] = column_sum(panel.astype(F32))
-            if which == 2:
-                small_ref[places + 3 : places + 4, side * cols : side * cols + cols] = column_sum(panel.astype(F32))
+            total = total + dot_nt(panel, w_ref[:, pl.ds(pl.multiple_of(which * width + at, 128), cols)])
+            if which != 1:
+                k = places + (2 if which == 0 else 3)
+                small_ref[k : k + 1, pl.ds(at, cols)] = column_sum(panel.astype(F32))
     normal, inv = normalise(h0_ref[...])
     small_ref[places : places + 1, :] = column_sum(total * normal)
     small_ref[places + 1 : places + 2, :] = column_sum(total)
-    grad = (gh_ref[...] + norm_back(total, normal, inv, g1_ref[...])).astype(BF)
+    grad = (gh_ref[...] + norm_back(total, normal, inv, line(g1_ref))).astype(BF)
     gx_ref[...] = grad
     hot = (lax.broadcasted_iota(jnp.int32, (places, half), 0) == pos_ref[...]).astype(F32).astype(BF)
     small_ref[:places, :] = dot_nn(hot, grad)
@@ -633,14 +687,15 @@
         small_ref[places + 8 + k : places + 9 + k, :] = b1_ref[:, k * width : (k + 1) * width]
 
 
-def front_back(blk, da, db, ha, hb, w, h0, gh, g1, pos, sums, b1, places):
+def front_back(blk, da, db, ha, hb, w, h0, gh, g1, pos, sums, b1, places, after):
     half, width = h0.shape
     return pl.pallas_call(
         front_back_kernel,
         grid_spec=pltpu.PrefetchScalarGridSpec(
             num_scalar_prefetch=1,
             grid=(1,),
-            in_specs=[whole(a.shape) for a in (da, db, ha, hb, w, h0, gh, g1, pos, sums, b1)],
+            in_specs=[whole(a.shape) for a in (da, db, ha, hb, w, h0, gh, g1, pos, sums, b1)]
+            + [pl.BlockSpec(memory_space=pl.ANY)] * len(after),
             out_specs=[whole((half, width)), whole((places + 12, width))],
             scratch_shapes=[pltpu.VMEM((2,) + da.shape, BF)],
         ),
@@ -651,7 +706,7 @@
         compiler_params=params(40),
         cost_estimate=cost(6 * half * width * width, 6 * width * width + 20 * half * width),
         name="front_back",
-    )(blk, da, db, ha, hb, w, h0, gh, g1, pos, sums, b1)
+    )(blk, da, db, ha, hb, w, h0, gh, g1, pos, sums, b1, *after)
 
 
 def swap(v):
@@ -666,31 +721,33 @@
     return v.astype(F32)
 
 
-def scatter_pairs(plan, ndp, parts):
-    later = []
-    for piece in range(2):
-        sent, kept = parts[2 * piece], parts[2 * piece + 1]
-        terms = [kept, across(sent, ndp, plan.rest << plan.orders[piece][0])]
-        later.append(terms)
-    count = plan.groups // 2
-    if plan.bits > 1:
-        for piece in range(2):
-            h = count // 2
-            out = sum(wide(t[:h]) for t in later[piece]).astype(BF)
-            got = across(out, ndp, plan.rest << plan.orders[piece][1])
-            later[piece] = [t[h:] for t in later[piece]] + [got]
-        count //= 2
+def open_pairs(plan, ndp, parts):
+    return [[parts[2 * k + 1], across(parts[2 * k], ndp, plan.rest << plan.orders[k][0])] for k in range(2)]
+
+
+def next_pairs(plan, ndp, later):
+    if plan.bits < 2:
+        return later, ()
+    h = plan.groups // 4
+    outs = tuple(sum(wide(t[:h]) for t in terms).astype(BF) for terms in later)
+    gots = [across(outs[k], ndp, plan.rest << plan.orders[k][1]) for k in range(2)]
+    return [[t[h:] for t in later[k]] + [gots[k]] for k in range(2)], outs
+
+
+def close_pairs(plan, ndp, later):
+    count = max(1, plan.groups // 4)
+    merged = [jnp.stack([sum(wide(t) for t in later[piece]) for piece in range(2)])]
     for bit in range(2, plan.bits):
         h = count // 2
-        if bit == 2:
-            merged = [jnp.stack([sum(wide(t) for t in later[piece]) for piece in range(2)])]
         out = sum(wide(t[:, :h]) for t in merged).astype(BF)
         got = across(out, ndp, plan.rest << bit)
         merged = [t[:, h:] for t in merged] + [got]
         count //= 2
-    if plan.bits <= 2:
-        merged = [jnp.stack([sum(wide(t) for t in later[piece]) for piece in range(2)])]
     return sum(wide(t) for t in merged)[:, 0]
+
+
+def behind(values, *others):
+    return lax.optimization_barrier((values, others))[0]
 
 
 def rest_of(plan, ndp, value, rows):
@@ -732,44 +789,49 @@
     dp = lax.axis_index("dp")
     blk1 = blk.astype(jnp.int32).reshape(1)
     own1 = (dp // plan.rest).astype(jnp.int32).reshape(1)
-    row = lambda v: v.reshape(1, -1)
 
     cot_other = swap(cot)
-    hidden0, n1 = embed(x, segments, positions, pos_table, row(ln1_gain), row(ln1_shift))
+    hidden0, n1 = embed(x, segments, positions, pos_table, ln1_gain, ln1_shift)
     n1_other = swap(n1)
-    qkv = qkv_own(n1, qkv_weight, row(query_bias), row(value_bias))
-    att, probs, kh, vh = attend(blk1, qkv, qkv_weight, row(value_bias), n1, n1_other, halo)
+    qkv = qkv_own(n1, qkv_weight, query_bias, value_bias)
+    att, probs, kh, vh = attend(blk1, qkv, qkv_weight, value_bias, n1, n1_other, halo)
     att_other = swap(att)
-    result, hidden1, n2, act, grad_send, grad_keep, gn2, b1_grad = feed(
-        blk1, att, hidden0, cot, out_weight, row(out_bias), row(ln2_gain), row(ln2_shift),
-        fc1_weight, row(fc1_bias), fc2_weight, row(fc2_bias),
+    hidden1, n2, act, grad_send, grad_keep, b1_grad = feed(
+        blk1, att, hidden0, cot, out_weight, out_bias, ln2_gain, ln2_shift, fc1_weight, fc1_bias, fc2_weight
     )
-    act_other, n2_other, grad_other = swap(act), swap(n2), swap(grad_send)
-    gh1, gb, ga, sums = mid(gn2, hidden1, cot, out_weight, row(ln2_gain))
+    grad_other, n2_other, act_other = swap(grad_send), swap(n2), swap(act)
+    result, gh1, gb, ga, sums = feed_back(
+        blk1, act, grad_send, grad_keep, fc1_weight, fc2_weight, hidden1, fc2_bias, cot, out_weight, ln2_gain
+    )
     gb_other = swap(gb)
-    first = feed_weights(plan, own1, blk1, act, act_other, cot, cot_other, n2, n2_other, grad_keep, grad_other)
-    summed_first = scatter_pairs(plan, ndp, first)
-
-    d_send, h_send = attend_back(1 - blk1, qkv, kh, vh, probs, ga)
+    fc1_parts = first_weights(plan, own1, n2, n2_other, grad_keep, grad_other)
+    fc2_parts = second_weights(plan, own1, blk1, act, act_other, cot, cot_other)
+    open_first = open_pairs(plan, ndp, fc2_parts + fc1_parts)
+    d_send, h_send = attend_back(1 - blk1, qkv, kh, vh, probs, ga, fc2_parts[0])
     d_other, h_other = swap(d_send), swap(h_send)
-    d_keep, h_keep = attend_back(blk1, qkv, kh, vh, probs, ga)
+    d_keep, h_keep = attend_back(blk1, qkv, kh, vh, probs, ga, d_send)
     h_late = swap(h_keep)
     second = attend_weights(
         plan, own1, blk1, n1, n1_other, d_keep, h_keep, d_other, h_other, att, att_other, gb, gb_other
     )
-    summed_second = scatter_pairs(plan, ndp, second)
-    is0 = blk == 0
-    pick = lambda a, b: jnp.where(is0, a, b)
+    kept = behind((open_first[0][0], open_first[1][0]), second[0])
+    open_first[0][0], open_first[1][0] = kept
+    open_first, outs = next_pairs(plan, ndp, open_first)
+    open_second = open_pairs(plan, ndp, behind(tuple(second), *outs))
+    pick = lambda a, b: jnp.where(blk == 0, a, b)
     grad_x, small = front_back(
-        blk1, pick(d_keep, d_send), pick(d_send, d_keep), pick(h_other, h_late), pick(h_late, h_other),
-        qkv_weight, hidden0, gh1, row(ln1_gain), positions, sums, b1_grad, places,
+        blk1, d_keep, d_send, h_other, h_late,
+        qkv_weight, hidden0, gh1, ln1_gain, positions, sums, b1_grad, places,
+        (second[0],) + outs,
     )
+    summed_first = close_pairs(plan, ndp, open_first)
+    open_second, _ = next_pairs(plan, ndp, open_second)
+    summed_second = close_pairs(plan, ndp, open_second)
     small = total_small(small, ndp)
 
     rg = width // ndp
     r1 = width // plan.groups
     cols = width // 2
-    r2 = hidden // plan.groups // 2
 
     def finish(value, lead):
         parts = value.reshape(lead, 2, -1, cols)
@@ -777,8 +839,8 @@
         got = swap(lax.dynamic_index_in_dim(parts, 1 - blk, 1, keepdims=False))
         return pick(jnp.stack([mine, got], 2), jnp.stack([got, mine], 2))
 
-    fc2_block = rest_of(plan, ndp, summed_first[:, :r2].reshape(1, 2 * r2, cols), hidden // ndp)
-    fc1_block = rest_of(plan, ndp, summed_first[:, r2:].reshape(4, r1, cols), rg)
+    fc2_block = rest_of(plan, ndp, summed_first[:1], hidden // ndp)
+    fc1_block = rest_of(plan, ndp, summed_first[1].reshape(4, r1, cols), rg)
     att_block = rest_of(plan, ndp, summed_second.reshape(4, r1, cols), rg)
     fc2_grad = finish(fc2_block, 1).reshape(-1, width)
     fc1_own = finish(fc1_block, 4)

time: 208 us -> 206 us (level)
  local copies, waits for them, and re-layouts: 37.7 us -> 33.4 us
  waiting for transfers between devices: 61.8 us -> 58 us
  Pallas kernels: 71.9 us -> 75.6 us
    pallas_call x2 -> x3, Pallas kernels: 12.8 us -> 25.7 us  [the longest x1 11.1 us: feed_back(): pl.pallas_call(feed_back_kernel, grid_spec=pltpu.PrefetchScalarGridSpec(n...]
    ppermute x16, waiting for transfers between devices: 59 us -> 49.6 us  [across(): return lax.ppermute(v, 'dp', [(i, i ^ flip) for i in range(ndp)])]
    pallas_call x1, Pallas kernels: 17.8 us -> 11.2 us  [feed(): pl.pallas_call(feed_kernel, grid_spec=pltpu.PrefetchScalarGridSpec(num_sc...]
    ppermute x15, waiting for transfers between devices: 2.78 us -> 8.3 us  [swap(): return lax.ppermute(v, 'blk', [(0, 1), (1, 0)])]
    reshape x8 -> x0, local copies, waits for them, and re-layouts: 5.51 us -> none  [per_device(): row = lambda v: v.reshape(1, -1)]
    select_n x4 -> x2, other arithmetic: 4.03 us -> 0.44 us  [per_device(): pick = lambda a, b: jnp.where(blk == 0, a, b)]
    convert_element_type x6, other arithmetic: 2.28 us -> 5.17 us  [the longest x4 3.21 us: next_pairs(): sum((wide(t[:h]) for t in terms)).astype(BF)]
    another operation x6, other arithmetic: 1.71 us -> 4.42 us  [the longest x4 2.75 us: close_pairs(): jnp.stack([sum((wide(t) for t in later[piece])) for piece in range(2)])]
  transfers between devices with their start and end apart: 31 -> 31, of which waited for: 11 -> 13; matrix products, arithmetic and copies ran while one was open for 9% -> 9% of each run, Pallas kernels for 16% -> 24%
where the time goes in v2:
time: 206 us; the launch traced here: 205 us
  Pallas kernels  75.6 us (37%)
  waiting for transfers between devices  58 us (28%)
  local copies, waits for them, and re-layouts  33.4 us (16%)
  starting transfers between devices  23 us (11%)
  other arithmetic  13.3 us (6%)
    ppermute x16, waiting for transfers between devices, across(): return lax.ppermute(v, 'dp', [(i, i ^ flip) for i in range(ndp)])  49.6 us
    unnamed x137, local copies, waits for them, and re-layouts  28.2 us
    ppermute x16, starting transfers between devices, across(): return lax.ppermute(v, 'dp', [(i, i ^ flip) for i in range(ndp)])  19.4 us
    pallas_call x2, Pallas kernels, attend_back(): pl.pallas_call(attend_back_kernel, grid_spec=pltpu.PrefetchScalarGridSpec...  15.4 us
    pallas_call x1, Pallas kernels, feed(): pl.pallas_call(feed_kernel, grid_spec=pltpu.PrefetchScalarGridSpec(num_sc...  11.2 us
    pallas_call x1, Pallas kernels, feed_back(): pl.pallas_call(feed_back_kernel, grid_spec=pltpu.PrefetchScalarGridSpec(n...  11.1 us
    pallas_call x1, Pallas kernels, attend(): pl.pallas_call(attend_kernel, grid_spec=pltpu.PrefetchScalarGridSpec(num_...  9.27 us
    ppermute x15, waiting for transfers between devices, swap(): return lax.ppermute(v, 'blk', [(0, 1), (1, 0)])  8.3 us
  transfers between devices with their start and end apart: 31, of which 13 were waited for; matrix products, arithmetic and copies ran while one was open for 9% of the time, Pallas kernels for 24%

profile of v2, /device:TPU:0, one launch (start us, length us, event | category | flops | bytes accessed | tf_op | source)
XLA Modules:
  0.0 204.6 jit_solution(17528960015832251559)
XLA Ops:
  0.7 1.1 copy-done.35
  6.2 1.0 copy-done.6
  7.6 2.0 copy-done
  11.0 2.5 %qkv_own.1.q_ref.k_ref.v_ref = bf16[3,392,768]{2,1,0:T(8,128)(2,1)S(1)} custom-call(bf16[392,896]{1,0:T(8,128)(2,1)S(1)} %get-tuple-element.53.n1_ref.hot_ref, bf16[768,2304]{1,0:T(8,128)(2,1)S(1)} %copy-done, f32[768]{0:T(1024)S(1)} %copy-done.58, f32[768]{0:T(1024)S(1)} %copy-done.49), custom_call_target="tpu_custom_call" | custom-call | flops 13872660 | bytes 59473 | tf_op jit(solution)/shard_map/qkv_own/pallas_call | solution.py:118
  14.4 1.1 copy-done.15
  15.6 9.3 %attend.1 = (bf16[392,768]{1,0:T(8,128)(2,1)}, bf16[12,392,640]{2,1,0:T(8,128)(2,1)S(1)}, bf16[248,768]{1,0:T(8,128)(2,1)S(1)}, bf16[248,768]{1,0:T(8,128)(2,1)S(1)}) custom-call(s32[1]{0:T(128)} %bitcast.blk_ref, bf16[3,392,768]{2,1,0:T(8,128)(2,1)S(1)} %qkv_own.1.q_ref.k_ref.v_ref, bf16[3,392,768]{2,1,0:T(8,128)(2,1)S(1)} %qkv_own.1.q_ref.k_ref.v_ref, ...), custom_call_target="tpu_custom_call" | custom-call | flops 30828134 | bytes 60211 | tf_op jit(solution)/shard_map/attend/pallas_call | solution.py:187
  24.8 2.5 %copy-done.3 = bf16[12,392,640]{2,1,0:T(8,128)(2,1)} copy-done((bf16[12,392,640]{2,1,0:T(8,128)(2,1)}, bf16[12,392,640]{2,1,0:T(8,128)(2,1)S(1)}, u32[]{:S(2)}) %copy-start.3) | copy-done | bytes 6021144
  27.4 11.2 %feed.1 = (f32[392,768]{1,0:T(8,128)S(1)}, bf16[392,768]{1,0:T(8,128)(2,1)}, bf16[392,3072]{1,0:T(8,128)(2,1)}, bf16[392,1536]{1,0:T(8,128)(2,1)}, bf16[392,1536]{1,0:T(8,128)(2,1)S(1)}, /*index=5*/f32[1,3072]{1,0:T(1,128)S(1)}) custom-call(s32[1]{0:T(128)} %bitcast.blk_ref, bf16[392,768]{1,0:T(8,128)(2,1)} %get-tuple-element.54.att_ref, ...), custom_call_target="tpu_custom_call" | custom-call | flops 41617980 | bytes 94371 | tf_op jit(solution)/shard_map/feed/pallas_call | solution.py:267
  38.7 1.0 copy-done.9
  39.7 1.0 copy-done.27
  41.8 7.4 %collective-permute-done.8.n2o_ref = bf16[392,768]{1,0:T(8,128)(2,1)} collective-permute-done((bf16[392,768]{1,0:T(8,128)(2,1)}, bf16[392,768]{1,0:T(8,128)(2,1)}, u32[]{:S(2)}, u32[]{:S(2)}) %collective-permute-start.8) | collective-permute-done | bytes 602144 | tf_op jit(solution)/shard_map/ppermute | solution.py:713
  49.2 1.3 copy-done.10
  50.5 7.1 %first_weights.1 = (bf16[8,192,384]{2,1,0:T(8,128)(2,1)}, bf16[8,192,384]{2,1,0:T(8,128)(2,1)S(1)}) custom-call(s32[1]{0:T(128)} %bitcast.4.own_ref, bf16[392,768]{1,0:T(8,128)(2,1)} %get-tuple-element.76.n2_ref, bf16[392,768]{1,0:T(8,128)(2,1)} %collective-permute-done.8.n2o_ref, bf16[392,1536]{1,0:T(8,128)(2,1)S(1)} %copy-done.10, ...), custom_call_target="tpu_custom_call" | custom-call | flops 18496880 | bytes 47677 | tf_op jit(solution)/shard_map/first_weights/pallas_call | solution.py:490
  57.5 1.0 copy-done.29
  58.6 2.7 %collective-permute-start.11 = (bf16[8,192,384]{2,1,0:T(8,128)(2,1)}, bf16[8,192,384]{2,1,0:T(8,128)(2,1)}, u32[]{:S(2)}, u32[]{:S(2)}) collective-permute-start(bf16[8,192,384]{2,1,0:T(8,128)(2,1)} %get-tuple-element.80), channel_id=1, source_target_pairs={{0,4},{2,6},{4,0},{6,2},{8,12},{10,14},{12,8},{14,10},{16,20},{18,... | collective-permute-start | bytes 3538952 | tf_op jit(solution)/shard_map/ppermute | solution.py:717
  61.3 11.1 %feed_back.1 = (bf16[392,768]{1,0:T(8,128)(2,1)}, f32[392,768]{1,0:T(8,128)S(1)}, bf16[392,768]{1,0:T(8,128)(2,1)S(1)}, bf16[392,768]{1,0:T(8,128)(2,1)S(1)}, f32[4,768]{1,0:T(4,128)S(1)}) custom-call(s32[1]{0:T(128)} %bitcast.blk_ref, bf16[392,3072]{1,0:T(8,128)(2,1)} %get-tuple-element.56.act_ref, bf16[392,1536]{1,0:T(8,128)(2,1)} %get-tuple-element.57.gs_ref, ...), custom_call_target="tpu_custom_call" | custom-call | flops 41617980 | bytes 94371 | tf_op jit(solution)/shard_map/feed_back/pallas_call | solution.py:352
  72.4 1.0 copy-done.25
  73.6 7.5 %second_weights.1 = (bf16[8,192,384]{2,1,0:T(8,128)(2,1)}, bf16[8,192,384]{2,1,0:T(8,128)(2,1)S(1)}) custom-call(s32[1]{0:T(128)} %bitcast.4.own_ref, s32[1]{0:T(128)} %bitcast.blk_ref, bf16[392,3072]{1,0:T(8,128)(2,1)} %get-tuple-element.56.act_ref, bf16[392,3072]{1,0:T(8,128)(2,1)} %collective-permute-done.1.acto_ref, bf16[392,768]{1,0:T(8,128)(2,1)S(1)} %bitcast.60, ...), custom_call_target="tpu_custom_call" | custom-call | flops 18496880 | bytes 71761 | tf_op jit(solution)/shard_map/second_weights/pallas_call | solution.py:448
  81.1 1.5 collective-permute-start.10
  82.6 8.1 %attend_back.2 = (bf16[3,392,384]{2,1,0:T(8,128)(2,1)S(1)}, bf16[2,248,384]{2,1,0:T(8,128)(2,1)}) custom-call(s32[1]{0:T(128)S(6)} %sub.6.blk_ref, bf16[3,392,768]{2,1,0:T(8,128)(2,1)S(1)} %qkv_own.1.q_ref.k_ref.v_ref, bf16[3,392,768]{2,1,0:T(8,128)(2,1)S(1)} %qkv_own.1.q_ref.k_ref.v_ref, bf16[3,392,768]{2,1,0:T(8,128)(2,1)S(1)} %qkv_own.1.q_ref.k_ref.v_ref, ...), custom_call_target="tpu_custom_call" | custom-call | flops 30828134 | bytes 30105 | tf_op jit(solution)/shard_map/attend_back/pallas_call | solution.py:551
  92.1 2.7 %copy-done.4 = bf16[12,392,640]{2,1,0:T(8,128)(2,1)S(1)} copy-done((bf16[12,392,640]{2,1,0:T(8,128)(2,1)S(1)}, bf16[12,392,640]{2,1,0:T(8,128)(2,1)}, u32[]{:S(2)}) %copy-start.4) | copy-done | bytes 6021144
  94.8 1.1 copy-done.18
  95.9 1.0 copy-done.21
  96.9 1.0 copy-done.24
  97.9 7.3 %attend_back.3 = (bf16[3,392,384]{2,1,0:T(8,128)(2,1)S(1)}, bf16[2,248,384]{2,1,0:T(8,128)(2,1)S(1)}) custom-call(s32[1]{0:T(128)} %bitcast.blk_ref, bf16[3,392,768]{2,1,0:T(8,128)(2,1)S(1)} %qkv_own.1.q_ref.k_ref.v_ref, bf16[3,392,768]{2,1,0:T(8,128)(2,1)S(1)} %qkv_own.1.q_ref.k_ref.v_ref, bf16[3,392,768]{2,1,0:T(8,128)(2,1)S(1)} %qkv_own.1.q_ref.k_ref.v_ref, ...), custom_call_target="tpu_custom_call" | custom-call | flops 30828134 | bytes 30105 | tf_op jit(solution)/shard_map/attend_back/pallas_call | solution.py:551
  105.8 5.7 %attend_weights.1 = (bf16[8,96,384]{2,1,0:T(8,128)(2,1)S(1)}, bf16[8,96,384]{2,1,0:T(8,128)(2,1)S(1)}, bf16[8,96,384]{2,1,0:T(8,128)(2,1)S(1)}, bf16[8,96,384]{2,1,0:T(8,128)(2,1)S(1)}) custom-call(s32[1]{0:T(128)} %bitcast.4.own_ref, s32[1]{0:T(128)} %bitcast.blk_ref, bf16[392,896]{1,0:T(8,128)(2,1)S(1)} %get-tuple-element.53.n1_ref.hot_ref, ...), custom_call_target="tpu_custom_call" | custom-call | flops 18496880 | bytes 95846 | tf_op jit(solution)/shard_map/attend_weights/pallas_call | solution.py:622
  112.4 1.8 add_convert_fusion.rest_2_
  114.2 1.2 add_convert_fusion.1.rest_1_
  115.5 5.1 %front_back.1 = (bf16[392,768]{1,0:T(8,128)(2,1)}, f32[208,768]{1,0:T(8,128)S(1)}) custom-call(s32[1]{0:T(128)} %bitcast.blk_ref, bf16[3,392,384]{2,1,0:T(8,128)(2,1)S(1)} %get-tuple-element.67.d_ref.da_ref, bf16[3,392,384]{2,1,0:T(8,128)(2,1)S(1)} %get-tuple-element.66.after_ref.db_ref, bf16[2,248,384]{2,1,0:T(8,128)(2,1)} %collective-permute-done.3.dho_ref.ha_ref, ...), custom_call_target="tpu_custom_call" | custom-call | flops 13872660 | bytes 95600 | tf_op jit(solution)/shard_map/front_back/pallas_call | solution.py:692
  123.3 2.7 %collective-permute-start.13 = (bf16[208,384]{1,0:T(8,128)(2,1)S(1)}, bf16[208,384]{1,0:T(8,128)(2,1)S(1)}, u32[]{:S(2)}, u32[]{:S(2)}) collective-permute-start(bf16[208,384]{1,0:T(8,128)(2,1)S(1)} %add_convert_fusion.8), channel_id=1, source_target_pairs={{0,16},{2,18},{4,20},{6,22},{8,24},{10,26},{12,28},{14,30},{16,0},... | collective-permute-start | bytes 479240 | tf_op jit(solution)/shard_map/ppermute | solution.py:717
  126.4 1.5 collective-permute-start.20
  128.6 5.3 %collective-permute-done.13 = bf16[208,384]{1,0:T(8,128)(2,1)S(1)} collective-permute-done((bf16[208,384]{1,0:T(8,128)(2,1)S(1)}, bf16[208,384]{1,0:T(8,128)(2,1)S(1)}, u32[]{:S(2)}, u32[]{:S(2)}) %collective-permute-start.13) | collective-permute-done | bytes 159776 | tf_op jit(solution)/shard_map/ppermute | solution.py:717
  134.6 2.4 %collective-permute-done.26 = bf16[4,192,384]{2,1,0:T(8,128)(2,1)S(1)} collective-permute-done((bf16[4,192,384]{2,1,0:T(8,128)(2,1)S(1)}, bf16[4,192,384]{2,1,0:T(8,128)(2,1)S(1)}, u32[]{:S(2)}, u32[]{:S(2)}) %collective-permute-start.26) | collective-permute-done | bytes 589856 | tf_op jit(solution)/shard_map/ppermute | solution.py:717
  137.0 1.3 add_bitcast_fusion
  139.9 2.3 %collective-permute-done.25 = bf16[4,192,384]{2,1,0:T(8,128)(2,1)S(1)} collective-permute-done((bf16[4,192,384]{2,1,0:T(8,128)(2,1)S(1)}, bf16[4,192,384]{2,1,0:T(8,128)(2,1)S(1)}, u32[]{:S(2)}, u32[]{:S(2)}) %collective-permute-start.25) | collective-permute-done | bytes 589856 | tf_op jit(solution)/shard_map/ppermute | solution.py:717
  142.2 1.3 add_bitcast_fusion.1
  144.4 1.6 collective-permute-start.27
  145.9 8.9 %collective-permute-done.20 = bf16[8,96,384]{2,1,0:T(8,128)(2,1)S(1)} collective-permute-done((bf16[8,96,384]{2,1,0:T(8,128)(2,1)}, bf16[8,96,384]{2,1,0:T(8,128)(2,1)S(1)}, u32[]{:S(2)}, u32[]{:S(2)}) %collective-permute-start.20) | collective-permute-done | bytes 589856 | tf_op jit(solution)/shard_map/ppermute | solution.py:717
  155.5 1.6 collective-permute-done.15
  158.5 6.8 %collective-permute-done.16 = bf16[208,384]{1,0:T(8,128)(2,1)S(1)} collective-permute-done((bf16[208,384]{1,0:T(8,128)(2,1)S(1)}, bf16[208,384]{1,0:T(8,128)(2,1)S(1)}, u32[]{:S(2)}, u32[]{:S(2)}) %collective-permute-start.16) | collective-permute-done | bytes 159776 | tf_op jit(solution)/shard_map/ppermute | solution.py:717
  166.6 1.6 collective-permute-start.22
  169.9 1.7 slice_reduce_fusion
  171.6 4.5 %collective-permute-done.22 = bf16[2,2,96,384]{3,2,1,0:T(8,128)(2,1)} collective-permute-done((bf16[2,2,96,384]{3,2,1,0:T(8,128)(2,1)}, bf16[2,2,96,384]{3,2,1,0:T(8,128)(2,1)}, u32[]{:S(2)}, u32[]{:S(2)}) %collective-permute-start.22) | collective-permute-done | bytes 294944 | tf_op jit(solution)/shard_map/ppermute | solution.py:717
  177.5 1.0 fusion.8
  178.5 2.6 %collective-permute-start.28 = (bf16[2,1,192,384]{3,2,1,0:T(8,128)(2,1)S(1)}, bf16[2,1,192,384]{3,2,1,0:T(8,128)(2,1)S(1)}, u32[]{:S(2)}, u32[]{:S(2)}) collective-permute-start(bf16[2,1,192,384]{3,2,1,0:T(8,128)(2,1)S(1)} %fusion.8), channel_id=1, source_target_pairs={{0,16},{2,18},{4,20},{6,22},{8,24},{10,26},{12,28},{14,30},{16,0},... | collective-permute-start | bytes 884744 | tf_op jit(solution)/shard_map/ppermute | solution.py:717
  181.1 12.7 %collective-permute-done.23 = bf16[2,1,96,384]{3,2,1,0:T(8,128)(2,1)S(1)} collective-permute-done((bf16[2,1,96,384]{3,2,1,0:T(8,128)(2,1)S(1)}, bf16[2,1,96,384]{3,2,1,0:T(8,128)(2,1)S(1)}, u32[]{:S(2)}, u32[]{:S(2)}) %collective-permute-start.23) | collective-permute-done | bytes 147488 | tf_op jit(solution)/shard_map/ppermute | solution.py:717
  195.0 4.1 %collective-permute-done.28 = bf16[2,1,192,384]{3,2,1,0:T(8,128)(2,1)S(1)} collective-permute-done((bf16[2,1,192,384]{3,2,1,0:T(8,128)(2,1)S(1)}, bf16[2,1,192,384]{3,2,1,0:T(8,128)(2,1)S(1)}, u32[]{:S(2)}, u32[]{:S(2)}) %collective-permute-start.28) | collective-permute-done | bytes 294944 | tf_op jit(solution)/shard_map/ppermute | solution.py:717
  199.0 1.0 fusion.6
  (204 shorter events, 30.3 us)
Async XLA Ops:
  7.2 6.4 %collective-permute-start = (bf16[392,896]{1,0:T(8,128)(2,1)S(1)}, bf16[392,896]{1,0:T(8,128)(2,1)S(1)}, u32[]{:S(2)}, u32[]{:S(2)}) collective-permute-start(bf16[392,896]{1,0:T(8,128)(2,1)S(1)} %get-tuple-element.53.n1_ref.hot_ref), channel_id=1, source_target_pairs={{0,1},{1,0},{2,3},{3,2},{4,5},{5,4},{6,7},{7,6},{8,9},{9,8},{10,11... | collective-permute-start | bytes 2107400 | tf_op jit(solution)/shard_map/ppermute | solution.py:713
  15.5 11.9 %copy-start.5 = (bf16[1,392,768]{2,1,0:T(8,128)(2,1)S(1)}, bf16[1,392,768]{2,1,0:T(8,128)(2,1)}, u32[]{:S(2)}) copy-start(bf16[1,392,768]{2,1,0:T(8,128)(2,1)} %param.35) | copy-start | bytes 1806340
  15.5 11.9 %copy-start.7 = (f32[392,768]{1,0:T(8,128)S(1)}, f32[392,768]{1,0:T(8,128)}, u32[]{:S(2)}) copy-start(f32[392,768]{1,0:T(8,128)} %copy-done.6) | copy-start | bytes 3612676
  15.5 11.9 %copy-start.12 = (bf16[768,768]{1,0:T(8,128)(2,1)S(1)}, bf16[768,768]{1,0:T(8,128)(2,1)}, u32[]{:S(2)}) copy-start(bf16[768,768]{1,0:T(8,128)(2,1)} %wo_ref.3) | copy-start | bytes 3538948
  15.5 11.9 %copy-start.51 = (f32[768]{0:T(1024)S(1)}, f32[768]{0:T(1024)}, u32[]{:S(2)}) copy-start(f32[768]{0:T(1024)} %g2_ref.3) | copy-start | bytes 9220
  15.5 11.9 %copy-start.52 = (f32[3072]{0:T(1024)S(1)}, f32[3072]{0:T(1024)}, u32[]{:S(2)}) copy-start(f32[3072]{0:T(1024)} %b1_ref.1) | copy-start | bytes 36868
  15.6 11.9 %copy-start.56 = (f32[768]{0:T(1024)S(1)}, f32[768]{0:T(1024)}, u32[]{:S(2)}) copy-start(f32[768]{0:T(1024)} %bo_ref.1) | copy-start | bytes 9220
  15.6 11.9 %copy-start.57 = (f32[768]{0:T(1024)S(1)}, f32[768]{0:T(1024)}, u32[]{:S(2)}) copy-start(f32[768]{0:T(1024)} %s2_ref.1) | copy-start | bytes 9220
  27.4 11.3 %copy-start.19 = (bf16[248,768]{1,0:T(8,128)(2,1)}, bf16[248,768]{1,0:T(8,128)(2,1)S(1)}, u32[]{:S(2)}) copy-start(bf16[248,768]{1,0:T(8,128)(2,1)S(1)} %get-tuple-element.61.kh_ref) | copy-start | bytes 1142788
  27.4 11.3 %copy-start.22 = (bf16[248,768]{1,0:T(8,128)(2,1)}, bf16[248,768]{1,0:T(8,128)(2,1)S(1)}, u32[]{:S(2)}) copy-start(bf16[248,768]{1,0:T(8,128)(2,1)S(1)} %get-tuple-element.62.vh_ref) | copy-start | bytes 1142788
  40.8 32.8 %collective-permute-start.1 = (bf16[392,3072]{1,0:T(8,128)(2,1)}, bf16[392,3072]{1,0:T(8,128)(2,1)}, u32[]{:S(2)}, u32[]{:S(2)}) collective-permute-start(bf16[392,3072]{1,0:T(8,128)(2,1)} %get-tuple-element.56.act_ref), channel_id=1, source_target_pairs={{0,1},{1,0},{2,3},{3,2},{4,5},{5,4},{6,7},{7,6},{8,9},{9,8},{10,11... | collective-permute-start | bytes 7225352 | tf_op jit(solution)/shard_map/ppermute | solution.py:713
  40.9 8.3 %collective-permute-start.9 = (bf16[392,1536]{1,0:T(8,128)(2,1)}, bf16[392,1536]{1,0:T(8,128)(2,1)}, u32[]{:S(2)}, u32[]{:S(2)}) collective-permute-start(bf16[392,1536]{1,0:T(8,128)(2,1)} %get-tuple-element.57.gs_ref), channel_id=1, source_target_pairs={{0,1},{1,0},{2,3},{3,2},{4,5},{5,4},{6,7},{7,6},{8,9},{9,8},{10,11... | collective-permute-start | bytes 3612680 | tf_op jit(solution)/shard_map/ppermute | solution.py:713
  41.3 7.9 %collective-permute-start.8 = (bf16[392,768]{1,0:T(8,128)(2,1)}, bf16[392,768]{1,0:T(8,128)(2,1)}, u32[]{:S(2)}, u32[]{:S(2)}) collective-permute-start(bf16[392,768]{1,0:T(8,128)(2,1)} %get-tuple-element.76.n2_ref), channel_id=1, source_target_pairs={{0,1},{1,0},{2,3},{3,2},{4,5},{5,4},{6,7},{7,6},{8,9},{9,8},{10,11... | collective-permute-start | bytes 1806344 | tf_op jit(solution)/shard_map/ppermute | solution.py:713
  41.4 32.2 %collective-permute-start.2 = (bf16[392,768]{1,0:T(8,128)(2,1)S(1)}, bf16[392,768]{1,0:T(8,128)(2,1)}, u32[]{:S(2)}, u32[]{:S(2)}) collective-permute-start(bf16[392,768]{1,0:T(8,128)(2,1)S(1)} %bitcast.58), channel_id=1, source_target_pairs={{0,1},{1,0},{2,3},{3,2},{4,5},{5,4},{6,7},{7,6},{8,9},{9,8},{10,11... | collective-permute-start | bytes 1806344 | tf_op jit(solution)/shard_map/ppermute | solution.py:713
  50.5 10.8 %copy-start.13 = (bf16[768,768]{1,0:T(8,128)(2,1)S(1)}, bf16[768,768]{1,0:T(8,128)(2,1)}, u32[]{:S(2)}) copy-start(bf16[768,768]{1,0:T(8,128)(2,1)} %wo_ref.3) | copy-start | bytes 3538948
  50.5 10.8 %copy-start.28 = (f32[392,768]{1,0:T(8,128)S(1)}, f32[392,768]{1,0:T(8,128)}, u32[]{:S(2)}) copy-start(f32[392,768]{1,0:T(8,128)} %copy-done.27) | copy-start | bytes 3612676
  50.5 10.8 %copy-start.59 = (f32[768]{0:T(1024)S(1)}, f32[768]{0:T(1024)}, u32[]{:S(2)}) copy-start(f32[768]{0:T(1024)} %b2_ref.1) | copy-start | bytes 9220
  58.6 53.8 %collective-permute-start.11 = (bf16[8,192,384]{2,1,0:T(8,128)(2,1)}, bf16[8,192,384]{2,1,0:T(8,128)(2,1)}, u32[]{:S(2)}, u32[]{:S(2)}) collective-permute-start(bf16[8,192,384]{2,1,0:T(8,128)(2,1)} %get-tuple-element.80), channel_id=1, source_target_pairs={{0,4},{2,6},{4,0},{6,2},{8,12},{10,14},{12,8},{14,10},{16,20},{18,... | collective-permute-start | bytes 3538952 | tf_op jit(solution)/shard_map/ppermute | solution.py:717
  61.3 21.3 %slice-start = ((s8[6021120]{0:T(1024)(128)(4,1)}), s8[4194304]{0:T(1024)(128)(4,1)S(1)}, s32[]{:S(2)}) async-start(s8[6021120]{0:T(1024)(128)(4,1)} %bitcast.55), calls=%async_computation | async-start | bytes 8388608
  61.3 21.3 %slice-start.1 = ((s8[6021120]{0:T(1024)(128)(4,1)}), s8[1826816]{0:T(1024)(128)(4,1)S(1)}, s32[]{:S(2)}) async-start(s8[6021120]{0:T(1024)(128)(4,1)} %bitcast.55), calls=%async_computation.1 | async-start | bytes 3653632
  73.4 17.8 %collective-permute-start.7 = (bf16[392,768]{1,0:T(8,128)(2,1)S(1)}, bf16[392,768]{1,0:T(8,128)(2,1)S(1)}, u32[]{:S(2)}, u32[]{:S(2)}) collective-permute-start(bf16[392,768]{1,0:T(8,128)(2,1)S(1)} %get-tuple-element.73.gb_ref), channel_id=1, source_target_pairs={{0,1},{1,0},{2,3},{3,2},{4,5},{5,4},{6,7},{7,6},{8,9},{9,8},{10,11... | collective-permute-start | bytes 1806344 | tf_op jit(solution)/shard_map/ppermute | solution.py:713
  81.1 33.1 %collective-permute-start.10 = (bf16[8,192,384]{2,1,0:T(8,128)(2,1)}, bf16[8,192,384]{2,1,0:T(8,128)(2,1)}, u32[]{:S(2)}, u32[]{:S(2)}) collective-permute-start(bf16[8,192,384]{2,1,0:T(8,128)(2,1)} %get-tuple-element.65.after_ref), channel_id=1, source_target_pairs={{0,2},{2,0},{4,6},{6,4},{8,10},{10,8},{12,14},{14,12},{16,18},{18,... | collective-permute-start | bytes 3538952 | tf_op jit(solution)/shard_map/ppermute | solution.py:717
  90.7 15.0 %collective-permute-start.5 = (bf16[3,392,384]{2,1,0:T(8,128)(2,1)S(1)}, bf16[3,392,384]{2,1,0:T(8,128)(2,1)}, u32[]{:S(2)}, u32[]{:S(2)}) collective-permute-start(bf16[3,392,384]{2,1,0:T(8,128)(2,1)S(1)} %get-tuple-element.66.after_ref.db_ref), channel_id=1, source_target_pairs={{0,1},{1,0},{2,3},{3,2},{4,5},{5,4},{6,7},{7,6},{8,9},{9,8},{10,11... | collective-permute-start | bytes 2709512 | tf_op jit(solution)/shard_map/ppermute | solution.py:713
  90.7 14.4 %collective-permute-start.6 = (bf16[392,768]{1,0:T(8,128)(2,1)}, bf16[392,768]{1,0:T(8,128)(2,1)}, u32[]{:S(2)}, u32[]{:S(2)}) collective-permute-start(bf16[392,768]{1,0:T(8,128)(2,1)} %get-tuple-element.54.att_ref), channel_id=1, source_target_pairs={{0,1},{1,0},{2,3},{3,2},{4,5},{5,4},{6,7},{7,6},{8,9},{9,8},{10,11... | collective-permute-start | bytes 1806344 | tf_op jit(solution)/shard_map/ppermute | solution.py:713
  92.1 13.6 %collective-permute-start.3 = (bf16[2,248,384]{2,1,0:T(8,128)(2,1)}, bf16[2,248,384]{2,1,0:T(8,128)(2,1)}, u32[]{:S(2)}, u32[]{:S(2)}) collective-permute-start(bf16[2,248,384]{2,1,0:T(8,128)(2,1)} %get-tuple-element.68), channel_id=1, source_target_pairs={{0,1},{1,0},{2,3},{3,2},{4,5},{5,4},{6,7},{7,6},{8,9},{9,8},{10,11... | collective-permute-start | bytes 1142792 | tf_op jit(solution)/shard_map/ppermute | solution.py:713
  105.2 10.3 %collective-permute-start.4 = (bf16[2,248,384]{2,1,0:T(8,128)(2,1)S(1)}, bf16[2,248,384]{2,1,0:T(8,128)(2,1)S(1)}, u32[]{:S(2)}, u32[]{:S(2)}) collective-permute-start(bf16[2,248,384]{2,1,0:T(8,128)(2,1)S(1)} %get-tuple-element.69.dh_ref), channel_id=1, source_target_pairs={{0,1},{1,0},{2,3},{3,2},{4,5},{5,4},{6,7},{7,6},{8,9},{9,8},{10,11... | collective-permute-start | bytes 1142792 | tf_op jit(solution)/shard_map/ppermute | solution.py:713
  120.7 16.4 %copy-start.31 = (bf16[8,192,384]{2,1,0:T(8,128)(2,1)S(1)}, bf16[8,192,384]{2,1,0:T(8,128)(2,1)}, u32[]{:S(2)}) copy-start(bf16[8,192,384]{2,1,0:T(8,128)(2,1)} %copy-done.29) | copy-start | bytes 3538948
  120.7 1.6 collective-permute-start.12
  120.8 16.2 %collective-permute-start.26 = (bf16[4,192,384]{2,1,0:T(8,128)(2,1)S(1)}, bf16[4,192,384]{2,1,0:T(8,128)(2,1)S(1)}, u32[]{:S(2)}, u32[]{:S(2)}) collective-permute-start(bf16[4,192,384]{2,1,0:T(8,128)(2,1)S(1)} %add_convert_fusion.rest_2_), channel_id=1, source_target_pairs={{0,2},{2,0},{4,6},{6,4},{8,10},{10,8},{12,14},{14,12},{16,18},{18,... | collective-permute-start | bytes 1769480 | tf_op jit(solution)/shard_map/ppermute | solution.py:717
  123.3 10.6 %collective-permute-start.13 = (bf16[208,384]{1,0:T(8,128)(2,1)S(1)}, bf16[208,384]{1,0:T(8,128)(2,1)S(1)}, u32[]{:S(2)}, u32[]{:S(2)}) collective-permute-start(bf16[208,384]{1,0:T(8,128)(2,1)S(1)} %add_convert_fusion.8), channel_id=1, source_target_pairs={{0,16},{2,18},{4,20},{6,22},{8,24},{10,26},{12,28},{14,30},{16,0},... | collective-permute-start | bytes 479240 | tf_op jit(solution)/shard_map/ppermute | solution.py:717
  125.9 16.2 %collective-permute-start.25 = (bf16[4,192,384]{2,1,0:T(8,128)(2,1)S(1)}, bf16[4,192,384]{2,1,0:T(8,128)(2,1)S(1)}, u32[]{:S(2)}, u32[]{:S(2)}) collective-permute-start(bf16[4,192,384]{2,1,0:T(8,128)(2,1)S(1)} %add_convert_fusion.1.rest_1_), channel_id=1, source_target_pairs={{0,4},{2,6},{4,0},{6,2},{8,12},{10,14},{12,8},{14,10},{16,20},{18,... | collective-permute-start | bytes 1769480 | tf_op jit(solution)/shard_map/ppermute | solution.py:717
  126.4 28.4 %collective-permute-start.20 = (bf16[8,96,384]{2,1,0:T(8,128)(2,1)}, bf16[8,96,384]{2,1,0:T(8,128)(2,1)S(1)}, u32[]{:S(2)}, u32[]{:S(2)}) collective-permute-start(bf16[8,96,384]{2,1,0:T(8,128)(2,1)} %copy-done.61), channel_id=1, source_target_pairs={{0,4},{2,6},{4,0},{6,2},{8,12},{10,14},{12,8},{14,10},{16,20},{18,... | collective-permute-start | bytes 1769480 | tf_op jit(solution)/shard_map/ppermute | solution.py:717
  128.0 29.9 %collective-permute-start.18 = (bf16[8,96,384]{2,1,0:T(8,128)(2,1)S(1)}, bf16[8,96,384]{2,1,0:T(8,128)(2,1)S(1)}, u32[]{:S(2)}, u32[]{:S(2)}) collective-permute-start(bf16[8,96,384]{2,1,0:T(8,128)(2,1)S(1)} %copy-done.41), channel_id=1, source_target_pairs={{0,2},{2,0},{4,6},{6,4},{8,10},{10,8},{12,14},{14,12},{16,18},{18,... | collective-permute-start | bytes 1769480 | tf_op jit(solution)/shard_map/ppermute | solution.py:717
  133.9 5.4 %collective-permute-start.14 = (bf16[208,384]{1,0:T(8,128)(2,1)S(1)}, bf16[208,384]{1,0:T(8,128)(2,1)S(1)}, u32[]{:S(2)}, u32[]{:S(2)}) collective-permute-start(bf16[208,384]{1,0:T(8,128)(2,1)S(1)} %add_convert_fusion.7), channel_id=1, source_target_pairs={{0,8},{2,10},{4,12},{6,14},{8,0},{10,2},{12,4},{14,6},{16,24},{18,... | collective-permute-start | bytes 479240 | tf_op jit(solution)/shard_map/ppermute | solution.py:717
  139.3 17.8 %collective-permute-start.15 = (bf16[208,384]{1,0:T(8,128)(2,1)S(1)}, bf16[208,384]{1,0:T(8,128)(2,1)S(1)}, u32[]{:S(2)}, u32[]{:S(2)}) collective-permute-start(bf16[208,384]{1,0:T(8,128)(2,1)S(1)} %add_convert_fusion.6), channel_id=1, source_target_pairs={{0,4},{2,6},{4,0},{6,2},{8,12},{10,14},{12,8},{14,10},{16,20},{18,... | collective-permute-start | bytes 479240 | tf_op jit(solution)/shard_map/ppermute | solution.py:717
  143.4 11.4 %copy-start.45 = (bf16[8,96,384]{2,1,0:T(8,128)(2,1)S(1)}, bf16[8,96,384]{2,1,0:T(8,128)(2,1)}, u32[]{:S(2)}) copy-start(bf16[8,96,384]{2,1,0:T(8,128)(2,1)} %copy-done.44) | copy-start | bytes 1769476
  144.4 13.5 %copy-start.43 = (bf16[8,96,384]{2,1,0:T(8,128)(2,1)S(1)}, bf16[8,96,384]{2,1,0:T(8,128)(2,1)}, u32[]{:S(2)}) copy-start(bf16[8,96,384]{2,1,0:T(8,128)(2,1)} %copy-done.42) | copy-start | bytes 1769476
  144.4 33.1 %collective-permute-start.27 = (bf16[2,2,192,384]{3,2,1,0:T(8,128)(2,1)}, bf16[2,2,192,384]{3,2,1,0:T(8,128)(2,1)}, u32[]{:S(2)}, u32[]{:S(2)}) collective-permute-start(bf16[2,2,192,384]{3,2,1,0:T(8,128)(2,1)} %fusion.1), channel_id=1, source_target_pairs={{0,8},{2,10},{4,12},{6,14},{8,0},{10,2},{12,4},{14,6},{16,24},{18,... | collective-permute-start | bytes 1769480 | tf_op jit(solution)/shard_map/ppermute | solution.py:717
  154.9 10.5 %collective-permute-start.21 = (bf16[4,96,384]{2,1,0:T(8,128)(2,1)S(1)}, bf16[4,96,384]{2,1,0:T(8,128)(2,1)S(1)}, u32[]{:S(2)}, u32[]{:S(2)}) collective-permute-start(bf16[4,96,384]{2,1,0:T(8,128)(2,1)S(1)} %add_convert_fusion.2), channel_id=1, source_target_pairs={{0,2},{2,0},{4,6},{6,4},{8,10},{10,8},{12,14},{14,12},{16,18},{18,... | collective-permute-start | bytes 884744 | tf_op jit(solution)/shard_map/ppermute | solution.py:717
  157.2 8.1 %collective-permute-start.16 = (bf16[208,384]{1,0:T(8,128)(2,1)S(1)}, bf16[208,384]{1,0:T(8,128)(2,1)S(1)}, u32[]{:S(2)}, u32[]{:S(2)}) collective-permute-start(bf16[208,384]{1,0:T(8,128)(2,1)S(1)} %add_convert_fusion.5), channel_id=1, source_target_pairs={{0,2},{2,0},{4,6},{6,4},{8,10},{10,8},{12,14},{14,12},{16,18},{18,... | collective-permute-start | bytes 479240 | tf_op jit(solution)/shard_map/ppermute | solution.py:717
  157.9 7.8 %collective-permute-start.19 = (bf16[4,96,384]{2,1,0:T(8,128)(2,1)S(1)}, bf16[4,96,384]{2,1,0:T(8,128)(2,1)S(1)}, u32[]{:S(2)}, u32[]{:S(2)}) collective-permute-start(bf16[4,96,384]{2,1,0:T(8,128)(2,1)S(1)} %add_convert_fusion.3), channel_id=1, source_target_pairs={{0,4},{2,6},{4,0},{6,2},{8,12},{10,14},{12,8},{14,10},{16,20},{18,... | collective-permute-start | bytes 884744 | tf_op jit(solution)/shard_map/ppermute | solution.py:717
  165.3 2.9 %collective-permute-start.17 = (bf16[208,384]{1,0:T(8,128)(2,1)S(1)}, bf16[208,384]{1,0:T(8,128)(2,1)S(1)}, u32[]{:S(2)}, u32[]{:S(2)}) collective-permute-start(bf16[208,384]{1,0:T(8,128)(2,1)S(1)} %add_convert_fusion.4), channel_id=1, source_target_pairs={{0,1},{1,0},{2,3},{3,2},{4,5},{5,4},{6,7},{7,6},{8,9},{9,8},{10,11... | collective-permute-start | bytes 479240 | tf_op jit(solution)/shard_map/ppermute | solution.py:713
  166.6 9.5 %collective-permute-start.22 = (bf16[2,2,96,384]{3,2,1,0:T(8,128)(2,1)}, bf16[2,2,96,384]{3,2,1,0:T(8,128)(2,1)}, u32[]{:S(2)}, u32[]{:S(2)}) collective-permute-start(bf16[2,2,96,384]{3,2,1,0:T(8,128)(2,1)} %fusion.3), channel_id=1, source_target_pairs={{0,8},{2,10},{4,12},{6,14},{8,0},{10,2},{12,4},{14,6},{16,24},{18,... | collective-permute-start | bytes 884744 | tf_op jit(solution)/shard_map/ppermute | solution.py:717
  177.0 16.8 %collective-permute-start.23 = (bf16[2,1,96,384]{3,2,1,0:T(8,128)(2,1)S(1)}, bf16[2,1,96,384]{3,2,1,0:T(8,128)(2,1)S(1)}, u32[]{:S(2)}, u32[]{:S(2)}) collective-permute-start(bf16[2,1,96,384]{3,2,1,0:T(8,128)(2,1)S(1)} %fusion.14), channel_id=1, source_target_pairs={{0,16},{2,18},{4,20},{6,22},{8,24},{10,26},{12,28},{14,30},{16,0},... | collective-permute-start | bytes 442376 | tf_op jit(solution)/shard_map/ppermute | solution.py:717
  178.5 20.5 %collective-permute-start.28 = (bf16[2,1,192,384]{3,2,1,0:T(8,128)(2,1)S(1)}, bf16[2,1,192,384]{3,2,1,0:T(8,128)(2,1)S(1)}, u32[]{:S(2)}, u32[]{:S(2)}) collective-permute-start(bf16[2,1,192,384]{3,2,1,0:T(8,128)(2,1)S(1)} %fusion.8), channel_id=1, source_target_pairs={{0,16},{2,18},{4,20},{6,22},{8,24},{10,26},{12,28},{14,30},{16,0},... | collective-permute-start | bytes 884744 | tf_op jit(solution)/shard_map/ppermute | solution.py:717
  194.9 6.1 %collective-permute-start.24 = (f32[4,24,384]{2,1,0:T(8,128)S(1)}, f32[4,24,384]{2,1,0:T(8,128)S(1)}, u32[]{:S(2)}, u32[]{:S(2)}) collective-permute-start(f32[4,24,384]{2,1,0:T(8,128)S(1)} %get-tuple-element.105), channel_id=1, source_target_pairs={{0,1},{1,0},{2,3},{3,2},{4,5},{5,4},{6,7},{7,6},{8,9},{9,8},{10,11... | collective-permute-start | bytes 442376 | tf_op jit(solution)/shard_map/ppermute | solution.py:713
  200.3 2.3 %collective-permute-start.30 = (f32[1,96,384]{2,0,1:T(1,128)S(1)}, f32[1,96,384]{2,0,1:T(1,128)S(1)}, u32[]{:S(2)}, u32[]{:S(2)}) collective-permute-start(f32[1,96,384]{2,0,1:T(1,128)S(1)} %squeeze.60), channel_id=1, source_target_pairs={{0,1},{1,0},{2,3},{3,2},{4,5},{5,4},{6,7},{7,6},{8,9},{9,8},{10,11... | collective-permute-start | bytes 442376 | tf_op jit(solution)/shard_map/ppermute | solution.py:713
  200.4 3.3 %collective-permute-start.29 = (f32[4,24,384]{2,1,0:T(8,128)S(1)}, f32[4,24,384]{2,1,0:T(8,128)S(1)}, u32[]{:S(2)}, u32[]{:S(2)}) collective-permute-start(f32[4,24,384]{2,1,0:T(8,128)S(1)} %get-tuple-element.103), channel_id=1, source_target_pairs={{0,1},{1,0},{2,3},{3,2},{4,5},{5,4},{6,7},{7,6},{8,9},{9,8},{10,11... | collective-permute-start | bytes 442376 | tf_op jit(solution)/shard_map/ppermute | solution.py:713
  (50 other events, 201.9 us)

commit v3 on v2

v3 whole, which is shorter than its diff:
```python
import functools

import jax
import jax.numpy as jnp
from jax import lax
from jax.experimental import pallas as pl
from jax.experimental.pallas import tpu as pltpu
from jax.sharding import PartitionSpec as P

HD = 64
SEG_MOST = 196
EPS = 1e-06
inv_root_two = 0.7071067811865476
inv_root_two_pi = 0.3989422804014327
BF = jnp.bfloat16
F32 = jnp.float32
MIB = 1 << 20


def dot_nn(a, b):
    return jnp.dot(a, b, preferred_element_type=F32)


def dot_nt(a, b):
    return lax.dot_general(a, b, (((1,), (1,)), ((), ())), preferred_element_type=F32)


def dot_tn(a, b):
    return lax.dot_general(a, b, (((0,), (0,)), ((), ())), preferred_element_type=F32)


def normalise(hidden):
    mean = jnp.mean(hidden, -1, keepdims=True)
    centred = hidden - mean
    inv = lax.rsqrt(jnp.mean(centred * centred, -1, keepdims=True) + EPS)
    return centred * inv, inv


def norm_back(grad, normal, inv, gain):
    scaled = grad * gain
    centre = jnp.mean(scaled, -1, keepdims=True)
    along = jnp.mean(scaled * normal, -1, keepdims=True)
    return inv * (scaled - centre - normal * along)


def line(ref):
    return ref[...].reshape(1, -1)


def column_sum(v):
    return jnp.sum(v, axis=0, keepdims=True)


def params(vmem):
    return pltpu.CompilerParams(vmem_limit_bytes=(60 if vmem > 24 else vmem) * MIB)


def cost(flops, bytes_accessed, trans=0):
    return pl.CostEstimate(
        flops=int(flops) // 100, bytes_accessed=int(bytes_accessed) // 100, transcendentals=int(trans) // 100
    )


def whole(shape):
    return pl.BlockSpec(shape, lambda *_: (0,) * len(shape))


def lanes_of(shape, head):
    return (lax.broadcasted_iota(jnp.int32, shape, 1) % 128 < HD) == (head % 2 == 0)


def embedded(x_ref, pos_ref, table_ref):
    half = x_ref.shape[0]
    places = table_ref.shape[0]
    hot = (lax.broadcasted_iota(jnp.int32, (places, half), 0) == pos_ref[...]).astype(F32).astype(BF)
    return x_ref[...].astype(F32) + dot_tn(hot, table_ref[...])


def crop_lanes(seg_ref):
    half = seg_ref.shape[1]
    hot = (lax.broadcasted_iota(jnp.int32, (8, half), 0) == seg_ref[...]).astype(F32).astype(BF)
    eye = lax.broadcasted_iota(jnp.int32, (8, 128), 0) == lax.broadcasted_iota(jnp.int32, (8, 128), 1)
    return dot_tn(hot, eye.astype(F32).astype(BF)).astype(BF)


def front_kernel(
    block,
    blk_ref, x_ref, xo_ref, seg_ref, sego_ref, pos_ref, poso_ref, cot_ref, table_ref,
    g1_ref, s1_ref, qb_ref, vb_ref, bo_ref, g2_ref, s2_ref, b1_ref, b2_ref,
    wqkv_hbm, wo_hbm, w1_hbm, w2_hbm,
    h0_out, n1_out, n1o_out, q_out, k_out, v_out, att_out, p_out, n2_out,
    gs_out, gk_out, as_out, ak_out, res_out, gh_out, gb_out, ga_out, b1g_ref, sums_ref,
    wqkv_ref, wo_ref, w1_ref, w2_ref, h0_ref, n1_ref, n1o_ref, hoto_ref, q_ref, k_ref, v_ref, bias_ref,
    att_ref, p_ref, h1_ref, n2_ref, gp_ref, act_ref, mixed_ref, gn_ref, res_ref, gh_ref, gb_ref, ga_ref,
    in_sem, out_sem, p_sem, late_sem,
):
    step = pl.program_id(0)
    half, width = x_ref.shape
    keys = k_ref.shape[0]
    halo = keys - half
    hidden = w1_ref.shape[1]
    blk = blk_ref[0]
    start = pl.multiple_of(blk * (half - halo), 16)
    loads = [
        pltpu.make_async_copy(src, dst, in_sem.at[k])
        for k, (src, dst) in enumerate(
            ((wqkv_hbm, wqkv_ref), (wo_hbm, wo_ref), (w1_hbm, w1_ref), (w2_hbm, w2_ref))
        )
    ]
    outs = [
        pltpu.make_async_copy(src, dst, out_sem.at[k])
        for k, (src, dst) in enumerate(
            (
                (h0_ref, h0_out), (n1_ref.at[:half], n1_out), (n1o_ref, n1o_out), (q_ref, q_out), (k_ref, k_out),
                (v_ref, v_out), (att_ref, att_out), (n2_ref, n2_out), (res_ref, res_out), (gh_ref, gh_out),
                (gb_ref, gb_out), (ga_ref, ga_out),
            )
        )
    ]

    def p_copy(i, slot):
        return pltpu.make_async_copy(p_ref.at[slot], p_out.at[pl.ds(4 * i, 4)], p_sem.at[slot])

    @pl.when(step == 0)
    def _():
        for load in loads:
            load.start()
        hidden0 = embedded(x_ref, pos_ref, table_ref)
        h0_ref[...] = hidden0
        normal, _ = normalise(hidden0)
        n1_ref[:half, :] = (normal * line(g1_ref) + line(s1_ref)).astype(BF)
        normal, _ = normalise(embedded(xo_ref, poso_ref, table_ref))
        n1o_ref[...] = (normal * line(g1_ref) + line(s1_ref)).astype(BF)
        n1_ref[half:, :] = n1o_ref[pl.ds(start, halo), :]
        hot = crop_lanes(seg_ref)
        hoto_ref[...] = crop_lanes(sego_ref)
        bias_ref[:, :half] = (dot_nt(hot, hot) - 1.0) * 1e9
        bias_ref[:, half:] = (dot_nt(hot, hoto_ref[pl.ds(start, halo), :]) - 1.0) * 1e9
        loads[0].wait()
        q = dot_nn(n1_ref[:half, :], wqkv_ref[:, :width]) + line(qb_ref)
        q_ref[...] = (q.astype(BF).astype(F32) * 0.125).astype(BF)
        k_ref[...] = dot_nn(n1_ref[...], wqkv_ref[:, width : 2 * width]).astype(BF)
        v_ref[...] = (dot_nn(n1_ref[...], wqkv_ref[:, 2 * width :]) + line(vb_ref)).astype(BF)
        for out in outs[:6]:
            out.start()

    @pl.when(step < 3)
    def _():
        slot = step % 2

        @pl.when(step == 2)
        def _():
            p_copy(0, 0).wait()

        for pair in range(2):
            cols = pl.ds(pl.multiple_of(step * 256 + pair * 128, 128), 128)
            q = q_ref[:, cols]
            both = []
            for head in range(2):
                q_one = jnp.where(lanes_of(q.shape, head), q, jnp.zeros_like(q))
                scores = dot_nt(q_one, k_ref[:, cols]) + bias_ref[...]
                top = jnp.max(scores, -1, keepdims=True)
                weight = jnp.exp(scores - top)
                probs = (weight * (1.0 / jnp.sum(weight, -1, keepdims=True))).astype(BF)
                p_ref[slot, 2 * pair + head] = probs
                both.append(dot_nn(probs, v_ref[:, cols]))
            att_ref[:, cols] = jnp.where(lanes_of(both[0].shape, 0), both[0], both[1]).astype(BF)
        p_copy(step, slot).start()

    @pl.when(step == 3)
    def _():
        outs[6].start()
        loads[1].wait()
        hidden1 = h0_ref[...] + dot_nn(att_ref[...], wo_ref[...]) + line(bo_ref)
        h1_ref[...] = hidden1
        normal, _ = normalise(hidden1)
        n2_ref[...] = (normal * line(g2_ref) + line(s2_ref)).astype(BF)
        outs[7].start()
        loads[2].wait()
        loads[3].wait()
        late = []
        chunk = 768
        part = chunk // 2
        for j in range(hidden // chunk):
            at = slice(j * chunk, (j + 1) * chunk)
            pre = dot_nn(n2_ref[...], w1_ref[:, at]) + b1_ref[at].reshape(1, -1)
            grad_act = dot_nt(cot_ref[...], w2_ref[at, :])
            cdf = 0.5 + 0.5 * lax.erf(pre * inv_root_two)
            act = (pre * cdf).astype(BF)
            slope = cdf + pre * jnp.exp(-0.5 * pre * pre) * inv_root_two_pi
            grad_pre = (grad_act * slope).astype(BF)
            b1g_ref[:, at] = column_sum(grad_pre.astype(F32))
            side, sub = divmod(j * chunk, hidden // 2)
            gp_ref[side, :, sub : sub + chunk] = grad_pre
            mine = slice(j * part, (j + 1) * part)
            for c in range(2):
                act_ref[c, :, mine] = jnp.concatenate(
                    [act[:, t : t + block] for t in range(c * block, chunk, 2 * block)], 1
                )
            mixed = dot_nn(act, w2_ref[at, :])
            grad_norm = dot_nt(grad_pre, w1_ref[:, at])
            mixed_ref[...] = mixed if j == 0 else mixed_ref[...] + mixed
            gn_ref[...] = grad_norm if j == 0 else gn_ref[...] + grad_norm
        for c, dst in enumerate((ak_out, as_out)):
            late.append((act_ref.at[(blk + c) % 2], dst))
        for c, dst in enumerate((gk_out, gs_out)):
            late.append((gp_ref.at[(blk + c) % 2], dst))
        late = [pltpu.make_async_copy(src, dst, late_sem.at[k]) for k, (src, dst) in enumerate(late)]
        for copy in late:
            copy.start()
        res_ref[...] = (h1_ref[...] + mixed_ref[...] + line(b2_ref)).astype(BF)
        outs[8].start()
        normal, inv = normalise(h1_ref[...])
        total = gn_ref[...]
        cot = cot_ref[...].astype(F32)
        sums_ref[0:1, :] = column_sum(total * normal)
        sums_ref[1:2, :] = column_sum(total)
        grad_hidden1 = cot + norm_back(total, normal, inv, line(g2_ref))
        gh_ref[...] = grad_hidden1
        branch = grad_hidden1.astype(BF)
        gb_ref[...] = branch
        outs[9].start()
        outs[10].start()
        sums_ref[2:3, :] = column_sum(branch.astype(F32))
        sums_ref[3:4, :] = column_sum(cot)
        ga_ref[...] = dot_nt(branch, wo_ref[...]).astype(BF)
        outs[11].start()
        p_copy(1, 1).wait()
        p_copy(2, 0).wait()
        for out in outs:
            out.wait()
        for copy in late:
            copy.wait()


def front(plan, halo, blk, x, xo, seg, sego, pos, poso, cot, table, vectors, wqkv, wo, w1, w2):
    half, width = x.shape
    hidden = w1.shape[1]
    keys = half + halo
    heads = width // HD
    anywhere = pl.BlockSpec(memory_space=pl.ANY)
    shapes = [
        ((half, width), F32),
        ((half, width), BF),
        ((half, width), BF),
        ((half, width), BF),
        ((keys, width), BF),
        ((keys, width), BF),
        ((half, width), BF),
        ((heads, half, keys), BF),
        ((half, width), BF),
        ((half, hidden // 2), BF),
        ((half, hidden // 2), BF),
        ((half, hidden // 2), BF),
        ((half, hidden // 2), BF),
        ((half, width), BF),
        ((half, width), F32),
        ((half, width), BF),
        ((half, width), BF),
        ((1, hidden), F32),
        ((4, width), F32),
    ]
    return pl.pallas_call(
        functools.partial(front_kernel, hidden // plan.groups // 2),
        grid_spec=pltpu.PrefetchScalarGridSpec(
            num_scalar_prefetch=1,
            grid=(4,),
            in_specs=[whole(a.shape) for a in (x, xo, seg, sego, pos, poso, cot, table) + vectors] + [anywhere] * 4,
            out_specs=[anywhere] * 17 + [whole((1, hidden)), whole((4, width))],
            scratch_shapes=[
                pltpu.VMEM(wqkv.shape, BF),
                pltpu.VMEM(wo.shape, BF),
                pltpu.VMEM(w1.shape, BF),
                pltpu.VMEM(w2.shape, BF),
                pltpu.VMEM((half, width), F32),
                pltpu.VMEM((keys, width), BF),
                pltpu.VMEM((half, width), BF),
                pltpu.VMEM((half, 128), BF),
                pltpu.VMEM((half, width), BF),
                pltpu.VMEM((keys, width), BF),
                pltpu.VMEM((keys, width), BF),
                pltpu.VMEM((half, keys), F32),
                pltpu.VMEM((half, width), BF),
                pltpu.VMEM((2, 4, half, keys), BF),
                pltpu.VMEM((half, width), F32),
                pltpu.VMEM((half, width), BF),
                pltpu.VMEM((2, half, hidden // 2), BF),
                pltpu.VMEM((2, half, hidden // 2), BF),
                pltpu.VMEM((half, width), F32),
                pltpu.VMEM((half, width), F32),
                pltpu.VMEM((half, width), BF),
                pltpu.VMEM((half, width), F32),
                pltpu.VMEM((half, width), BF),
                pltpu.VMEM((half, width), BF),
                pltpu.SemaphoreType.DMA((4,)),
                pltpu.SemaphoreType.DMA((12,)),
                pltpu.SemaphoreType.DMA((2,)),
                pltpu.SemaphoreType.DMA((4,)),
            ],
        ),
        out_shape=[jax.ShapeDtypeStruct(*s) for s in shapes],
        compiler_params=params(60),
        cost_estimate=cost(
            200 * half * width * (5 * width + 4 * hidden) + 400 * half * keys * width, 800 * width * hidden
        ),
        name="front",
    )(blk, x, xo, seg, sego, pos, poso, cot, table, *vectors, wqkv, wo, w1, w2)


class Plan:
    def __init__(self, ndp):
        self.ndp = ndp
        self.groups = min(16, ndp)
        self.bits = self.groups.bit_length() - 1
        self.rest = ndp // self.groups
        wanted = {"first": (2, 1, 0, 3), "second": (0, 1, 2, 3), "left": (0, 1, 2, 3), "right": (1, 0, 2, 3), "small": (1, 2, 3, 0)}
        self.orders = {k: [b for b in v if b < self.bits] for k, v in wanted.items()}

    def place(self, piece, p):
        code = 0
        for bit in self.orders[piece]:
            code = 2 * code + ((p >> bit) & 1)
        place = self.groups - 1 - code
        return divmod(place, self.groups // 2)


def feed_weights_kernel(
    plan, own_ref, n2_ref, n2o_ref, g_ref, go_ref, act_ref, acto_ref, cot_ref, coto_ref,
    first_send, first_keep, second_send, second_keep, acc1_ref, acc2_ref,
):
    i = pl.program_id(0)
    own = own_ref[0]
    per = plan.groups // 2
    rows1 = n2_ref.shape[1] // plan.groups
    rows2 = act_ref.shape[1] // per
    acc1_ref[...] = dot_tn(n2_ref[...], g_ref[...]) + dot_tn(n2o_ref[...], go_ref[...])
    acc2_ref[...] = dot_tn(act_ref[...], cot_ref[...]) + dot_tn(acto_ref[...], coto_ref[...])
    for step in range(2):

        @pl.when(i == step)
        def _():
            for p in range(plan.groups):
                block = acc1_ref[pl.ds(pl.multiple_of((own ^ p) * rows1, 16), rows1), :]
                kept, at = plan.place("first", p)
                (first_send, first_keep)[kept][at, step * rows1 : (step + 1) * rows1, :] = block.astype(BF)
            for low in range(per):
                block = acc2_ref[pl.ds(pl.multiple_of(((own % per) ^ low) * rows2, 16), rows2), :]
                kept, at = plan.place("second", step * per + low)
                (second_send, second_keep)[kept][at] = block.astype(BF)


def feed_weights(plan, own, n2, n2o, g, go, act, acto, cot, coto):
    half, width = n2.shape
    chunk = g.shape[1] // 2
    part = jax.ShapeDtypeStruct((plan.groups // 2, 2 * (width // plan.groups), chunk), BF)
    place = lambda i, o: (0, (o[0] // (plan.groups // 2)) ^ i)
    step = lambda i, o: (0, i)
    return pl.pallas_call(
        functools.partial(feed_weights_kernel, plan),
        grid_spec=pltpu.PrefetchScalarGridSpec(
            num_scalar_prefetch=1,
            grid=(2,),
            in_specs=[
                whole(n2.shape),
                whole(n2o.shape),
                pl.BlockSpec((half, chunk), step),
                pl.BlockSpec((half, chunk), step),
                pl.BlockSpec((half, chunk), place),
                pl.BlockSpec((half, chunk), place),
                whole(cot.shape),
                whole(coto.shape),
            ],
            out_specs=[whole(part.shape)] * 4,
            scratch_shapes=[pltpu.VMEM((width, chunk), F32), pltpu.VMEM((chunk, width), F32)],
        ),
        out_shape=(part,) * 4,
        compiler_params=params(40),
        cost_estimate=cost(8 * half * width * chunk * 2, 24 * width * chunk),
        name="feed_weights",
    )(own, n2, n2o, g, go, act, acto, cot, coto)


def attend_back_kernel(side_ref, q_ref, k_ref, v_ref, p_ref, ga_ref, *rest):
    d_ref, dh_ref = rest[-2:]
    half = q_ref.shape[0]
    q = q_ref[...]
    grad = ga_ref[...]
    dqs, dks, dvs = [], [], []
    for head in range(2):
        grad_one = jnp.where(lanes_of(grad.shape, head), grad, jnp.zeros_like(grad))
        grad_probs = dot_nt(grad_one, v_ref[...])
        probs = p_ref[head].astype(F32)
        row = jnp.sum(probs * grad_probs, -1, keepdims=True)
        grad_scores = (probs * (grad_probs - row)).astype(BF)
        dqs.append(dot_nn(grad_scores, k_ref[...]))
        dks.append(dot_tn(grad_scores, q))
        dvs.append(dot_tn(p_ref[head], grad))
    first = lanes_of(dqs[0].shape, 0)
    d_ref[0] = (jnp.where(first, dqs[0], dqs[1]) * 0.125).astype(BF)
    first = lanes_of(dks[0].shape, 0)
    dk = jnp.where(first, dks[0], dks[1]).astype(BF)
    dv = jnp.where(first, dvs[0], dvs[1]).astype(BF)
    d_ref[1] = dk[:half]
    d_ref[2] = dv[:half]
    dh_ref[0] = dk[half:]
    dh_ref[1] = dv[half:]


def attend_back(side, q, k, v, probs, ga, *after):
    half, width = q.shape
    keys = k.shape[0]
    halo = keys - half
    steps = width // 256

    def col(i, s):
        return s[0] * steps + i

    return pl.pallas_call(
        attend_back_kernel,
        grid_spec=pltpu.PrefetchScalarGridSpec(
            num_scalar_prefetch=1,
            grid=(steps,),
            in_specs=[
                pl.BlockSpec((half, 128), lambda i, s: (0, col(i, s))),
                pl.BlockSpec((keys, 128), lambda i, s: (0, col(i, s))),
                pl.BlockSpec((keys, 128), lambda i, s: (0, col(i, s))),
                pl.BlockSpec((2, half, keys), lambda i, s: (col(i, s), 0, 0)),
                pl.BlockSpec((half, 128), lambda i, s: (0, col(i, s))),
            ]
            + [pl.BlockSpec(memory_space=pl.ANY)] * len(after),
            out_specs=[
                pl.BlockSpec((3, half, 128), lambda i, s: (0, 0, i)),
                pl.BlockSpec((2, halo, 128), lambda i, s: (0, 0, i)),
            ],
        ),
        out_shape=(
            jax.ShapeDtypeStruct((3, half, width // 2), BF),
            jax.ShapeDtypeStruct((2, halo, width // 2), BF),
        ),
        compiler_params=params(40),
        cost_estimate=cost(16 * half * keys * width, half * keys * width // HD),
        name="attend_back",
    )(side, q, k, v, probs, ga, *after)


def add_rows(ref, which, start, halo, extra):
    part = ref[which, pl.ds(start, halo), :].astype(F32) + extra.astype(F32)
    ref[which, pl.ds(start, halo), :] = part.astype(BF)


def attend_weights_kernel(
    plan, own_ref, blk_ref, n1_ref, n1o_ref, d_ref, dh_ref, do_ref, dho_ref, att_ref, atto_ref,
    gb_ref, gbo_ref, *rest
):
    outs, acc_ref, mine_ref, other_ref = rest[:4], rest[4], rest[5], rest[6]
    half = n1_ref.shape[0]
    halo = dh_ref.shape[1]
    width = att_ref.shape[1]
    own = own_ref[0]
    rows = width // plan.groups
    start = pl.multiple_of((1 - blk_ref[0]) * (half - halo), 16)
    start_other = pl.multiple_of(blk_ref[0] * (half - halo), 16)
    mine_ref[...] = d_ref[...]
    other_ref[...] = do_ref[...]
    for which in range(2):
        add_rows(mine_ref, 1 + which, start, halo, dho_ref[which])
        add_rows(other_ref, 1 + which, start_other, halo, dh_ref[which])
    for panel in range(4):
        if panel < 3:
            acc_ref[...] = dot_tn(n1_ref[...], mine_ref[panel]) + dot_tn(
                n1o_ref[...], other_ref[panel]
            )
        else:
            acc_ref[...] = dot_tn(att_ref[...], gb_ref[...]) + dot_tn(atto_ref[...], gbo_ref[...])
        for p in range(plan.groups):
            source = pl.multiple_of((own ^ p) * rows, 16)
            kept, place = plan.place(("left", "right")[panel // 2], p)
            at = (panel % 2) * (width // 2)
            outs[2 * (panel // 2) + kept][place, :, at : at + width // 2] = acc_ref[pl.ds(source, rows), :].astype(BF)


def attend_weights(plan, own, blk, n1, n1o, d, dh, do, dho, att, atto, gb, gbo):
    half, width = att.shape
    cols = width // 2
    part = jax.ShapeDtypeStruct((plan.groups // 2, width // plan.groups, width), BF)
    return pl.pallas_call(
        functools.partial(attend_weights_kernel, plan),
        grid_spec=pltpu.PrefetchScalarGridSpec(
            num_scalar_prefetch=2,
            grid=(1,),
            in_specs=[
                whole(n1.shape),
                whole(n1o.shape),
                whole(d.shape),
                whole(dh.shape),
                whole(do.shape),
                whole(dho.shape),
                whole(att.shape),
                whole(atto.shape),
                pl.BlockSpec((half, cols), lambda i, o, b: (0, b[0])),
                pl.BlockSpec((half, cols), lambda i, o, b: (0, b[0])),
            ],
            out_specs=[whole(part.shape)] * 4,
            scratch_shapes=[
                pltpu.VMEM((width, cols), F32),
                pltpu.VMEM(d.shape, BF),
                pltpu.VMEM(do.shape, BF),
            ],
        ),
        out_shape=(part,) * 4,
        compiler_params=params(40),
        cost_estimate=cost(8 * half * width * width, 4 * width * width + 24 * half * width),
        name="attend_weights",
    )(own, blk, n1, n1o, d, dh, do, dho, att, atto, gb, gbo)


def front_back_kernel(
    blk_ref, da_ref, db_ref, ha_ref, hb_ref, w_ref, h0_ref, gh_ref, g1_ref, pos_ref, sums_ref, b1_ref,
    *rest,
):
    gx_ref, mine_ref, other_ref, acc_ref, small_ref = rest[-5:]
    half, width = h0_ref.shape
    halo = ha_ref.shape[1]
    cols = width // 2
    places = small_ref.shape[0] - 12
    start = pl.multiple_of((1 - blk_ref[0]) * (half - halo), 16)
    acc_ref[0] = da_ref[...]
    acc_ref[1] = db_ref[...]
    for which in range(2):
        add_rows(acc_ref.at[0], 1 + which, start, halo, ha_ref[which])
        add_rows(acc_ref.at[1], 1 + which, start, halo, hb_ref[which])
    total = jnp.zeros((half, width), F32)
    for which in range(3):
        for side, ref in enumerate((acc_ref.at[0], acc_ref.at[1])):
            actual = blk_ref[0] if side == 0 else 1 - blk_ref[0]
            at = pl.multiple_of(actual * cols, 128)
            panel = ref[which]
            total = total + dot_nt(panel, w_ref[:, pl.ds(pl.multiple_of(which * width + at, 128), cols)])
            if which != 1:
                k = places + (2 if which == 0 else 3)
                small_ref[k : k + 1, pl.ds(at, cols)] = column_sum(panel.astype(F32))
    normal, inv = normalise(h0_ref[...])
    small_ref[places : places + 1, :] = column_sum(total * normal)
    small_ref[places + 1 : places + 2, :] = column_sum(total)
    grad = (gh_ref[...] + norm_back(total, normal, inv, line(g1_ref))).astype(BF)
    gx_ref[...] = grad
    hot = (lax.broadcasted_iota(jnp.int32, (places, half), 0) == pos_ref[...]).astype(F32).astype(BF)
    small_ref[:places, :] = dot_nn(hot, grad)
    small_ref[places + 4 : places + 8, :] = sums_ref[...]
    for k in range(4):
        small_ref[places + 8 + k : places + 9 + k, :] = b1_ref[:, k * width : (k + 1) * width]
    for ref, core in ((mine_ref, blk_ref[0]), (other_ref, 1 - blk_ref[0])):
        ref[...] = small_ref[:, pl.ds(pl.multiple_of(core * cols, 128), cols)].astype(BF)


def front_back(blk, da, db, ha, hb, w, h0, gh, g1, pos, sums, b1, places, after):
    half, width = h0.shape
    return pl.pallas_call(
        front_back_kernel,
        grid_spec=pltpu.PrefetchScalarGridSpec(
            num_scalar_prefetch=1,
            grid=(1,),
            in_specs=[whole(a.shape) for a in (da, db, ha, hb, w, h0, gh, g1, pos, sums, b1)]
            + [pl.BlockSpec(memory_space=pl.ANY)] * len(after),
            out_specs=[whole((half, width))] + [whole((places + 12, width // 2))] * 2,
            scratch_shapes=[pltpu.VMEM((2,) + da.shape, BF), pltpu.VMEM((places + 12, width), F32)],
        ),
        out_shape=(
            jax.ShapeDtypeStruct((half, width), BF),
            jax.ShapeDtypeStruct((places + 12, width // 2), BF),
            jax.ShapeDtypeStruct((places + 12, width // 2), BF),
        ),
        compiler_params=params(40),
        cost_estimate=cost(6 * half * width * width, 6 * width * width + 20 * half * width),
        name="front_back",
    )(blk, da, db, ha, hb, w, h0, gh, g1, pos, sums, b1, *after)


def swap(v):
    return lax.ppermute(v, "blk", [(0, 1), (1, 0)])


def across(v, ndp, flip):
    return lax.ppermute(v, "dp", [(i, i ^ flip) for i in range(ndp)])


def wide(v):
    return v.astype(F32)


def add_kernel(count, *refs):
    total = refs[0][...].astype(F32)
    for ref in refs[1:count]:
        total = total + ref[...].astype(F32)
    refs[-1][...] = total.astype(BF)


def spec_at(block, at):
    return pl.BlockSpec(block, lambda i: (at,) + (0,) * (len(block) - 1))


ANYWHERE = pl.BlockSpec(memory_space=pl.ANY)


def add(arrays, places, block, before):
    return pl.pallas_call(
        functools.partial(add_kernel, len(arrays)),
        grid=(1,),
        in_specs=[spec_at(block, at) for at in places] + [ANYWHERE] * len(before),
        out_specs=spec_at(block, 0),
        out_shape=jax.ShapeDtypeStruct(block, BF),
        compiler_params=params(24),
        cost_estimate=cost(1, 1),
        name="add",
    )(*arrays, *before)


class Piece:
    def __init__(self, plan, name, sent, kept):
        self.plan, self.order, self.phase = plan, plan.orders[name], 0
        self.terms, self.starts, self.at = [kept], [0], 0
        self.left = kept.shape[0]
        self.send(sent, 0)

    def send(self, value, start):
        self.sent = value
        self.terms.append(across(value, self.plan.ndp, self.plan.rest << self.order[self.phase]))
        self.starts.append(start)
        self.phase += 1

    def step(self, *before):
        if self.phase == self.plan.bits:
            return
        h = self.left // 2
        block = (h,) + self.terms[0].shape[1:]
        value = add(self.terms, [(self.at - s) // h for s in self.starts], block, before)
        self.at, self.left = self.at + h, h
        self.send(value, self.at)

    def rest(self):
        return self.terms, [self.at - s for s in self.starts]


class Everywhere:
    def __init__(self, plan, mine, other):
        self.plan, self.phase = plan, 0
        self.flips = [plan.rest << b for b in plan.orders["small"]] + [1 << b for b in range(plan.rest.bit_length() - 1)]
        self.sent, self.got = mine, swap(other)

    def step(self, *before):
        if self.phase > len(self.flips):
            return
        self.sent = add((self.sent, self.got), (0, 0), self.sent.shape, before)
        flips = self.flips + [None]
        flip = flips[self.phase]
        self.got = swap(self.sent) if flip is None else across(self.sent, self.plan.ndp, flip)
        self.phase += 1

    def both(self):
        while self.phase <= len(self.flips):
            self.step()
        return self.sent, self.got


def split_kernel(counts, blk_ref, *refs):
    outs = refs[-2 * len(counts) :]
    done = 0
    for g, count in enumerate(counts):
        total = refs[done][0].astype(F32)
        for ref in refs[done + 1 : done + count]:
            total = total + ref[0].astype(F32)
        done += count
        mine, other = outs[2 * g], outs[2 * g + 1]
        half = mine.shape[1]
        for k in range(mine.shape[0]):
            low = total[2 * k * half : (2 * k + 1) * half]
            high = total[(2 * k + 1) * half : (2 * k + 2) * half]
            first = blk_ref[0] == 0
            mine[k] = jnp.where(first, low, high)
            other[k] = jnp.where(first, high, low)


def split_rows(blk, rows, *pieces):
    arrays, specs, counts, shapes = [], [], [], []
    for piece in pieces:
        terms, places = piece.rest()
        block = (1,) + terms[0].shape[1:]
        arrays += terms
        specs += [pl.BlockSpec(block, functools.partial(lambda at, i, b: (at, 0, 0), at)) for at in places]
        counts.append(len(terms))
        shapes += [jax.ShapeDtypeStruct((block[1] // (2 * rows), rows, block[2]), F32)] * 2
    return pl.pallas_call(
        functools.partial(split_kernel, counts),
        grid_spec=pltpu.PrefetchScalarGridSpec(
            num_scalar_prefetch=1, grid=(1,), in_specs=specs, out_specs=[whole(v.shape) for v in shapes]
        ),
        out_shape=shapes,
        compiler_params=params(24),
        cost_estimate=cost(1, 1),
        name="split_rows",
    )(blk, *arrays)


def total_kernel(*refs):
    total = refs[0][0].astype(F32)
    for ref in refs[1:-1]:
        total = total + ref[0].astype(F32)
    refs[-1][...] = total


def total_of(piece):
    terms, places = piece.rest()
    block = (1,) + terms[0].shape[1:]
    return pl.pallas_call(
        total_kernel,
        grid=(1,),
        in_specs=[spec_at(block, at) for at in places],
        out_specs=whole(block[1:]),
        out_shape=jax.ShapeDtypeStruct(block[1:], F32),
        compiler_params=params(24),
        cost_estimate=cost(1, 1),
        name="total",
    )(*terms)


def join_feed_kernel(blk_ref, mine_ref, got_ref, out_ref):
    count, _, cols = mine_ref.shape
    for ref, core in ((mine_ref, blk_ref[0]), (got_ref, 1 - blk_ref[0])):
        for k in range(count):
            out_ref[:, pl.ds(pl.multiple_of((core * count + k) * cols, 128), cols)] = ref[k]


def join_feed(blk, mine, got):
    count, rows, cols = mine.shape
    shape = (rows, 2 * count * cols)
    return pl.pallas_call(
        join_feed_kernel,
        grid_spec=pltpu.PrefetchScalarGridSpec(
            num_scalar_prefetch=1, grid=(1,), in_specs=[whole(mine.shape)] * 2, out_specs=whole(shape)
        ),
        out_shape=jax.ShapeDtypeStruct(shape, F32),
        compiler_params=params(24),
        cost_estimate=cost(1, 1),
        name="join_feed",
    )(blk, mine, got)


def join_attend_kernel(blk_ref, left_ref, right_ref, left_got_ref, right_got_ref, qkv_ref, out_ref):
    width = left_ref.shape[2]
    cols = width // 2
    for left, right, core in (
        (left_ref, right_ref, blk_ref[0]),
        (left_got_ref, right_got_ref, 1 - blk_ref[0]),
    ):
        at = core * cols
        qkv_ref[:, pl.ds(pl.multiple_of(at, 128), cols)] = left[0, :, :cols]
        qkv_ref[:, pl.ds(pl.multiple_of(width + at, 128), cols)] = left[0, :, cols:]
        qkv_ref[:, pl.ds(pl.multiple_of(2 * width + at, 128), cols)] = right[0, :, :cols]
        out_ref[:, pl.ds(pl.multiple_of(at, 128), cols)] = right[0, :, cols:]


def join_attend(blk, left, right, left_got, right_got):
    _, rows, width = left.shape
    shapes = ((rows, 3 * width), (rows, width))
    return pl.pallas_call(
        join_attend_kernel,
        grid_spec=pltpu.PrefetchScalarGridSpec(
            num_scalar_prefetch=1,
            grid=(1,),
            in_specs=[whole(left.shape)] * 4,
            out_specs=[whole(v) for v in shapes],
        ),
        out_shape=[jax.ShapeDtypeStruct(v, F32) for v in shapes],
        compiler_params=params(24),
        cost_estimate=cost(1, 1),
        name="join_attend",
    )(blk, left, right, left_got, right_got)


def join_small_kernel(blk_ref, mine_ref, got_ref, *outs):
    joined_ref = outs[-1]
    cols = mine_ref.shape[1]
    width = 2 * cols
    places = outs[0].shape[0]
    for ref, core in ((mine_ref, blk_ref[0]), (got_ref, 1 - blk_ref[0])):
        joined_ref[:, pl.ds(pl.multiple_of(core * cols, 128), cols)] = ref[...].astype(F32)
    outs[0][...] = joined_ref[:places, :]
    for k, out in enumerate(outs[1:9]):
        out[...] = joined_ref[places + k, :]
    for k in range(outs[9].shape[0] // width):
        outs[9][k * width : (k + 1) * width] = joined_ref[places + 8 + k, :]


def join_small(blk, mine, got, places, hidden):
    rows, cols = mine.shape
    width = 2 * cols
    shapes = [(places, width)] + [(width,)] * 8 + [(hidden,)]
    return pl.pallas_call(
        join_small_kernel,
        grid_spec=pltpu.PrefetchScalarGridSpec(
            num_scalar_prefetch=1,
            grid=(1,),
            in_specs=[whole(mine.shape)] * 2,
            out_specs=[whole(v) for v in shapes],
            scratch_shapes=[pltpu.VMEM((rows, width), F32)],
        ),
        out_shape=[jax.ShapeDtypeStruct(v, F32) for v in shapes],
        compiler_params=params(24),
        cost_estimate=cost(1, 1),
        name="join_small",
    )(blk, mine, got)


def behind(values, *others):
    return lax.optimization_barrier((values, others))[0]


def rest_of(plan, value, blk):
    groups = [[g * plan.rest + i for i in range(plan.rest)] for g in range(plan.groups)]
    value = lax.psum(value, "dp", axis_index_groups=groups)
    rows = value.shape[0] // (2 * plan.rest)
    return lax.dynamic_slice_in_dim(value, ((lax.axis_index("dp") % plan.rest) * 2 + blk) * rows, rows, axis=0)


def per_device(
    ndp, inputs, segments, positions, pos_table, ln1_gain, ln1_shift, qkv_weight, query_bias,
    value_bias, out_weight, out_bias, ln2_gain, ln2_shift, fc1_weight, fc1_bias, fc2_weight,
    fc2_bias, cotangent,
):
    plan = Plan(ndp)
    x, cot = inputs[0], cotangent[0]
    half, width = x.shape
    hidden = fc1_weight.shape[1]
    places = pos_table.shape[0]
    halo = next(h for h in range(SEG_MOST - 1, half + 1) if (half + h) % 128 == 0 and (half - h) % 16 == 0)
    blk = lax.axis_index("blk")
    dp = lax.axis_index("dp")
    blk1 = blk.astype(jnp.int32).reshape(1)
    own1 = (dp // plan.rest).astype(jnp.int32).reshape(1)

    x_other, seg_other, pos_other = swap(x), swap(segments), swap(positions)
    cot_other = swap(cot)
    vectors = (ln1_gain, ln1_shift, query_bias, value_bias, out_bias, ln2_gain, ln2_shift, fc1_bias, fc2_bias)
    (
        hidden0, n1, n1_other, q, k, v, att, probs, n2, grad_send, grad_keep, act_send, act_keep, result, gh1, gb, ga,
        b1_grad, sums,
    ) = front(
        plan, halo, blk1, x, x_other, segments, seg_other, positions, pos_other, cot, pos_table, vectors,
        qkv_weight, out_weight, fc1_weight, fc2_weight,
    )
    grad_other, act_other, n2_other = swap(grad_send), swap(act_send), swap(behind(n2, cot_other))
    d_send, h_send = attend_back(1 - blk1, q, k, v, probs, ga)
    parts = feed_weights(
        plan, own1, n2, n2_other, grad_keep, grad_other, behind(act_keep, d_send), act_other, cot, cot_other
    )
    first, second = Piece(plan, "first", *parts[:2]), Piece(plan, "second", *parts[2:])
    att_other, gb_other, d_other, h_other = swap(att), swap(gb), swap(d_send), swap(h_send)
    d_keep, h_keep = attend_back(blk1, q, k, v, probs, ga, parts[0])
    h_late = swap(h_keep)
    parts = attend_weights(
        plan, own1, blk1, n1, n1_other, d_keep, h_keep, d_other, h_other, att, att_other, gb, gb_other
    )
    left, right = Piece(plan, "left", *parts[:2]), Piece(plan, "right", *parts[2:])
    grad_x, mine, other = front_back(
        blk1, d_keep, d_send, h_other, h_late,
        qkv_weight, hidden0, gh1, ln1_gain, positions, sums, b1_grad, places, (parts[0],),
    )
    small = Everywhere(plan, mine, other)
    before = grad_x
    for piece in (
        small, first, right, small, second, left, small, first, right, small, second, left, first, right, second, left
    ):
        piece.step(before)
        before = piece.sent
    rows = width // plan.groups // 2
    if plan.rest == 1:
        fc2_grad = total_of(second)
        first_mine, first_sent = split_rows(blk1, rows, first)
        first_got = swap(first_sent)
        left_mine, left_sent, right_mine, right_sent = split_rows(blk1, rows, left, right)
        left_got, right_got = swap(left_sent), swap(right_sent)
        fc1_grad = join_feed(blk1, first_mine, first_got)
        qkv_grad, out_grad = join_attend(blk1, left_mine, right_mine, left_got, right_got)
    else:
        both = lax.all_gather(total_of(second), "blk", axis=0, tiled=True)
        fc2_grad = rest_of(plan, both, blk)
        value = total_of(first).reshape(2, 2 * rows, -1)
        columns = [lax.all_gather(v, "blk", axis=1, tiled=True) for v in (value[0], value[1])]
        columns = jnp.concatenate(columns, 1).reshape(2 * rows, 2, 2, -1).transpose(0, 2, 1, 3)
        fc1_grad = rest_of(plan, columns.reshape(2 * rows, -1), blk)
        value = jnp.concatenate([total_of(left), total_of(right)], 1).reshape(2 * rows, 4, -1)
        value = lax.all_gather(value, "blk", axis=2, tiled=True)
        value = rest_of(plan, value.reshape(2 * rows, -1), blk)
        qkv_grad, out_grad = value[:, : 3 * width], value[:, 3 * width :]
    table, *vec, b1_all = join_small(blk1, *small.both(), places, hidden)
    return (
        result[None], grad_x[None], table, vec[0], vec[1], qkv_grad, vec[2], vec[3], out_grad,
        vec[6], vec[4], vec[5], fc1_grad, b1_all, fc2_grad, vec[7],
    )


def solution(mesh):
    split = P("dp", "blk", None)
    ids = P("dp", "blk")
    both = P(("dp", "blk"), None)
    none = P()
    return jax.shard_map(
        functools.partial(per_device, mesh.shape["dp"]),
        mesh=mesh,
        in_specs=(split, ids, ids) + (none,) * 14 + (split,),
        out_specs=(
            split, split, none, none, none, both, none, none, both, none, none, none, both, none, both, none,
        ),
        check_vma=False,
    )
```

time: 206 us -> 156 us (0.76)
  local copies, waits for them, and re-layouts: 33.4 us -> 5.76 us
  waiting for transfers between devices: 58 us -> 44.6 us
  other arithmetic: 13.3 us -> 0 us
  starting transfers between devices: 23 us -> 28.9 us
    unnamed x137 -> x30, local copies, waits for them, and re-layouts: 28.2 us -> 5.76 us
    ppermute x16 -> x20, waiting for transfers between devices: 49.6 us -> 42.2 us  [across(): return lax.ppermute(v, 'dp', [(i, i ^ flip) for i in range(ndp)])]
    pallas_call x7 -> x25, Pallas kernels: 49.4 us -> 42.4 us  [the longest x1 27.3 us: front(): pl.pallas_call(functools.partial(front_kernel, hidden // plan.groups // 2...]
    convert_element_type x13 -> x0, other arithmetic: 6.44 us -> none  [the longest x4 3.21 us: next_pairs(): sum((wide(t[:h]) for t in terms)).astype(BF)]
    ppermute x15 -> x17, waiting for transfers between devices: 8.3 us -> 2.37 us  [swap(): return lax.ppermute(v, 'blk', [(0, 1), (1, 0)])]
    ppermute x16 -> x20, starting transfers between devices: 19.4 us -> 25 us  [across(): return lax.ppermute(v, 'dp', [(i, i ^ flip) for i in range(ndp)])]
    another operation x6 -> x0, other arithmetic: 4.42 us -> none  [the longest x4 2.75 us: close_pairs(): jnp.stack([sum((wide(t) for t in later[piece])) for piece in range(2)])]
    pallas_call x1, Pallas kernels: 5.12 us -> 7.79 us  [front_back(): pl.pallas_call(front_back_kernel, grid_spec=pltpu.PrefetchScalarGridSpec(...]
  transfers between devices with their start and end apart: 31 -> 37, of which waited for: 13 -> 14; matrix products, arithmetic and copies ran while one was open for 9% -> 0% of each run, Pallas kernels for 24% -> 48%
where the time goes in v3:
time: 156 us; the launch traced here: 155 us
  Pallas kernels  75.2 us (48%)
  waiting for transfers between devices  44.6 us (29%)
  starting transfers between devices  28.9 us (19%)
  local copies, waits for them, and re-layouts  5.76 us (4%)
    ppermute x20, waiting for transfers between devices, across(): return lax.ppermute(v, 'dp', [(i, i ^ flip) for i in range(ndp)])  42.2 us
    pallas_call x1, Pallas kernels, front(): pl.pallas_call(functools.partial(front_kernel, hidden // plan.groups // 2...  27.3 us
    ppermute x20, starting transfers between devices, across(): return lax.ppermute(v, 'dp', [(i, i ^ flip) for i in range(ndp)])  25 us
    pallas_call x2, Pallas kernels, attend_back(): pl.pallas_call(attend_back_kernel, grid_spec=pltpu.PrefetchScalarGridSpec...  17.6 us
    pallas_call x1, Pallas kernels, feed_weights(): pl.pallas_call(functools.partial(feed_weights_kernel, plan), grid_spec=pl...  10.4 us
    pallas_call x1, Pallas kernels, front_back(): pl.pallas_call(front_back_kernel, grid_spec=pltpu.PrefetchScalarGridSpec(...  7.79 us
    pallas_call x1, Pallas kernels, attend_weights(): pl.pallas_call(functools.partial(attend_weights_kernel, plan), grid_spec=...  7.41 us
    unnamed x30, local copies, waits for them, and re-layouts  5.76 us
  transfers between devices with their start and end apart: 37, of which 14 were waited for; matrix products, arithmetic and copies ran while one was open for 0% of the time, Pallas kernels for 48%

profile of v3, /device:TPU:0, one launch (start us, length us, event | category | flops | bytes accessed | tf_op | source)
XLA Modules:
  0.0 155.3 jit_solution(1543691677158519391)
XLA Ops:
  0.6 0.5 collective-permute-start
  1.8 1.3 collective-permute-done.1.sego_ref
  3.1 0.6 copy-done.13
  3.9 27.3 %front.1 = (f32[392,768]{1,0:T(8,128)}, bf16[392,768]{1,0:T(8,128)(2,1)}, bf16[392,768]{1,0:T(8,128)(2,1)}, bf16[392,768]{1,0:T(8,128)(2,1)}, bf16[640,768]{1,0:...) custom-call(s32[1]{0:T(128)} %bitcast.blk_ref.side_ref, ...), custom_call_target="tpu_custom_call" | custom-call | flops 10481565696 | bytes 18874368 | tf_op jit(solution)/shard_map/front/pallas_call | solution.py:263
  32.2 8.8 %attend_back.2 = (bf16[3,392,384]{2,1,0:T(8,128)(2,1)}, bf16[2,248,384]{2,1,0:T(8,128)(2,1)}) custom-call(s32[1]{0:T(128)S(6)} %sub.5.side_ref, bf16[392,768]{1,0:T(8,128)(2,1)} %get-tuple-element.71.q_ref, bf16[640,768]{1,0:T(8,128)(2,1)} %get-tuple-element.72.k_ref, bf16[640,768]{1,0:T(8,128)(2,1)} %get-tuple-element.73.v_ref, ...), custom_call_target="tpu_custom_call" | custom-call | flops 30828134 | bytes 30105 | tf_op jit(solution)/shard_map/attend_back/pallas_call | solution.py:418
  41.5 1.0 copy-done.7
  43.0 10.4 %feed_weights.1 = (bf16[8,96,768]{2,1,0:T(8,128)(2,1)}, bf16[8,96,768]{2,1,0:T(8,128)(2,1)}, bf16[8,96,768]{2,1,0:T(8,128)(2,1)}, bf16[8,96,768]{2,1,0:T(8,128)(2,1)}) custom-call(s32[1]{0:T(128)} %bitcast.4.own_ref, bf16[392,768]{1,0:T(8,128)(2,1)} %get-tuple-element.77.n2_ref, bf16[392,768]{1,0:T(8,128)(2,1)} %collective-permute-done.4.n2o_ref, ...), custom_call_target="tpu_custom_call" | custom-call | flops 36993760 | bytes 141557 | tf_op jit(solution)/shard_map/feed_weights/pallas_call | solution.py:358
  53.5 2.8 %collective-permute-start.15 = (bf16[8,96,768]{2,1,0:T(8,128)(2,1)}, bf16[8,96,768]{2,1,0:T(8,128)(2,1)S(1)}, u32[]{:S(2)}, u32[]{:S(2)}) collective-permute-start(bf16[8,96,768]{2,1,0:T(8,128)(2,1)} %get-tuple-element.84.rest_0_), channel_id=1, source_target_pairs={{0,8},{2,10},{4,12},{6,14},{8,0},{10,2},{12,4},{14,6},{16,24},{18,... | collective-permute-start | bytes 3538952 | tf_op jit(solution)/shard_map/ppermute | solution.py:584
  56.8 1.5 collective-permute-start.18
  58.3 8.8 %attend_back.3 = (bf16[3,392,384]{2,1,0:T(8,128)(2,1)}, bf16[2,248,384]{2,1,0:T(8,128)(2,1)}) custom-call(s32[1]{0:T(128)} %bitcast.blk_ref.side_ref, bf16[392,768]{1,0:T(8,128)(2,1)} %get-tuple-element.71.q_ref, bf16[640,768]{1,0:T(8,128)(2,1)} %get-tuple-element.72.k_ref, bf16[640,768]{1,0:T(8,128)(2,1)} %get-tuple-element.73.v_ref, ...), custom_call_target="tpu_custom_call" | custom-call | flops 30828134 | bytes 30105 | tf_op jit(solution)/shard_map/attend_back/pallas_call | solution.py:418
  67.2 0.7 copy-done.10
  67.9 7.4 %attend_weights.1 = (bf16[8,48,768]{2,1,0:T(8,128)(2,1)}, bf16[8,48,768]{2,1,0:T(8,128)(2,1)}, bf16[8,48,768]{2,1,0:T(8,128)(2,1)}, bf16[8,48,768]{2,1,0:T(8,128)(2,1)}) custom-call(s32[1]{0:T(128)} %bitcast.4.own_ref, s32[1]{0:T(128)} %bitcast.blk_ref.side_ref, bf16[392,768]{1,0:T(8,128)(2,1)} %get-tuple-element.92.n1_ref, ...), custom_call_target="tpu_custom_call" | custom-call | flops 18496880 | bytes 95846 | tf_op jit(solution)/shard_map/attend_weights/pallas_call | solution.py:486
  75.3 1.5 collective-permute-start.14
  76.8 0.7 copy-done.11
  77.6 7.8 %front_back.1 = (bf16[392,768]{1,0:T(8,128)(2,1)}, bf16[208,384]{1,0:T(8,128)(2,1)}, bf16[208,384]{1,0:T(8,128)(2,1)}) custom-call(s32[1]{0:T(128)} %bitcast.blk_ref.side_ref, bf16[3,392,384]{2,1,0:T(8,128)(2,1)} %get-tuple-element.85.d_ref.da_ref, bf16[3,392,384]{2,1,0:T(8,128)(2,1)} %get-tuple-element.81.db_ref, bf16[2,248,384]{2,1,0:T(8,128)(2,1)} %copy-done.6, ...), custom_call_target="tpu_custom_call" | custom-call | flops 13872660 | bytes 95600 | tf_op jit(solution)/shard_map/front_back/pallas_call | solution.py:558
  85.4 0.5 collective-permute-start.17
  85.9 1.1 collective-permute-done.12.refs_1_
  87.0 1.1 copy-done.4
  88.0 0.9 copy-done.5
  89.0 0.6 collective-permute-start.13
  89.7 1.6 %collective-permute-start.21 = (bf16[4,96,768]{2,1,0:T(8,128)(2,1)S(1)}, bf16[4,96,768]{2,1,0:T(8,128)(2,1)S(1)}, u32[]{:S(2)}, u32[]{:S(2)}) collective-permute-start(bf16[4,96,768]{2,1,0:T(8,128)(2,1)S(1)} %add.19.refs_2_), channel_id=1, source_target_pairs={{0,4},{2,6},{4,0},{6,2},{8,12},{10,14},{12,8},{14,10},{16,20},{18,... | collective-permute-start | bytes 1769480 | tf_op jit(solution)/shard_map/ppermute | solution.py:584
  91.4 4.6 %collective-permute-done.13.refs_1_ = bf16[208,384]{1,0:T(8,128)(2,1)S(1)} collective-permute-done((bf16[208,384]{1,0:T(8,128)(2,1)S(1)}, bf16[208,384]{1,0:T(8,128)(2,1)S(1)}, u32[]{:S(2)}, u32[]{:S(2)}) %collective-permute-start.13) | collective-permute-done | bytes 159776 | tf_op jit(solution)/shard_map/ppermute | solution.py:584
  96.2 0.6 collective-permute-start.25
  97.7 4.0 %collective-permute-done.17.refs_1_ = bf16[8,48,768]{2,1,0:T(8,128)(2,1)S(1)} collective-permute-done((bf16[8,48,768]{2,1,0:T(8,128)(2,1)}, bf16[8,48,768]{2,1,0:T(8,128)(2,1)S(1)}, u32[]{:S(2)}, u32[]{:S(2)}) %collective-permute-start.17) | collective-permute-done | bytes 589856 | tf_op jit(solution)/shard_map/ppermute | solution.py:584
  102.1 2.6 %collective-permute-start.19 = (bf16[208,384]{1,0:T(8,128)(2,1)S(1)}, bf16[208,384]{1,0:T(8,128)(2,1)S(1)}, u32[]{:S(2)}, u32[]{:S(2)}) collective-permute-start(bf16[208,384]{1,0:T(8,128)(2,1)S(1)} %add.24.refs_3_.refs_0_), channel_id=1, source_target_pairs={{0,16},{2,18},{4,20},{6,22},{8,24},{10,26},{12,28},{14,30},{16,0},... | collective-permute-start | bytes 479240 | tf_op jit(solution)/shard_map/ppermute | solution.py:584
  104.8 2.0 %collective-permute-start.24 = (bf16[4,48,768]{2,1,0:T(8,128)(2,1)S(1)}, bf16[4,48,768]{2,1,0:T(8,128)(2,1)S(1)}, u32[]{:S(2)}, u32[]{:S(2)}) collective-permute-start(bf16[4,48,768]{2,1,0:T(8,128)(2,1)S(1)} %add.23.refs_2_), channel_id=1, source_target_pairs={{0,4},{2,6},{4,0},{6,2},{8,12},{10,14},{12,8},{14,10},{16,20},{18,... | collective-permute-start | bytes 884744 | tf_op jit(solution)/shard_map/ppermute | solution.py:584
  106.8 1.9 %collective-permute-done.21.refs_2_ = bf16[4,96,768]{2,1,0:T(8,128)(2,1)S(1)} collective-permute-done((bf16[4,96,768]{2,1,0:T(8,128)(2,1)S(1)}, bf16[4,96,768]{2,1,0:T(8,128)(2,1)S(1)}, u32[]{:S(2)}, u32[]{:S(2)}) %collective-permute-start.21) | collective-permute-done | bytes 589856 | tf_op jit(solution)/shard_map/ppermute | solution.py:584
  108.8 0.6 collective-permute-start.29
  109.4 2.0 %collective-permute-done.19.refs_1_ = bf16[208,384]{1,0:T(8,128)(2,1)S(1)} collective-permute-done((bf16[208,384]{1,0:T(8,128)(2,1)S(1)}, bf16[208,384]{1,0:T(8,128)(2,1)S(1)}, u32[]{:S(2)}, u32[]{:S(2)}) %collective-permute-start.19) | collective-permute-done | bytes 159776 | tf_op jit(solution)/shard_map/ppermute | solution.py:584
  111.5 9.8 %collective-permute-done.25.refs_2_ = bf16[4,96,768]{2,1,0:T(8,128)(2,1)S(1)} collective-permute-done((bf16[4,96,768]{2,1,0:T(8,128)(2,1)S(1)}, bf16[4,96,768]{2,1,0:T(8,128)(2,1)S(1)}, u32[]{:S(2)}, u32[]{:S(2)}) %collective-permute-start.25) | collective-permute-done | bytes 589856 | tf_op jit(solution)/shard_map/ppermute | solution.py:584
  121.4 0.5 collective-permute-start.27
  121.9 0.5 collective-permute-start.22
  122.5 1.6 %collective-permute-start.28 = (bf16[2,48,768]{2,1,0:T(8,128)(2,1)S(1)}, bf16[2,48,768]{2,1,0:T(8,128)(2,1)S(1)}, u32[]{:S(2)}, u32[]{:S(2)}) collective-permute-start(bf16[2,48,768]{2,1,0:T(8,128)(2,1)S(1)} %add.26.refs_2_), channel_id=1, source_target_pairs={{0,8},{2,10},{4,12},{6,14},{8,0},{10,2},{12,4},{14,6},{16,24},{18,... | collective-permute-start | bytes 442376 | tf_op jit(solution)/shard_map/ppermute | solution.py:584
  124.0 2.8 %collective-permute-done.24.refs_2_ = bf16[4,48,768]{2,1,0:T(8,128)(2,1)S(1)} collective-permute-done((bf16[4,48,768]{2,1,0:T(8,128)(2,1)S(1)}, bf16[4,48,768]{2,1,0:T(8,128)(2,1)S(1)}, u32[]{:S(2)}, u32[]{:S(2)}) %collective-permute-start.24) | collective-permute-done | bytes 294944 | tf_op jit(solution)/shard_map/ppermute | solution.py:584
  126.9 0.5 collective-permute-start.26
  127.5 2.7 %collective-permute-start.34 = (bf16[1,96,768]{2,1,0:T(8,128)(2,1)S(1)}, bf16[1,96,768]{2,1,0:T(8,128)(2,1)S(1)}, u32[]{:S(2)}, u32[]{:S(2)}) collective-permute-start(bf16[1,96,768]{2,1,0:T(8,128)(2,1)S(1)} %add.31.refs_4_), channel_id=1, source_target_pairs={{0,16},{2,18},{4,20},{6,22},{8,24},{10,26},{12,28},{14,30},{16,0},... | collective-permute-start | bytes 442376 | tf_op jit(solution)/shard_map/ppermute | solution.py:584
  130.3 6.5 %collective-permute-done.28.refs_3_.refs_8_ = bf16[2,48,768]{2,1,0:T(8,128)(2,1)S(1)} collective-permute-done((bf16[2,48,768]{2,1,0:T(8,128)(2,1)S(1)}, bf16[2,48,768]{2,1,0:T(8,128)(2,1)S(1)}, u32[]{:S(2)}, u32[]{:S(2)}) %collective-permute-start.28) | collective-permute-done | bytes 147488 | tf_op jit(solution)/shard_map/ppermute | solution.py:584
  136.9 1.4 collective-permute-done.26.refs_3_
  138.4 1.1 collective-permute-start.30
  139.5 1.9 %collective-permute-start.31 = (bf16[1,48,768]{2,1,0:T(8,128)(2,1)S(1)}, bf16[1,48,768]{2,1,0:T(8,128)(2,1)S(1)}, u32[]{:S(2)}, u32[]{:S(2)}) collective-permute-start(bf16[1,48,768]{2,1,0:T(8,128)(2,1)S(1)} %add.32.refs_4_), channel_id=1, source_target_pairs={{0,16},{2,18},{4,20},{6,22},{8,24},{10,26},{12,28},{14,30},{16,0},... | collective-permute-start | bytes 221192 | tf_op jit(solution)/shard_map/ppermute | solution.py:584
  141.4 1.0 collective-permute-start.36
  142.6 5.8 %collective-permute-done.30.refs_4_ = bf16[1,48,768]{2,1,0:T(8,128)(2,1)S(1)} collective-permute-done((bf16[1,48,768]{2,1,0:T(8,128)(2,1)S(1)}, bf16[1,48,768]{2,1,0:T(8,128)(2,1)S(1)}, u32[]{:S(2)}, u32[]{:S(2)}) %collective-permute-start.30) | collective-permute-done | bytes 73760 | tf_op jit(solution)/shard_map/ppermute | solution.py:584
  148.4 1.6 %collective-permute-done.31.refs_9_ = bf16[1,48,768]{2,1,0:T(8,128)(2,1)S(1)} collective-permute-done((bf16[1,48,768]{2,1,0:T(8,128)(2,1)S(1)}, bf16[1,48,768]{2,1,0:T(8,128)(2,1)S(1)}, u32[]{:S(2)}, u32[]{:S(2)}) %collective-permute-start.31) | collective-permute-done | bytes 73760 | tf_op jit(solution)/shard_map/ppermute | solution.py:584
  150.7 0.9 join_small.1
  151.6 1.4 collective-permute-done.36.refs_4_
  153.1 0.8 total.1
  153.9 0.7 join_attend.1
  154.6 0.7 join_feed.1
  (85 shorter events, 6.8 us)
Async XLA Ops:
  0.6 2.4 %collective-permute-start = (bf16[392,768]{1,0:T(8,128)(2,1)}, bf16[392,768]{1,0:T(8,128)(2,1)S(1)}, u32[]{:S(2)}, u32[]{:S(2)}) collective-permute-start(bf16[392,768]{1,0:T(8,128)(2,1)} %bitcast.10), channel_id=1, source_target_pairs={{0,1},{1,0},{2,3},{3,2},{4,5},{5,4},{6,7},{7,6},{8,9},{9,8},{10,11... | collective-permute-start | bytes 1806344 | tf_op jit(solution)/shard_map/ppermute | solution.py:580
  1.2 1.9 %collective-permute-start.1 = (s32[1,392]{1,0:T(1,128)}, s32[1,392]{1,0:T(1,128)S(1)}, u32[]{:S(2)}, u32[]{:S(2)}) collective-permute-start(s32[1,392]{1,0:T(1,128)} %seg_ref.1), channel_id=1, source_target_pairs={{0,1},{1,0},{2,3},{3,2},{4,5},{5,4},{6,7},{7,6},{8,9},{9,8},{10,11... | collective-permute-start | bytes 4712 | tf_op jit(solution)/shard_map/ppermute | solution.py:580
  1.2 1.8 %collective-permute-start.2 = (s32[1,392]{1,0:T(1,128)}, s32[1,392]{1,0:T(1,128)S(1)}, u32[]{:S(2)}, u32[]{:S(2)}) collective-permute-start(s32[1,392]{1,0:T(1,128)} %pos_ref.3), channel_id=1, source_target_pairs={{0,1},{1,0},{2,3},{3,2},{4,5},{5,4},{6,7},{7,6},{8,9},{9,8},{10,11... | collective-permute-start | bytes 4712 | tf_op jit(solution)/shard_map/ppermute | solution.py:580
  1.7 30.1 %collective-permute-start.3 = (bf16[392,768]{1,0:T(8,128)(2,1)}, bf16[392,768]{1,0:T(8,128)(2,1)S(1)}, u32[]{:S(2)}, u32[]{:S(2)}) collective-permute-start(bf16[392,768]{1,0:T(8,128)(2,1)} %bitcast.7), channel_id=1, source_target_pairs={{0,1},{1,0},{2,3},{3,2},{4,5},{5,4},{6,7},{7,6},{8,9},{9,8},{10,11... | collective-permute-start | bytes 1806344 | tf_op jit(solution)/shard_map/ppermute | solution.py:580
  3.0 0.8 copy-start.12
  31.2 10.3 %collective-permute-start.5 = (bf16[392,1536]{1,0:T(8,128)(2,1)}, bf16[392,1536]{1,0:T(8,128)(2,1)S(1)}, u32[]{:S(2)}, u32[]{:S(2)}) collective-permute-start(bf16[392,1536]{1,0:T(8,128)(2,1)} %get-tuple-element.79), channel_id=1, source_target_pairs={{0,1},{1,0},{2,3},{3,2},{4,5},{5,4},{6,7},{7,6},{8,9},{9,8},{10,11... | collective-permute-start | bytes 3612680 | tf_op jit(solution)/shard_map/ppermute | solution.py:580
  31.6 9.9 %collective-permute-start.6 = (bf16[392,1536]{1,0:T(8,128)(2,1)}, bf16[392,1536]{1,0:T(8,128)(2,1)S(1)}, u32[]{:S(2)}, u32[]{:S(2)}) collective-permute-start(bf16[392,1536]{1,0:T(8,128)(2,1)} %get-tuple-element.83), channel_id=1, source_target_pairs={{0,1},{1,0},{2,3},{3,2},{4,5},{5,4},{6,7},{7,6},{8,9},{9,8},{10,11... | collective-permute-start | bytes 3612680 | tf_op jit(solution)/shard_map/ppermute | solution.py:580
  31.8 9.2 %copy-start.9 = (bf16[392,768]{1,0:T(8,128)(2,1)}, bf16[392,768]{1,0:T(8,128)(2,1)S(1)}, u32[]{:S(2)}) copy-start(bf16[392,768]{1,0:T(8,128)(2,1)S(1)} %collective-permute-done.3.coto_ref) | copy-start | bytes 1806340
  31.8 9.7 %collective-permute-start.4 = (bf16[392,768]{1,0:T(8,128)(2,1)}, bf16[392,768]{1,0:T(8,128)(2,1)}, u32[]{:S(2)}, u32[]{:S(2)}) collective-permute-start(bf16[392,768]{1,0:T(8,128)(2,1)} %get-tuple-element.77.n2_ref), channel_id=1, source_target_pairs={{0,1},{1,0},{2,3},{3,2},{4,5},{5,4},{6,7},{7,6},{8,9},{9,8},{10,11... | collective-permute-start | bytes 1806344 | tf_op jit(solution)/shard_map/ppermute | solution.py:580
  40.9 15.8 %collective-permute-start.7 = (bf16[2,248,384]{2,1,0:T(8,128)(2,1)}, bf16[2,248,384]{2,1,0:T(8,128)(2,1)S(1)}, u32[]{:S(2)}, u32[]{:S(2)}) collective-permute-start(bf16[2,248,384]{2,1,0:T(8,128)(2,1)} %get-tuple-element.86), channel_id=1, source_target_pairs={{0,1},{1,0},{2,3},{3,2},{4,5},{5,4},{6,7},{7,6},{8,9},{9,8},{10,11... | collective-permute-start | bytes 1142792 | tf_op jit(solution)/shard_map/ppermute | solution.py:580
  41.2 26.0 %collective-permute-start.9 = (bf16[3,392,384]{2,1,0:T(8,128)(2,1)}, bf16[3,392,384]{2,1,0:T(8,128)(2,1)}, u32[]{:S(2)}, u32[]{:S(2)}) collective-permute-start(bf16[3,392,384]{2,1,0:T(8,128)(2,1)} %get-tuple-element.81.db_ref), channel_id=1, source_target_pairs={{0,1},{1,0},{2,3},{3,2},{4,5},{5,4},{6,7},{7,6},{8,9},{9,8},{10,11... | collective-permute-start | bytes 2709512 | tf_op jit(solution)/shard_map/ppermute | solution.py:580
  41.5 1.0 copy-start.7
  41.5 1.5 copy-start.8
  53.5 36.1 %collective-permute-start.15 = (bf16[8,96,768]{2,1,0:T(8,128)(2,1)}, bf16[8,96,768]{2,1,0:T(8,128)(2,1)S(1)}, u32[]{:S(2)}, u32[]{:S(2)}) collective-permute-start(bf16[8,96,768]{2,1,0:T(8,128)(2,1)} %get-tuple-element.84.rest_0_), channel_id=1, source_target_pairs={{0,8},{2,10},{4,12},{6,14},{8,0},{10,2},{12,4},{14,6},{16,24},{18,... | collective-permute-start | bytes 3538952 | tf_op jit(solution)/shard_map/ppermute | solution.py:584
  56.2 10.8 %collective-permute-start.10 = (bf16[392,768]{1,0:T(8,128)(2,1)}, bf16[392,768]{1,0:T(8,128)(2,1)S(1)}, u32[]{:S(2)}, u32[]{:S(2)}) collective-permute-start(bf16[392,768]{1,0:T(8,128)(2,1)} %get-tuple-element.94.att_ref), channel_id=1, source_target_pairs={{0,1},{1,0},{2,3},{3,2},{4,5},{5,4},{6,7},{7,6},{8,9},{9,8},{10,11... | collective-permute-start | bytes 1806344 | tf_op jit(solution)/shard_map/ppermute | solution.py:580
  56.3 10.9 %collective-permute-start.11 = (bf16[392,768]{1,0:T(8,128)(2,1)}, bf16[392,768]{1,0:T(8,128)(2,1)}, u32[]{:S(2)}, u32[]{:S(2)}) collective-permute-start(bf16[392,768]{1,0:T(8,128)(2,1)} %get-tuple-element.95.gb_ref), channel_id=1, source_target_pairs={{0,1},{1,0},{2,3},{3,2},{4,5},{5,4},{6,7},{7,6},{8,9},{9,8},{10,11... | collective-permute-start | bytes 1806344 | tf_op jit(solution)/shard_map/ppermute | solution.py:580
  56.8 10.3 %copy-start.6 = (bf16[2,248,384]{2,1,0:T(8,128)(2,1)}, bf16[2,248,384]{2,1,0:T(8,128)(2,1)S(1)}, u32[]{:S(2)}) copy-start(bf16[2,248,384]{2,1,0:T(8,128)(2,1)S(1)} %collective-permute-done.7.dho_ref.ha_ref) | copy-start | bytes 1142788
  56.8 39.3 %collective-permute-start.18 = (bf16[8,96,768]{2,1,0:T(8,128)(2,1)}, bf16[8,96,768]{2,1,0:T(8,128)(2,1)S(1)}, u32[]{:S(2)}, u32[]{:S(2)}) collective-permute-start(bf16[8,96,768]{2,1,0:T(8,128)(2,1)} %get-tuple-element.105), channel_id=1, source_target_pairs={{0,2},{2,0},{4,6},{6,4},{8,10},{10,8},{12,14},{14,12},{16,18},{18,... | collective-permute-start | bytes 3538952 | tf_op jit(solution)/shard_map/ppermute | solution.py:584
  67.1 9.7 %collective-permute-start.8 = (bf16[2,248,384]{2,1,0:T(8,128)(2,1)}, bf16[2,248,384]{2,1,0:T(8,128)(2,1)S(1)}, u32[]{:S(2)}, u32[]{:S(2)}) collective-permute-start(bf16[2,248,384]{2,1,0:T(8,128)(2,1)} %get-tuple-element.87.dh_ref), channel_id=1, source_target_pairs={{0,1},{1,0},{2,3},{3,2},{4,5},{5,4},{6,7},{7,6},{8,9},{9,8},{10,11... | collective-permute-start | bytes 1142792 | tf_op jit(solution)/shard_map/ppermute | solution.py:580
  75.3 16.0 %collective-permute-start.14 = (bf16[8,48,768]{2,1,0:T(8,128)(2,1)}, bf16[8,48,768]{2,1,0:T(8,128)(2,1)S(1)}, u32[]{:S(2)}, u32[]{:S(2)}) collective-permute-start(bf16[8,48,768]{2,1,0:T(8,128)(2,1)} %get-tuple-element.101), channel_id=1, source_target_pairs={{0,4},{2,6},{4,0},{6,2},{8,12},{10,14},{12,8},{14,10},{16,20},{18,... | collective-permute-start | bytes 1769480 | tf_op jit(solution)/shard_map/ppermute | solution.py:584
  77.6 12.0 %copy-start.1 = (bf16[8,96,768]{2,1,0:T(8,128)(2,1)S(1)}, bf16[8,96,768]{2,1,0:T(8,128)(2,1)}, u32[]{:S(2)}) copy-start(bf16[8,96,768]{2,1,0:T(8,128)(2,1)} %get-tuple-element.102.refs_0_) | copy-start | bytes 3538948
  85.4 1.6 %collective-permute-start.12 = (bf16[208,384]{1,0:T(8,128)(2,1)}, bf16[208,384]{1,0:T(8,128)(2,1)S(1)}, u32[]{:S(2)}, u32[]{:S(2)}) collective-permute-start(bf16[208,384]{1,0:T(8,128)(2,1)} %get-tuple-element.99), channel_id=1, source_target_pairs={{0,1},{1,0},{2,3},{3,2},{4,5},{5,4},{6,7},{7,6},{8,9},{9,8},{10,11... | collective-permute-start | bytes 479240 | tf_op jit(solution)/shard_map/ppermute | solution.py:580
  85.4 16.3 %collective-permute-start.17 = (bf16[8,48,768]{2,1,0:T(8,128)(2,1)}, bf16[8,48,768]{2,1,0:T(8,128)(2,1)S(1)}, u32[]{:S(2)}, u32[]{:S(2)}) collective-permute-start(bf16[8,48,768]{2,1,0:T(8,128)(2,1)} %get-tuple-element.96.rest_0_), channel_id=1, source_target_pairs={{0,2},{2,0},{4,6},{6,4},{8,10},{10,8},{12,14},{14,12},{16,18},{18,... | collective-permute-start | bytes 1769480 | tf_op jit(solution)/shard_map/ppermute | solution.py:584
  87.0 1.1 copy-start.4
  88.0 0.9 copy-start.5
  89.0 7.0 %collective-permute-start.13 = (bf16[208,384]{1,0:T(8,128)(2,1)S(1)}, bf16[208,384]{1,0:T(8,128)(2,1)S(1)}, u32[]{:S(2)}, u32[]{:S(2)}) collective-permute-start(bf16[208,384]{1,0:T(8,128)(2,1)S(1)} %add.18.refs_2_.refs_0_), channel_id=1, source_target_pairs={{0,4},{2,6},{4,0},{6,2},{8,12},{10,14},{12,8},{14,10},{16,20},{18,... | collective-permute-start | bytes 479240 | tf_op jit(solution)/shard_map/ppermute | solution.py:584
  89.6 1.7 %copy-start.3 = (bf16[8,48,768]{2,1,0:T(8,128)(2,1)S(1)}, bf16[8,48,768]{2,1,0:T(8,128)(2,1)}, u32[]{:S(2)}) copy-start(bf16[8,48,768]{2,1,0:T(8,128)(2,1)} %get-tuple-element.100.refs_0_.refs_5_) | copy-start | bytes 1769476
  89.7 18.9 %collective-permute-start.21 = (bf16[4,96,768]{2,1,0:T(8,128)(2,1)S(1)}, bf16[4,96,768]{2,1,0:T(8,128)(2,1)S(1)}, u32[]{:S(2)}, u32[]{:S(2)}) collective-permute-start(bf16[4,96,768]{2,1,0:T(8,128)(2,1)S(1)} %add.19.refs_2_), channel_id=1, source_target_pairs={{0,4},{2,6},{4,0},{6,2},{8,12},{10,14},{12,8},{14,10},{16,20},{18,... | collective-permute-start | bytes 1769480 | tf_op jit(solution)/shard_map/ppermute | solution.py:584
  91.3 4.8 %copy-start = (bf16[8,96,768]{2,1,0:T(8,128)(2,1)S(1)}, bf16[8,96,768]{2,1,0:T(8,128)(2,1)}, u32[]{:S(2)}) copy-start(bf16[8,96,768]{2,1,0:T(8,128)(2,1)} %get-tuple-element.104.refs_0_) | copy-start | bytes 3538948
  96.1 5.6 %copy-start.2 = (bf16[8,48,768]{2,1,0:T(8,128)(2,1)S(1)}, bf16[8,48,768]{2,1,0:T(8,128)(2,1)}, u32[]{:S(2)}) copy-start(bf16[8,48,768]{2,1,0:T(8,128)(2,1)} %get-tuple-element.103.refs_0_) | copy-start | bytes 1769476
  96.2 25.1 %collective-permute-start.25 = (bf16[4,96,768]{2,1,0:T(8,128)(2,1)S(1)}, bf16[4,96,768]{2,1,0:T(8,128)(2,1)S(1)}, u32[]{:S(2)}, u32[]{:S(2)}) collective-permute-start(bf16[4,96,768]{2,1,0:T(8,128)(2,1)S(1)} %add.22.refs_2_), channel_id=1, source_target_pairs={{0,4},{2,6},{4,0},{6,2},{8,12},{10,14},{12,8},{14,10},{16,20},{18,... | collective-permute-start | bytes 1769480 | tf_op jit(solution)/shard_map/ppermute | solution.py:584
  96.8 5.3 %collective-permute-start.16 = (bf16[208,384]{1,0:T(8,128)(2,1)S(1)}, bf16[208,384]{1,0:T(8,128)(2,1)S(1)}, u32[]{:S(2)}, u32[]{:S(2)}) collective-permute-start(bf16[208,384]{1,0:T(8,128)(2,1)S(1)} %add.21.refs_2_.refs_0_), channel_id=1, source_target_pairs={{0,8},{2,10},{4,12},{6,14},{8,0},{10,2},{12,4},{14,6},{16,24},{18,... | collective-permute-start | bytes 479240 | tf_op jit(solution)/shard_map/ppermute | solution.py:584
  97.3 12.1 %collective-permute-start.20 = (bf16[4,48,768]{2,1,0:T(8,128)(2,1)S(1)}, bf16[4,48,768]{2,1,0:T(8,128)(2,1)S(1)}, u32[]{:S(2)}, u32[]{:S(2)}) collective-permute-start(bf16[4,48,768]{2,1,0:T(8,128)(2,1)S(1)} %add.20.refs_2_), channel_id=1, source_target_pairs={{0,2},{2,0},{4,6},{6,4},{8,10},{10,8},{12,14},{14,12},{16,18},{18,... | collective-permute-start | bytes 884744 | tf_op jit(solution)/shard_map/ppermute | solution.py:584
  102.1 9.3 %collective-permute-start.19 = (bf16[208,384]{1,0:T(8,128)(2,1)S(1)}, bf16[208,384]{1,0:T(8,128)(2,1)S(1)}, u32[]{:S(2)}, u32[]{:S(2)}) collective-permute-start(bf16[208,384]{1,0:T(8,128)(2,1)S(1)} %add.24.refs_3_.refs_0_), channel_id=1, source_target_pairs={{0,16},{2,18},{4,20},{6,22},{8,24},{10,26},{12,28},{14,30},{16,0},... | collective-permute-start | bytes 479240 | tf_op jit(solution)/shard_map/ppermute | solution.py:584
  104.8 22.0 %collective-permute-start.24 = (bf16[4,48,768]{2,1,0:T(8,128)(2,1)S(1)}, bf16[4,48,768]{2,1,0:T(8,128)(2,1)S(1)}, u32[]{:S(2)}, u32[]{:S(2)}) collective-permute-start(bf16[4,48,768]{2,1,0:T(8,128)(2,1)S(1)} %add.23.refs_2_), channel_id=1, source_target_pairs={{0,4},{2,6},{4,0},{6,2},{8,12},{10,14},{12,8},{14,10},{16,20},{18,... | collective-permute-start | bytes 884744 | tf_op jit(solution)/shard_map/ppermute | solution.py:584
  108.8 18.6 %collective-permute-start.29 = (bf16[2,96,768]{2,1,0:T(8,128)(2,1)S(1)}, bf16[2,96,768]{2,1,0:T(8,128)(2,1)S(1)}, u32[]{:S(2)}, u32[]{:S(2)}) collective-permute-start(bf16[2,96,768]{2,1,0:T(8,128)(2,1)S(1)} %add.25.refs_3_), channel_id=1, source_target_pairs={{0,2},{2,0},{4,6},{6,4},{8,10},{10,8},{12,14},{14,12},{16,18},{18,... | collective-permute-start | bytes 884744 | tf_op jit(solution)/shard_map/ppermute | solution.py:584
  121.4 15.4 %collective-permute-start.27 = (bf16[2,96,768]{2,1,0:T(8,128)(2,1)S(1)}, bf16[2,96,768]{2,1,0:T(8,128)(2,1)S(1)}, u32[]{:S(2)}, u32[]{:S(2)}) collective-permute-start(bf16[2,96,768]{2,1,0:T(8,128)(2,1)S(1)} %add.29.refs_3_), channel_id=1, source_target_pairs={{0,8},{2,10},{4,12},{6,14},{8,0},{10,2},{12,4},{14,6},{16,24},{18,... | collective-permute-start | bytes 884744 | tf_op jit(solution)/shard_map/ppermute | solution.py:584
  121.9 8.2 %collective-permute-start.22 = (bf16[208,384]{1,0:T(8,128)(2,1)S(1)}, bf16[208,384]{1,0:T(8,128)(2,1)S(1)}, u32[]{:S(2)}, u32[]{:S(2)}) collective-permute-start(bf16[208,384]{1,0:T(8,128)(2,1)S(1)} %add.27.refs_0_.refs_3_), channel_id=1, source_target_pairs={{0,2},{2,0},{4,6},{6,4},{8,10},{10,8},{12,14},{14,12},{16,18},{18,... | collective-permute-start | bytes 479240 | tf_op jit(solution)/shard_map/ppermute | solution.py:584
  122.5 14.3 %collective-permute-start.28 = (bf16[2,48,768]{2,1,0:T(8,128)(2,1)S(1)}, bf16[2,48,768]{2,1,0:T(8,128)(2,1)S(1)}, u32[]{:S(2)}, u32[]{:S(2)}) collective-permute-start(bf16[2,48,768]{2,1,0:T(8,128)(2,1)S(1)} %add.26.refs_2_), channel_id=1, source_target_pairs={{0,8},{2,10},{4,12},{6,14},{8,0},{10,2},{12,4},{14,6},{16,24},{18,... | collective-permute-start | bytes 442376 | tf_op jit(solution)/shard_map/ppermute | solution.py:584
  126.9 11.5 %collective-permute-start.26 = (bf16[2,48,768]{2,1,0:T(8,128)(2,1)S(1)}, bf16[2,48,768]{2,1,0:T(8,128)(2,1)S(1)}, u32[]{:S(2)}, u32[]{:S(2)}) collective-permute-start(bf16[2,48,768]{2,1,0:T(8,128)(2,1)S(1)} %add.30.refs_4_), channel_id=1, source_target_pairs={{0,8},{2,10},{4,12},{6,14},{8,0},{10,2},{12,4},{14,6},{16,24},{18,... | collective-permute-start | bytes 442376 | tf_op jit(solution)/shard_map/ppermute | solution.py:584
  127.5 15.0 %collective-permute-start.34 = (bf16[1,96,768]{2,1,0:T(8,128)(2,1)S(1)}, bf16[1,96,768]{2,1,0:T(8,128)(2,1)S(1)}, u32[]{:S(2)}, u32[]{:S(2)}) collective-permute-start(bf16[1,96,768]{2,1,0:T(8,128)(2,1)S(1)} %add.31.refs_4_), channel_id=1, source_target_pairs={{0,16},{2,18},{4,20},{6,22},{8,24},{10,26},{12,28},{14,30},{16,0},... | collective-permute-start | bytes 442376 | tf_op jit(solution)/shard_map/ppermute | solution.py:584
  130.2 20.5 %collective-permute-start.23 = (bf16[208,384]{1,0:T(8,128)(2,1)S(1)}, bf16[208,384]{1,0:T(8,128)(2,1)S(1)}, u32[]{:S(2)}, u32[]{:S(2)}) collective-permute-start(bf16[208,384]{1,0:T(8,128)(2,1)S(1)} %add.28.mine_ref), channel_id=1, source_target_pairs={{0,1},{1,0},{2,3},{3,2},{4,5},{5,4},{6,7},{7,6},{8,9},{9,8},{10,11... | collective-permute-start | bytes 479240 | tf_op jit(solution)/shard_map/ppermute | solution.py:580
  138.4 10.0 %collective-permute-start.30 = (bf16[1,48,768]{2,1,0:T(8,128)(2,1)S(1)}, bf16[1,48,768]{2,1,0:T(8,128)(2,1)S(1)}, u32[]{:S(2)}, u32[]{:S(2)}) collective-permute-start(bf16[1,48,768]{2,1,0:T(8,128)(2,1)S(1)} %add.34), channel_id=1, source_target_pairs={{0,16},{2,18},{4,20},{6,22},{8,24},{10,26},{12,28},{14,30},{16,0},... | collective-permute-start | bytes 221192 | tf_op jit(solution)/shard_map/ppermute | solution.py:584
  139.5 10.5 %collective-permute-start.31 = (bf16[1,48,768]{2,1,0:T(8,128)(2,1)S(1)}, bf16[1,48,768]{2,1,0:T(8,128)(2,1)S(1)}, u32[]{:S(2)}, u32[]{:S(2)}) collective-permute-start(bf16[1,48,768]{2,1,0:T(8,128)(2,1)S(1)} %add.32.refs_4_), channel_id=1, source_target_pairs={{0,16},{2,18},{4,20},{6,22},{8,24},{10,26},{12,28},{14,30},{16,0},... | collective-permute-start | bytes 221192 | tf_op jit(solution)/shard_map/ppermute | solution.py:584
  141.4 11.6 %collective-permute-start.36 = (bf16[1,96,768]{2,1,0:T(8,128)(2,1)S(1)}, bf16[1,96,768]{2,1,0:T(8,128)(2,1)S(1)}, u32[]{:S(2)}, u32[]{:S(2)}) collective-permute-start(bf16[1,96,768]{2,1,0:T(8,128)(2,1)S(1)} %add.33.refs_4_), channel_id=1, source_target_pairs={{0,16},{2,18},{4,20},{6,22},{8,24},{10,26},{12,28},{14,30},{16,0},... | collective-permute-start | bytes 442376 | tf_op jit(solution)/shard_map/ppermute | solution.py:584
  142.5 12.1 %collective-permute-start.35 = (f32[2,24,768]{2,1,0:T(8,128)S(1)}, f32[2,24,768]{2,1,0:T(8,128)S(1)}, u32[]{:S(2)}, u32[]{:S(2)}) collective-permute-start(f32[2,24,768]{2,1,0:T(8,128)S(1)} %get-tuple-element.121), channel_id=1, source_target_pairs={{0,1},{1,0},{2,3},{3,2},{4,5},{5,4},{6,7},{7,6},{8,9},{9,8},{10,11... | collective-permute-start | bytes 442376 | tf_op jit(solution)/shard_map/ppermute | solution.py:580
  150.1 3.8 %collective-permute-start.32 = (f32[1,24,768]{2,1,0:T(8,128)S(1)}, f32[1,24,768]{2,1,0:T(8,128)S(1)}, u32[]{:S(2)}, u32[]{:S(2)}) collective-permute-start(f32[1,24,768]{2,1,0:T(8,128)S(1)} %get-tuple-element.111), channel_id=1, source_target_pairs={{0,1},{1,0},{2,3},{3,2},{4,5},{5,4},{6,7},{7,6},{8,9},{9,8},{10,11... | collective-permute-start | bytes 221192 | tf_op jit(solution)/shard_map/ppermute | solution.py:580
  150.2 3.7 %collective-permute-start.33 = (f32[1,24,768]{2,1,0:T(8,128)S(1)}, f32[1,24,768]{2,1,0:T(8,128)S(1)}, u32[]{:S(2)}, u32[]{:S(2)}) collective-permute-start(f32[1,24,768]{2,1,0:T(8,128)S(1)} %get-tuple-element.112), channel_id=1, source_target_pairs={{0,1},{1,0},{2,3},{3,2},{4,5},{5,4},{6,7},{7,6},{8,9},{9,8},{10,11... | collective-permute-start | bytes 221192 | tf_op jit(solution)/shard_map/ppermute | solution.py:580
  (4 other events, 2.7 us)
